TPU v7x, 32 devices: a whole 2x2x4 slice. The times are simulated.
32 devices in a mesh: groups: 2 (over y), row: 8 (over z, x), col: 2 (over core).
Axes of the slice: x: 2, y: 2, z: 4, core: 2. Of those that a mesh axis runs over, the one named last changes fastest.
Arguments:
- tile_blocks: bfloat16 [256, 128, 128], P(('groups', 'row', 'col')), parts along dimension 0, may hold values from -0.25 to 0.25
- tile_rows: int32 [256], P(('groups', 'row', 'col')), parts along dimension 0, may hold values from 0 to 127, as said below
- tile_cols: int32 [256], P(('groups', 'row', 'col')), parts along dimension 0, may hold values from 0 to 31, as said below
- saved_primal: bfloat16 [4, 64, 32, 128], P(None, ('groups', 'row')), parts along dimension 1, may hold values from -6 to 6
- saved_dual: bfloat16 [3, 256, 32, 128], P(None, ('groups', 'row', 'col')), parts along dimension 1, may hold values from -6 to 6
- primal_active: int32 [3, 64, 128], P(None, ('groups', 'row')), parts along dimension 1, may hold values 0 or 1
- dual_active: int32 [3, 256, 128], P(None, ('groups', 'row', 'col')), parts along dimension 1, may hold values 0 or 1
- primal_mix: float32 [3, 32, 32], replicated, may hold values from -1 to 1
- dual_mix: float32 [3, 32, 32], replicated, may hold values from -1 to 1
- step_fracs: int32 [3, 4], replicated, may hold values from 2 to 9, as said below
- cot_primal: float32 [64, 32, 128], P(('groups', 'row')), parts along dimension 0, may hold values from -6 to 6
- cot_dual: float32 [256, 32, 128], P(('groups', 'row', 'col')), parts along dimension 0, may hold values from -6 to 6
Outputs:
- grad_primal: float32 [64, 32, 128], P(('groups', 'row')), parts along dimension 0
- grad_dual: float32 [256, 32, 128], P(('groups', 'row', 'col')), parts along dimension 0
- grad_primal_mix: float32 [6, 32, 32], P('groups'), parts along dimension 0
- grad_dual_mix: float32 [6, 32, 32], P('groups'), parts along dimension 0
There are 2 independent parts, one for each index of `groups`. A program takes and returns all parts, laid end to end along the dimension named above; an argument that names none is the same for every part. Nothing has to cross between parts.
Inputs may be any that keep to these rules, and one draw needn't show every extreme that they name: `tile_rows`: tiles come in blocks of 8, one block per device in the order of row then col. Dual block b belongs to the device numbered b // 8 in that order. The tiles of the device with row index r and col index c lie in primal blocks r * 4 to (r + 1) * 4 - 1 and in dual blocks of devices with col index c, exactly one tile in the dual blocks of the devices of each row index. `tile_cols`: see tile_rows. `step_fracs`: numerators lie in 2 to 4, denominators in 6 to 9.
All inputs are finite; a program needn't handle non-finite values. No bound on the sum of `primal_active` or of `dual_active` on one device may be relied on, other than what follows from the above.
Results may differ from a plain program's by a relative error of at most 0.007.
Values may be sent and summed in bfloat16 or wider, within the bound.
No kernel may reach another device: no remote copies, remote signals or barrier semaphores. Data moves between devices by JAX's collectives and lax.ppermute only.
A program may use at most 64 MiB of HBM per device.

v0:
```python
from functools import partial
import math

import jax
import jax.numpy as jnp
from jax import lax
from jax.sharding import PartitionSpec as P


def outgoing(tile_blocks, local_cols, peers, primal):
    picked = jnp.take(primal, local_cols, axis=0)
    product = jnp.einsum(
        "tij,tcj->tci", tile_blocks, picked, preferred_element_type=jnp.float32
    ).astype(jnp.bfloat16)
    return jnp.zeros_like(product).at[peers].set(product)


def incoming_sum(owner_table, received):
    return jnp.einsum("js,sci->jci", owner_table, received, preferred_element_type=jnp.float32)


def pull_back(tile_blocks, peers, column_table, fetched):
    picked = jnp.take(fetched, peers, axis=0)
    product = jnp.einsum("tij,tci->tcj", tile_blocks, picked, preferred_element_type=jnp.float32)
    return jnp.einsum("pt,tcj->pcj", column_table, product, precision=lax.Precision.HIGHEST)


def per_device(
    tile_blocks,
    tile_rows,
    tile_cols,
    saved_primal,
    saved_dual,
    primal_active,
    dual_active,
    primal_mix,
    dual_mix,
    step_fracs,
    cot_primal,
    cot_dual,
):
    highest = lax.Precision.HIGHEST
    row_count = lax.axis_size("row")
    col_count = lax.axis_size("col")
    owned = saved_dual.shape[1]
    primal_count = saved_primal.shape[1]
    tile_side = tile_blocks.shape[1]
    layer_count = primal_mix.shape[0]
    local_cols = tile_cols % primal_count
    peers = tile_rows // owned // col_count
    wanted = jnp.zeros((row_count,), jnp.int32).at[peers].set(tile_rows % owned)
    incoming = lax.all_to_all(wanted, "row", split_axis=0, concat_axis=0, tiled=True)
    owner_table = (incoming[None, :] == jnp.arange(owned, dtype=jnp.int32)[:, None]).astype(
        jnp.bfloat16
    )
    column_table = (
        local_cols[None, :] == jnp.arange(primal_count, dtype=jnp.int32)[:, None]
    ).astype(jnp.float32)
    row_scale = 1.0 / math.sqrt(owned * row_count * col_count * tile_side)
    col_scale = 1.0 / math.sqrt(primal_count * row_count * tile_side)
    col_first = (lax.axis_index("col") == 0).astype(jnp.float32)
    fractions = step_fracs.astype(jnp.float32)
    primal_steps = fractions[:, 0] / fractions[:, 1]
    dual_steps = fractions[:, 2] / fractions[:, 3]
    send_local = partial(outgoing, tile_blocks, local_cols, peers)
    gather_local = partial(incoming_sum, owner_table)
    adjoint_local = partial(pull_back, tile_blocks, peers, column_table)
    grad_x = cot_primal
    grad_y = cot_dual
    primal_terms = [None] * layer_count
    dual_terms = [None] * layer_count
    for layer_id in reversed(range(layer_count)):
        tau_now = primal_steps[layer_id]
        sigma_now = dual_steps[layer_id]
        extrapolated = (
            2.0 * saved_primal[layer_id + 1].astype(jnp.float32)
            - saved_primal[layer_id].astype(jnp.float32)
        ).astype(jnp.bfloat16)
        images = gather_local(
            lax.all_to_all(send_local(extrapolated), "row", split_axis=0, concat_axis=0, tiled=True)
        )
        fetched_saved = lax.all_to_all(
            jnp.take(saved_dual[layer_id], incoming, axis=0),
            "row",
            split_axis=0,
            concat_axis=0,
            tiled=True,
        )
        pulled = lax.psum(adjoint_local(fetched_saved).astype(jnp.bfloat16), "col").astype(
            jnp.float32
        )
        dual_cot = dual_active[layer_id][:, None, :].astype(jnp.float32) * grad_y
        mixed_dual = (
            -sigma_now * jnp.einsum("ce,bei->bci", dual_mix[layer_id], dual_cot, precision=highest)
        ).astype(jnp.bfloat16)
        fetched_mixed = lax.all_to_all(
            jnp.take(mixed_dual, incoming, axis=0), "row", split_axis=0, concat_axis=0, tiled=True
        )
        back_primal = lax.psum(adjoint_local(fetched_mixed), "col")
        primal_cot = primal_active[layer_id][:, None, :].astype(jnp.float32) * (
            grad_x + 2.0 * back_primal
        )
        grad_x = primal_cot - back_primal
        mixed_primal = (
            -tau_now
            * jnp.einsum("ce,bei->bci", primal_mix[layer_id], primal_cot, precision=highest)
        ).astype(jnp.bfloat16)
        pushed = gather_local(
            lax.all_to_all(send_local(mixed_primal), "row", split_axis=0, concat_axis=0, tiled=True)
        )
        grad_y = dual_cot + pushed
        dual_terms[layer_id] = (
            -sigma_now * row_scale * jnp.einsum("bci,bei->ce", images, dual_cot, precision=highest)
        )
        primal_terms[layer_id] = col_first * (
            -tau_now * col_scale * jnp.einsum("bci,bei->ce", pulled, primal_cot, precision=highest)
        )
    primal_mix_grad, dual_mix_grad = lax.psum(
        (jnp.stack(primal_terms), jnp.stack(dual_terms)), ("row", "col")
    )
    return (grad_x, grad_y, primal_mix_grad, dual_mix_grad)


def solution(mesh):
    return jax.shard_map(
        per_device,
        mesh=mesh,
        in_specs=(
            P(("groups", "row", "col"), None, None),
            P(("groups", "row", "col")),
            P(("groups", "row", "col")),
            P(None, ("groups", "row"), None, None),
            P(None, ("groups", "row", "col"), None, None),
            P(None, ("groups", "row"), None),
            P(None, ("groups", "row", "col"), None),
            P(),
            P(),
            P(),
            P(("groups", "row"), None, None),
            P(("groups", "row", "col"), None, None),
        ),
        out_specs=(
            P(("groups", "row"), None, None),
            P(("groups", "row", "col"), None, None),
            P("groups", None, None),
            P("groups", None, None),
        ),
        check_vma=False,
    )
```

profile of v0, /device:TPU:0, one launch (start us, length us, event | category | flops | bytes accessed | tf_op | source)
XLA Modules:
  0.0 308.1 jit_solution(9390707222798884906)
XLA Ops:
  9.2 7.3 %all-to-all-start = ((s32[8,1,1]{2,1,0:T(1,128)}), s32[8,1,1]{2,1,0:T(1,128)S(1)}, u32[]{:S(2)}, u32[]{:S(2)}) async-start(s32[8,1,1]{2,1,0:T(1,128)} %copy.109), calls=%async_computation | async-start | bytes 8192 | tf_op jit(solution)/shard_map/all_to_all | solution.py:52
  36.3 6.0 %all-to-all-start.10 = ((bf16[8,32,128]{2,1,0:T(8,128)(2,1)}), bf16[8,32,128]{2,1,0:T(8,128)(2,1)S(1)}, u32[]{:S(2)}, u32[]{:S(2)}) async-start(bf16[8,32,128]{2,1,0:T(8,128)(2,1)} %scatter_fusion.3), calls=%async_computation.10 | async-start | bytes 131072 | tf_op jit(solution)/shard_map/all_to_all | solution.py:80
  45.5 3.7 %all-to-all-done.10 = bf16[8,32,128]{2,1,0:T(8,128)(2,1)S(1)} async-done(((bf16[8,32,128]{2,1,0:T(8,128)(2,1)}), bf16[8,32,128]{2,1,0:T(8,128)(2,1)S(1)}, u32[]{:S(2)}, u32[]{:S(2)}) %all-to-all-start.10) | async-done | bytes 65568 | tf_op jit(solution)/shard_map/all_to_all | solution.py:80
  49.2 3.4 %all-to-all-start.12 = ((bf16[8,32,128]{2,1,0:T(8,128)(2,1)}), bf16[8,32,128]{2,1,0:T(8,128)(2,1)S(1)}, u32[]{:S(2)}, u32[]{:S(2)}) async-start(bf16[8,32,128]{2,1,0:T(8,128)(2,1)} %scatter_fusion.5), calls=%async_computation.12 | async-start | bytes 131072 | tf_op jit(solution)/shard_map/all_to_all | solution.py:80
  52.7 6.7 %all-to-all-done.12 = bf16[8,32,128]{2,1,0:T(8,128)(2,1)S(1)} async-done(((bf16[8,32,128]{2,1,0:T(8,128)(2,1)}), bf16[8,32,128]{2,1,0:T(8,128)(2,1)S(1)}, u32[]{:S(2)}, u32[]{:S(2)}) %all-to-all-start.12) | async-done | bytes 65568 | tf_op jit(solution)/shard_map/all_to_all | solution.py:80
  59.4 3.4 %all-to-all-start.1 = ((bf16[8,32,128]{2,1,0:T(8,128)(2,1)}), bf16[8,32,128]{2,1,0:T(8,128)(2,1)S(1)}, u32[]{:S(2)}, u32[]{:S(2)}) async-start(bf16[8,32,128]{2,1,0:T(8,128)(2,1)} %broadcast_select_fusion.5), calls=%async_computation.1 | async-start | bytes 131072 | tf_op jit(solution)/shard_map/all_to_all | solution.py:96
  62.9 6.7 %all-to-all-done.1 = bf16[8,32,128]{2,1,0:T(8,128)(2,1)S(1)} async-done(((bf16[8,32,128]{2,1,0:T(8,128)(2,1)}), bf16[8,32,128]{2,1,0:T(8,128)(2,1)S(1)}, u32[]{:S(2)}, u32[]{:S(2)}) %all-to-all-start.1) | async-done | bytes 65568 | tf_op jit(solution)/shard_map/all_to_all | solution.py:96
  74.7 5.1 %all-to-all-done.11 = bf16[8,32,128]{2,1,0:T(8,128)(2,1)S(1)} async-done(((bf16[8,32,128]{2,1,0:T(8,128)(2,1)}), bf16[8,32,128]{2,1,0:T(8,128)(2,1)S(1)}, u32[]{:S(2)}, u32[]{:S(2)}) %all-to-all-start.11) | async-done | bytes 65568 | tf_op jit(solution)/shard_map/all_to_all | solution.py:80
  79.9 15.8 %all-reduce.7.cloned.1.call-done = f32[4,32,128]{2,0,1:T(4,128)} async-done(((f32[4,32,128]{2,0,1:T(4,128)}), f32[4,32,128]{2,0,1:T(4,128)}) %all-reduce.7.cloned.1.call-update) | async-done | bytes 65552 | tf_op jit(solution)/shard_map/psum | solution.py:99
  100.4 5.8 %all-to-all-start.2 = ((bf16[8,32,128]{2,1,0:T(8,128)(2,1)}), bf16[8,32,128]{2,1,0:T(8,128)(2,1)S(1)}, u32[]{:S(2)}, u32[]{:S(2)}) async-start(bf16[8,32,128]{2,1,0:T(8,128)(2,1)} %scatter_fusion), calls=%async_computation.2 | async-start | bytes 131072 | tf_op jit(solution)/shard_map/all_to_all | solution.py:109
  106.4 6.6 %all-to-all-done.2 = bf16[8,32,128]{2,1,0:T(8,128)(2,1)S(1)} async-done(((bf16[8,32,128]{2,1,0:T(8,128)(2,1)}), bf16[8,32,128]{2,1,0:T(8,128)(2,1)S(1)}, u32[]{:S(2)}, u32[]{:S(2)}) %all-to-all-start.2) | async-done | bytes 65568 | tf_op jit(solution)/shard_map/all_to_all | solution.py:109
  118.4 6.6 %all-to-all-done.9 = bf16[8,32,128]{2,1,0:T(8,128)(2,1)S(1)} async-done(((bf16[8,32,128]{2,1,0:T(8,128)(2,1)}), bf16[8,32,128]{2,1,0:T(8,128)(2,1)S(1)}, u32[]{:S(2)}, u32[]{:S(2)}) %all-to-all-start.9) | async-done | bytes 65568 | tf_op jit(solution)/shard_map/all_to_all | solution.py:82
  129.2 6.0 %all-to-all-done.8 = bf16[8,32,128]{2,1,0:T(8,128)(2,1)S(1)} async-done(((bf16[8,32,128]{2,1,0:T(8,128)(2,1)}), bf16[8,32,128]{2,1,0:T(8,128)(2,1)S(1)}, u32[]{:S(2)}, u32[]{:S(2)}) %all-to-all-start.8) | async-done | bytes 65568 | tf_op jit(solution)/shard_map/all_to_all | solution.py:82
  135.2 3.4 %all-to-all-start.3 = ((bf16[8,32,128]{2,1,0:T(8,128)(2,1)}), bf16[8,32,128]{2,1,0:T(8,128)(2,1)S(1)}, u32[]{:S(2)}, u32[]{:S(2)}) async-start(bf16[8,32,128]{2,1,0:T(8,128)(2,1)} %get-tuple-element.58), calls=%async_computation.3 | async-start | bytes 131072 | tf_op jit(solution)/shard_map/all_to_all | solution.py:96
  140.3 5.2 %all-to-all-done.3 = bf16[8,32,128]{2,1,0:T(8,128)(2,1)S(1)} async-done(((bf16[8,32,128]{2,1,0:T(8,128)(2,1)}), bf16[8,32,128]{2,1,0:T(8,128)(2,1)S(1)}, u32[]{:S(2)}, u32[]{:S(2)}) %all-to-all-start.3) | async-done | bytes 65568 | tf_op jit(solution)/shard_map/all_to_all | solution.py:96
  151.5 4.1 %all-to-all-done.7 = bf16[8,32,128]{2,1,0:T(8,128)(2,1)S(1)} async-done(((bf16[8,32,128]{2,1,0:T(8,128)(2,1)}), bf16[8,32,128]{2,1,0:T(8,128)(2,1)S(1)}, u32[]{:S(2)}, u32[]{:S(2)}) %all-to-all-start.7) | async-done | bytes 65568 | tf_op jit(solution)/shard_map/all_to_all | solution.py:82
  157.3 14.2 %all-reduce.9.cloned.1.call-done = f32[4,32,128]{2,0,1:T(4,128)} async-done(((f32[4,32,128]{2,0,1:T(4,128)}), f32[4,32,128]{2,0,1:T(4,128)}) %all-reduce.9.cloned.1.call-update) | async-done | bytes 65552 | tf_op jit(solution)/shard_map/psum | solution.py:99
  176.1 5.8 %all-to-all-start.4 = ((bf16[8,32,128]{2,1,0:T(8,128)(2,1)}), bf16[8,32,128]{2,1,0:T(8,128)(2,1)S(1)}, u32[]{:S(2)}, u32[]{:S(2)}) async-start(bf16[8,32,128]{2,1,0:T(8,128)(2,1)} %scatter_fusion.1), calls=%async_computation.4 | async-start | bytes 131072 | tf_op jit(solution)/shard_map/all_to_all | solution.py:109
  181.9 11.9 %all-reduce.13.cloned.1.call-done = (bf16[4,32,128]{2,0,1:T(4,128)(2,1)}, bf16[4,32,128]{2,0,1:T(4,128)(2,1)}, bf16[4,32,128]{2,0,1:T(4,128)(2,1)}) async-done(((bf16[4,32,128]{2,0,1:T(4,128)(2,1)}, bf16[4,32,128]{2,0,1:T(4,128)(2,1)}, bf16[4,32,128]{2,0,1:T(4,128)(2,1)}), (bf16[4,32,128]{2,0,1:T(4,128)(2,1)}, bf16[4,32,128]{2,0,1:T(4,128)(2,1)}, ...) | async-done | bytes 98320 | tf_op jit(solution)/shard_map/psum | solution.py:89
  196.6 5.8 %all-to-all-start.5 = ((bf16[8,32,128]{2,1,0:T(8,128)(2,1)}), bf16[8,32,128]{2,1,0:T(8,128)(2,1)S(1)}, u32[]{:S(2)}, u32[]{:S(2)}) async-start(bf16[8,32,128]{2,1,0:T(8,128)(2,1)} %broadcast_select_fusion.3), calls=%async_computation.5 | async-start | bytes 131072 | tf_op jit(solution)/shard_map/all_to_all | solution.py:96
  202.7 6.6 %all-to-all-done.5 = bf16[8,32,128]{2,1,0:T(8,128)(2,1)S(1)} async-done(((bf16[8,32,128]{2,1,0:T(8,128)(2,1)}), bf16[8,32,128]{2,1,0:T(8,128)(2,1)S(1)}, u32[]{:S(2)}, u32[]{:S(2)}) %all-to-all-start.5) | async-done | bytes 65568 | tf_op jit(solution)/shard_map/all_to_all | solution.py:96
  211.1 15.3 %all-reduce.11.cloned.1.call-done = f32[4,32,128]{2,0,1:T(4,128)} async-done(((f32[4,32,128]{2,0,1:T(4,128)}), f32[4,32,128]{2,0,1:T(4,128)}) %all-reduce.11.cloned.1.call-update) | async-done | bytes 65552 | tf_op jit(solution)/shard_map/psum | solution.py:99
  231.6 5.9 %all-to-all-start.6 = ((bf16[8,32,128]{2,1,0:T(8,128)(2,1)}), bf16[8,32,128]{2,1,0:T(8,128)(2,1)S(1)}, u32[]{:S(2)}, u32[]{:S(2)}) async-start(bf16[8,32,128]{2,1,0:T(8,128)(2,1)} %scatter_fusion.2), calls=%async_computation.6 | async-start | bytes 131072 | tf_op jit(solution)/shard_map/all_to_all | solution.py:109
  237.7 63.1 %all-reduce = (f32[3,32,32]{2,1,0:T(8,128)}, f32[3,32,32]{2,1,0:T(8,128)}) all-reduce(f32[3,32,32]{2,1,0:T(8,128)S(1)} %pad_maximum_fusion, f32[3,32,32]{2,1,0:T(8,128)S(1)} %pad_maximum_fusion.1), channel_id=1, replica_groups=mesh['groups'=2,'row'=8,'col'=2] {'row','col'}, use_global_device_ids=true, to_apply=%region_10.13 | all-reduce | flops 6144 | bytes 49152 | tf_op jit(solution)/shard_map/psum | solution.py:118
  (135 shorter events, 65.8 us)
Async XLA Ops:
  7.2 18.0 %copy-start = (bf16[8,128,128]{2,1,0:T(8,128)(2,1)S(1)}, bf16[8,128,128]{2,1,0:T(8,128)(2,1)}, u32[]{:S(2)}) copy-start(bf16[8,128,128]{2,1,0:T(8,128)(2,1)} %param.16) | copy-start | bytes 786436
  7.2 16.8 %copy-start.4 = (bf16[4,4,32,128]{3,2,1,0:T(8,128)(2,1)S(1)}, bf16[4,4,32,128]{3,2,1,0:T(8,128)(2,1)}, u32[]{:S(2)}) copy-start(bf16[4,4,32,128]{3,2,1,0:T(8,128)(2,1)} %param.19) | copy-start | bytes 393220
  9.2 27.0 %all-to-all-start = ((s32[8,1,1]{2,1,0:T(1,128)}), s32[8,1,1]{2,1,0:T(1,128)S(1)}, u32[]{:S(2)}, u32[]{:S(2)}) async-start(s32[8,1,1]{2,1,0:T(1,128)} %copy.109), calls=%async_computation | async-start | bytes 8192 | tf_op jit(solution)/shard_map/all_to_all | solution.py:52
  29.9 2.6 copy-start.5
  36.3 12.9 %all-to-all-start.10 = ((bf16[8,32,128]{2,1,0:T(8,128)(2,1)}), bf16[8,32,128]{2,1,0:T(8,128)(2,1)S(1)}, u32[]{:S(2)}, u32[]{:S(2)}) async-start(bf16[8,32,128]{2,1,0:T(8,128)(2,1)} %scatter_fusion.3), calls=%async_computation.10 | async-start | bytes 131072 | tf_op jit(solution)/shard_map/all_to_all | solution.py:80
  49.2 10.2 %all-to-all-start.12 = ((bf16[8,32,128]{2,1,0:T(8,128)(2,1)}), bf16[8,32,128]{2,1,0:T(8,128)(2,1)S(1)}, u32[]{:S(2)}, u32[]{:S(2)}) async-start(bf16[8,32,128]{2,1,0:T(8,128)(2,1)} %scatter_fusion.5), calls=%async_computation.12 | async-start | bytes 131072 | tf_op jit(solution)/shard_map/all_to_all | solution.py:80
  59.4 10.2 %all-to-all-start.1 = ((bf16[8,32,128]{2,1,0:T(8,128)(2,1)}), bf16[8,32,128]{2,1,0:T(8,128)(2,1)S(1)}, u32[]{:S(2)}, u32[]{:S(2)}) async-start(bf16[8,32,128]{2,1,0:T(8,128)(2,1)} %broadcast_select_fusion.5), calls=%async_computation.1 | async-start | bytes 131072 | tf_op jit(solution)/shard_map/all_to_all | solution.py:96
  69.6 10.2 %all-to-all-start.11 = ((bf16[8,32,128]{2,1,0:T(8,128)(2,1)}), bf16[8,32,128]{2,1,0:T(8,128)(2,1)S(1)}, u32[]{:S(2)}, u32[]{:S(2)}) async-start(bf16[8,32,128]{2,1,0:T(8,128)(2,1)} %scatter_fusion.4), calls=%async_computation.11 | async-start | bytes 131072 | tf_op jit(solution)/shard_map/all_to_all | solution.py:80
  72.9 22.8 %all-reduce.7.cloned.1.call-start = ((), (), s32[]{:S(2)}) async-start(), calls=%async_computation.13 | async-start | bytes 131072 | tf_op jit(solution)/shard_map/psum | solution.py:99
  74.7 21.0 %copy-start.6 = (f32[4,32,128]{2,1,0:T(8,128)S(1)}, f32[4,32,128]{2,1,0:T(8,128)}, u32[]{:S(2)}) copy-start(f32[4,32,128]{2,1,0:T(8,128)} %param.26) | copy-start | bytes 196612
  100.4 12.7 %all-to-all-start.2 = ((bf16[8,32,128]{2,1,0:T(8,128)(2,1)}), bf16[8,32,128]{2,1,0:T(8,128)(2,1)S(1)}, u32[]{:S(2)}, u32[]{:S(2)}) async-start(bf16[8,32,128]{2,1,0:T(8,128)(2,1)} %scatter_fusion), calls=%async_computation.2 | async-start | bytes 131072 | tf_op jit(solution)/shard_map/all_to_all | solution.py:109
  114.8 10.2 %all-to-all-start.9 = ((bf16[8,32,128]{2,1,0:T(8,128)(2,1)}), bf16[8,32,128]{2,1,0:T(8,128)(2,1)S(1)}, u32[]{:S(2)}, u32[]{:S(2)}) async-start(bf16[8,32,128]{2,1,0:T(8,128)(2,1)} %get-tuple-element.60), calls=%async_computation.9 | async-start | bytes 131072 | tf_op jit(solution)/shard_map/all_to_all | solution.py:82
  125.0 10.2 %all-to-all-start.8 = ((bf16[8,32,128]{2,1,0:T(8,128)(2,1)}), bf16[8,32,128]{2,1,0:T(8,128)(2,1)S(1)}, u32[]{:S(2)}, u32[]{:S(2)}) async-start(bf16[8,32,128]{2,1,0:T(8,128)(2,1)} %get-tuple-element.59), calls=%async_computation.8 | async-start | bytes 131072 | tf_op jit(solution)/shard_map/all_to_all | solution.py:82
  135.2 10.2 %all-to-all-start.3 = ((bf16[8,32,128]{2,1,0:T(8,128)(2,1)}), bf16[8,32,128]{2,1,0:T(8,128)(2,1)S(1)}, u32[]{:S(2)}, u32[]{:S(2)}) async-start(bf16[8,32,128]{2,1,0:T(8,128)(2,1)} %get-tuple-element.58), calls=%async_computation.3 | async-start | bytes 131072 | tf_op jit(solution)/shard_map/all_to_all | solution.py:96
  145.4 10.2 %all-to-all-start.7 = ((bf16[8,32,128]{2,1,0:T(8,128)(2,1)}), bf16[8,32,128]{2,1,0:T(8,128)(2,1)S(1)}, u32[]{:S(2)}, u32[]{:S(2)}) async-start(bf16[8,32,128]{2,1,0:T(8,128)(2,1)} %get-tuple-element.57), calls=%async_computation.7 | async-start | bytes 131072 | tf_op jit(solution)/shard_map/all_to_all | solution.py:82
  148.8 22.8 %all-reduce.9.cloned.1.call-start = ((), (), s32[]{:S(2)}) async-start(), calls=%async_computation.14 | async-start | bytes 131072 | tf_op jit(solution)/shard_map/psum | solution.py:99
  150.6 43.2 %all-reduce.13.cloned.1.call-start = ((), (), s32[]{:S(2)}) async-start(), calls=%async_computation.16 | async-start | bytes 196608 | tf_op jit(solution)/shard_map/psum | solution.py:89
  157.3 14.3 %copy-start.1 = (f32[4,32,128]{2,0,1:T(4,128)S(1)}, f32[4,32,128]{2,0,1:T(4,128)}, u32[]{:S(2)}) copy-start(f32[4,32,128]{2,0,1:T(4,128)} %all-reduce.7.cloned.1.call-done) | copy-start | bytes 196612
  176.1 18.8 %all-to-all-start.4 = ((bf16[8,32,128]{2,1,0:T(8,128)(2,1)}), bf16[8,32,128]{2,1,0:T(8,128)(2,1)S(1)}, u32[]{:S(2)}, u32[]{:S(2)}) async-start(bf16[8,32,128]{2,1,0:T(8,128)(2,1)} %scatter_fusion.1), calls=%async_computation.4 | async-start | bytes 131072 | tf_op jit(solution)/shard_map/all_to_all | solution.py:109
  196.6 12.7 %all-to-all-start.5 = ((bf16[8,32,128]{2,1,0:T(8,128)(2,1)}), bf16[8,32,128]{2,1,0:T(8,128)(2,1)S(1)}, u32[]{:S(2)}, u32[]{:S(2)}) async-start(bf16[8,32,128]{2,1,0:T(8,128)(2,1)} %broadcast_select_fusion.3), calls=%async_computation.5 | async-start | bytes 131072 | tf_op jit(solution)/shard_map/all_to_all | solution.py:96
  202.4 24.0 %all-reduce.11.cloned.1.call-start = ((), (), s32[]{:S(2)}) async-start(), calls=%async_computation.15 | async-start | bytes 131072 | tf_op jit(solution)/shard_map/psum | solution.py:99
  211.1 15.4 %copy-start.2 = (f32[4,32,128]{2,0,1:T(4,128)S(1)}, f32[4,32,128]{2,0,1:T(4,128)}, u32[]{:S(2)}) copy-start(f32[4,32,128]{2,0,1:T(4,128)} %all-reduce.9.cloned.1.call-done) | copy-start | bytes 196612
  231.6 5.9 %copy-start.9 = (bf16[4,32,128]{2,0,1:T(4,128)(2,1)S(1)}, bf16[4,32,128]{2,0,1:T(4,128)(2,1)}, u32[]{:S(2)}) copy-start(bf16[4,32,128]{2,0,1:T(4,128)(2,1)} %get-tuple-element.30) | copy-start | bytes 98308
  231.6 69.2 %all-to-all-start.6 = ((bf16[8,32,128]{2,1,0:T(8,128)(2,1)}), bf16[8,32,128]{2,1,0:T(8,128)(2,1)S(1)}, u32[]{:S(2)}, u32[]{:S(2)}) async-start(bf16[8,32,128]{2,1,0:T(8,128)(2,1)} %scatter_fusion.2), calls=%async_computation.6 | async-start | bytes 131072 | tf_op jit(solution)/shard_map/all_to_all | solution.py:109
  (5 other events, 4.3 us)
Sparse Core Ops, SparseCore 0:
  76.6 19.0 all-reduce.6
  152.5 19.0 all-reduce.8
  174.6 19.1 all-reduce.12
  211.2 15.1 all-reduce.10
where the time goes:
time: 310 us; the launch traced here: 308 us
  waiting for transfers between devices  115 us (37%)
  blocking collectives  63.1 us (20%)
  starting transfers between devices  60.1 us (19%)
  local copies, waits for them, and re-layouts  30.7 us (10%)
  between operations  18.2 us (6%)
  matrix products  12.6 us (4%)
  other arithmetic  8.87 us (3%)
    psum x1, blocking collectives, per_device(): lax.psum((jnp.stack(primal_terms), jnp.stack(dual_terms)), ('row', 'col'))  63.1 us
    psum x3, waiting for transfers between devices, per_device(): back_primal = lax.psum(adjoint_local(fetched_mixed), 'col')  45.4 us
    all_to_all x3, waiting for transfers between devices, per_device(): lax.all_to_all(jnp.take(mixed_dual, incoming, axis=0), 'row', split_axis=...  18.4 us
    all_to_all x3, starting transfers between devices, per_device(): lax.all_to_all(send_local(mixed_primal), 'row', split_axis=0, concat_axis...  17.5 us
    all_to_all x3, waiting for transfers between devices, per_device(): lax.all_to_all(jnp.take(saved_dual[layer_id], incoming, axis=0), 'row', s...  16.8 us
    all_to_all x3, waiting for transfers between devices, per_device(): lax.all_to_all(send_local(extrapolated), 'row', split_axis=0, concat_axis...  15.4 us
    all_to_all x3, starting transfers between devices, per_device(): lax.all_to_all(send_local(extrapolated), 'row', split_axis=0, concat_axis...  12.7 us
    all_to_all x3, starting transfers between devices, per_device(): lax.all_to_all(jnp.take(mixed_dual, incoming, axis=0), 'row', split_axis=...  12.5 us
  transfers between devices with their start and end apart: 17, of which 14 were waited for; matrix products, arithmetic and copies ran while one was open for 11% of the time, Pallas kernels for 0%

commit v1 on v0

v1 whole, which is shorter than its diff:
```python
from functools import partial
import math

import jax
import jax.numpy as jnp
from jax import lax
from jax.experimental import pallas as pl
from jax.experimental.pallas import tpu as pltpu
from jax.sharding import PartitionSpec as P

SMEM = pl.BlockSpec(memory_space=pltpu.SMEM)
VMEM = pl.BlockSpec(memory_space=pltpu.VMEM)
F32 = jnp.float32
BF16 = jnp.bfloat16
PARAMS = pltpu.CompilerParams(vmem_limit_bytes=16 * 1024 * 1024)


def loop(count, body):
    if count <= 16:
        for i in range(count):
            body(i)
    else:
        lax.fori_loop(0, count, lambda i, _: (body(i), 0)[1], 0)


def exact_dot(a, b, dims):
    return lax.dot_general(
        a, b, (dims, ((), ())), precision=lax.Precision.HIGHEST, preferred_element_type=F32
    )


def mask_and_send(layer, mask_ref, saved_ref, index_ref, cot_ref, send_ref):
    owned, channels, _ = cot_ref.shape
    for b in range(owned):
        cot_ref[b] = mask_ref[layer, pl.ds(b, 1), :].astype(F32) * cot_ref[b]

    def one(r):
        d = index_ref[0, r]
        send_ref[r, :channels, :] = cot_ref[d].astype(BF16)
        send_ref[r, channels:, :] = saved_ref[layer, d]

    loop(send_ref.shape[0], one)


def add_pushed(index_ref, received_ref, cot_ref):
    channels = cot_ref.shape[1]

    def one(r):
        d = index_ref[0, r]
        cot_ref[d] = cot_ref[d] + received_ref[r, :channels, :].astype(F32)

    loop(received_ref.shape[0], one)


def sum_terms(received_ref):
    channels = received_ref.shape[1] // 2
    rows = received_ref.shape[0]
    if rows <= 16:
        total = received_ref[0, channels:, :].astype(F32)
        for r in range(1, rows):
            total = total + received_ref[r, channels:, :].astype(F32)
    else:
        total = lax.fori_loop(
            0,
            rows,
            lambda r, t: t + received_ref[r, channels:, :].astype(F32),
            jnp.zeros((channels, received_ref.shape[2]), F32),
        )
    return total + pltpu.roll(total, total.shape[1] // 2, 1)


def first_dual_kernel(layer, index_ref, cot_in, mask_ref, saved_ref, cot_ref, send_ref):
    cot_ref[...] = cot_in[...]
    mask_and_send(layer, mask_ref, saved_ref, index_ref, cot_ref, send_ref)


def dual_kernel(
    layer, index_ref, received_ref, cot_in, mask_ref, saved_ref, cot_ref, send_ref, terms_ref
):
    cot_ref[...] = cot_in[...]
    add_pushed(index_ref, received_ref, cot_ref)
    mask_and_send(layer, mask_ref, saved_ref, index_ref, cot_ref, send_ref)
    terms_ref[...] = sum_terms(received_ref)


def last_dual_kernel(index_ref, received_ref, cot_in, cot_ref, terms_ref):
    cot_ref[...] = cot_in[...]
    add_pushed(index_ref, received_ref, cot_ref)
    terms_ref[...] = sum_terms(received_ref)


def pull_kernel(index_ref, tiles_ref, received_ref, sum_ref):
    sum_ref[...] = jnp.zeros_like(sum_ref)

    def one(t):
        product = jnp.dot(received_ref[index_ref[1, t]], tiles_ref[t], preferred_element_type=F32)
        p = index_ref[2, t]
        sum_ref[p] = sum_ref[p] + product

    loop(tiles_ref.shape[0], one)


def primal_kernel(
    layer,
    index_ref,
    steps_ref,
    tiles_ref,
    mine_ref,
    other_ref,
    grad_in,
    mask_ref,
    saved_ref,
    dual_mix_ref,
    primal_mix_ref,
    grad_ref,
    send_ref,
    mixed_ref,
):
    blocks, channels, side = grad_ref.shape
    sigma = steps_ref[layer, 1]
    tau = steps_ref[layer, 0]
    pad = jnp.zeros((side - 2 * channels, side), F32)
    none = jnp.zeros((channels, side), F32)
    terms = jnp.zeros((channels, side), F32)
    for p in range(blocks):
        both = mine_ref[p] + other_ref[p]
        pulled_mixed, pulled_saved = both[:channels], both[channels:]
        back = -sigma * exact_dot(dual_mix_ref[layer], pulled_mixed, ((1,), (0,)))
        primal_cot = mask_ref[layer, pl.ds(p, 1), :].astype(F32) * (grad_in[p] + 2.0 * back)
        grad_ref[p] = primal_cot - back
        mixed_ref[p] = (
            -tau * exact_dot(primal_mix_ref[layer], primal_cot, ((1,), (0,)))
        ).astype(BF16)
        extrapolated = (
            2.0 * saved_ref[layer + 1, p].astype(F32) - saved_ref[layer, p].astype(F32)
        ).astype(BF16).astype(F32)
        terms = terms + exact_dot(
            extrapolated, jnp.concatenate([pulled_mixed, none, pad], 0), ((1,), (1,))
        )
        terms = terms + exact_dot(
            pulled_saved, jnp.concatenate([none, primal_cot, pad], 0), ((1,), (1,))
        )
    high = terms.astype(BF16).astype(F32)
    packed = (high + pltpu.roll(terms - high, side // 2, 1)).astype(BF16)

    def one(t):
        product = lax.dot_general(
            mixed_ref[index_ref[2, t]],
            tiles_ref[t],
            (((1,), (1,)), ((), ())),
            preferred_element_type=F32,
        )
        peer = index_ref[1, t]
        send_ref[peer, :channels, :] = product.astype(BF16)
        send_ref[peer, channels:, :] = packed

    loop(tiles_ref.shape[0], one)


def per_device(
    tile_blocks,
    tile_rows,
    tile_cols,
    saved_primal,
    saved_dual,
    primal_active,
    dual_active,
    primal_mix,
    dual_mix,
    step_fracs,
    cot_primal,
    cot_dual,
):
    row_count = lax.axis_size("row")
    col_count = lax.axis_size("col")
    owned, channels, side = cot_dual.shape
    primal_count = cot_primal.shape[0]
    layer_count = primal_mix.shape[0]
    row_scale = 1.0 / math.sqrt(owned * row_count * col_count * side)
    col_scale = 1.0 / math.sqrt(primal_count * row_count * side)
    local_cols = tile_cols % primal_count
    peers = tile_rows // (owned * col_count)
    peer_ids = jnp.arange(row_count, dtype=jnp.int32)
    wanted = jnp.sum(
        jnp.where(peers[None, :] == peer_ids[:, None], (tile_rows % owned)[None, :], 0), axis=1
    )

    def exchange(x):
        return lax.all_to_all(x, "row", split_axis=0, concat_axis=0, tiled=True)

    incoming = exchange(wanted)
    index = jnp.stack([incoming, peers, local_cols])
    fractions = step_fracs.astype(F32)
    steps = jnp.stack(
        [fractions[:, 0] / fractions[:, 1], fractions[:, 2] / fractions[:, 3]], axis=1
    )
    swap = [(i, col_count - 1 - i) for i in range(col_count)]
    message = jax.ShapeDtypeStruct((row_count, 2 * channels, side), BF16)
    dual_shape = jax.ShapeDtypeStruct(cot_dual.shape, F32)
    terms_shape = jax.ShapeDtypeStruct((channels, side), F32)
    grad_x, cot = cot_primal, cot_dual
    received = None
    all_terms = []
    for layer in reversed(range(layer_count)):
        if received is None:
            cot, send = pl.pallas_call(
                partial(first_dual_kernel, layer),
                out_shape=(dual_shape, message),
                in_specs=[SMEM] + [VMEM] * 3,
                out_specs=(VMEM, VMEM),
                compiler_params=PARAMS,
            )(index, cot, dual_active, saved_dual)
        else:
            cot, send, terms = pl.pallas_call(
                partial(dual_kernel, layer),
                out_shape=(dual_shape, message, terms_shape),
                in_specs=[SMEM] + [VMEM] * 4,
                out_specs=(VMEM,) * 3,
                compiler_params=PARAMS,
            )(index, received, cot, dual_active, saved_dual)
            all_terms.append(terms)
        fetched = exchange(send)
        mine = pl.pallas_call(
            pull_kernel,
            out_shape=jax.ShapeDtypeStruct((primal_count, 2 * channels, side), F32),
            in_specs=[SMEM] + [VMEM] * 2,
            out_specs=VMEM,
            compiler_params=PARAMS,
        )(index, tile_blocks, fetched)
        other = lax.ppermute(mine, "col", swap)
        grad_x, push = pl.pallas_call(
            partial(primal_kernel, layer),
            out_shape=(jax.ShapeDtypeStruct(cot_primal.shape, F32), message),
            in_specs=[SMEM] * 2 + [VMEM] * 8,
            out_specs=(VMEM, VMEM),
            scratch_shapes=[pltpu.VMEM(cot_primal.shape, BF16)],
            compiler_params=PARAMS,
        )(
            index,
            steps,
            tile_blocks,
            mine,
            other,
            grad_x,
            primal_active,
            saved_primal,
            dual_mix,
            primal_mix,
        )
        received = exchange(push)
    grad_y, terms = pl.pallas_call(
        last_dual_kernel,
        out_shape=(dual_shape, terms_shape),
        in_specs=[SMEM] + [VMEM] * 2,
        out_specs=(VMEM, VMEM),
        compiler_params=PARAMS,
    )(index, received, cot)
    all_terms.append(terms)
    terms = jnp.stack(all_terms[::-1])
    dual_mix_grad = (-row_scale * steps[:, 1])[:, None, None] * terms[:, :, :channels]
    primal_mix_grad = (-col_scale * steps[:, 0])[:, None, None] * terms[
        :, :, channels : 2 * channels
    ]
    return (grad_x, grad_y, primal_mix_grad, dual_mix_grad)


def solution(mesh):
    return jax.shard_map(
        per_device,
        mesh=mesh,
        in_specs=(
            P(("groups", "row", "col"), None, None),
            P(("groups", "row", "col")),
            P(("groups", "row", "col")),
            P(None, ("groups", "row"), None, None),
            P(None, ("groups", "row", "col"), None, None),
            P(None, ("groups", "row"), None),
            P(None, ("groups", "row", "col"), None),
            P(),
            P(),
            P(),
            P(("groups", "row"), None, None),
            P(("groups", "row", "col"), None, None),
        ),
        out_specs=(
            P(("groups", "row"), None, None),
            P(("groups", "row", "col"), None, None),
            P("groups", None, None),
            P("groups", None, None),
        ),
        check_vma=False,
    )
```

time: 310 us -> 96.4 us (0.31)
  waiting for transfers between devices: 115 us -> 17.3 us
  starting transfers between devices: 60.1 us -> 11.1 us
  local copies, waits for them, and re-layouts: 30.7 us -> 2.54 us
  between operations: 18.2 us -> 0.8 us
  blocking collectives: 63.1 us -> 49.7 us
  matrix products: 12.6 us -> 0 us
  Pallas kernels: 0 us -> 12.3 us
  other arithmetic: 8.87 us -> 2.02 us
    psum x1 -> x0, blocking collectives: 63.1 us -> none  [per_device(): lax.psum((jnp.stack(primal_terms), jnp.stack(dual_terms)), ('row', 'col'))]
    psum x4 -> x0, waiting for transfers between devices: 57.3 us -> none  [the longest x3 45.4 us: per_device(): back_primal = lax.psum(adjoint_local(fetched_mixed), 'col')]
    all_to_all x0 -> x5, blocking collectives: none -> 49.7 us  [exchange(): return lax.all_to_all(x, 'row', split_axis=0, concat_axis=0, tiled=True)]
    all_to_all x13 -> x2, starting transfers between devices: 60 us -> 10.9 us  [exchange(): return lax.all_to_all(x, 'row', split_axis=0, concat_axis=0, tiled=True)]
    all_to_all x13 -> x2, waiting for transfers between devices: 57.3 us -> 13.6 us  [exchange(): return lax.all_to_all(x, 'row', split_axis=0, concat_axis=0, tiled=True)]
    dot_general x36 -> x0, matrix products: 12.6 us -> none  [the longest x6 5.34 us: pull_back(): jnp.einsum('pt,tcj->pcj', column_table, product, precision=lax.Precision....]
    scatter x7 -> x0, local copies, waits for them, and re-layouts: 12.6 us -> none  [the longest x6 12 us: outgoing(): return jnp.zeros_like(product).at[peers].set(product)]
    pallas_call x0 -> x10, Pallas kernels: none -> 12.3 us  [the longest x3 6.16 us: per_device(): pl.pallas_call(partial(primal_kernel, layer), out_shape=(jax.ShapeDtypeSt...]
  transfers between devices with their start and end apart: 17 -> 5, of which waited for: 14 -> 5; matrix products, arithmetic and copies ran while one was open for 11% -> 0% of each run, Pallas kernels for 0% -> 0%
where the time goes in v1:
time: 96.4 us; the launch traced here: 95.8 us
  blocking collectives  49.7 us (52%)
  waiting for transfers between devices  17.3 us (18%)
  Pallas kernels  12.3 us (13%)
  starting transfers between devices  11.1 us (12%)
  local copies, waits for them, and re-layouts  2.54 us (3%)
  other arithmetic  2.02 us (2%)
    all_to_all x5, blocking collectives, exchange(): return lax.all_to_all(x, 'row', split_axis=0, concat_axis=0, tiled=True)  49.7 us
    all_to_all x2, waiting for transfers between devices, exchange(): return lax.all_to_all(x, 'row', split_axis=0, concat_axis=0, tiled=True)  13.6 us
    all_to_all x2, starting transfers between devices, exchange(): return lax.all_to_all(x, 'row', split_axis=0, concat_axis=0, tiled=True)  10.9 us
    pallas_call x3, Pallas kernels, per_device(): pl.pallas_call(partial(primal_kernel, layer), out_shape=(jax.ShapeDtypeSt...  6.16 us
    ppermute x3, waiting for transfers between devices, per_device(): other = lax.ppermute(mine, 'col', swap)  3.73 us
    pallas_call x3, Pallas kernels, per_device(): pl.pallas_call(pull_kernel, out_shape=jax.ShapeDtypeStruct((primal_count,...  2.32 us
  transfers between devices with their start and end apart: 5, of which 5 were waited for; matrix products, arithmetic and copies ran while one was open for 0% of the time, Pallas kernels for 0%

profile of v1, /device:TPU:0, one launch (start us, length us, event | category | flops | bytes accessed | tf_op | source)
XLA Modules:
  0.0 95.8 jit_solution(17581911953480396788)
XLA Ops:
  1.4 0.7 copy.18
  2.1 7.4 %all-to-all-start = ((s32[8,1,1]{2,1,0:T(1,128)}), s32[8,1,1]{2,1,0:T(1,128)S(1)}, u32[]{:S(2)}, u32[]{:S(2)}) async-start(s32[8,1,1]{2,1,0:T(1,128)} %copy.18), calls=%async_computation | async-start | bytes 8192 | tf_op jit(solution)/shard_map/all_to_all | solution.py:189
  9.5 6.4 %all-to-all-done = s32[8,1,1]{2,1,0:T(1,128)S(1)} async-done(((s32[8,1,1]{2,1,0:T(1,128)}), s32[8,1,1]{2,1,0:T(1,128)S(1)}, u32[]{:S(2)}, u32[]{:S(2)}) %all-to-all-start) | async-done | bytes 64 | tf_op jit(solution)/shard_map/all_to_all | solution.py:189
  16.1 0.9 copy-done.1
  17.1 0.9 copy-done.6
  18.0 1.2 %shard_map.147 = (f32[8,32,128]{2,1,0:T(8,128)S(1)}, bf16[8,64,128]{2,1,0:T(8,128)(2,1)}) custom-call(s32[3,8]{1,0:T(4,128)S(1)} %pad_add_fusion.index_ref, f32[8,32,128]{2,1,0:T(8,128)S(1)} %copy-done.6, s32[3,8,128]{2,1,0:T(8,128)S(1)} %copy-done.7, bf16[3,8,32,128]{3,2,1,0:T(8,128)(2,1)S(1)} %copy-done.1), custom_call_target="tpu_custom_call" | custom-call | tf_op jit(solution)/shard_map/pallas_call | solution.py:206
  19.2 3.5 %all-to-all-start.1 = ((bf16[8,64,128]{2,1,0:T(8,128)(2,1)}), bf16[8,64,128]{2,1,0:T(8,128)(2,1)S(1)}, u32[]{:S(2)}, u32[]{:S(2)}) async-start(bf16[8,64,128]{2,1,0:T(8,128)(2,1)} %get-tuple-element.20), calls=%async_computation.1 | async-start | bytes 262144 | tf_op jit(solution)/shard_map/all_to_all | solution.py:189
  22.8 7.2 %all-to-all-done.1.received_ref = bf16[8,64,128]{2,1,0:T(8,128)(2,1)S(1)} async-done(((bf16[8,64,128]{2,1,0:T(8,128)(2,1)}), bf16[8,64,128]{2,1,0:T(8,128)(2,1)S(1)}, u32[]{:S(2)}, u32[]{:S(2)}) %all-to-all-start.1) | async-done | bytes 131104 | tf_op jit(solution)/shard_map/all_to_all | solution.py:189
  30.0 0.8 shard_map.148.mine_ref
  31.2 1.1 %collective-permute-done.other_ref = f32[4,64,128]{2,1,0:T(8,128)S(1)} collective-permute-done((f32[4,64,128]{2,1,0:T(8,128)S(1)}, f32[4,64,128]{2,1,0:T(8,128)S(1)}, u32[]{:S(2)}, u32[]{:S(2)}) %collective-permute-start) | collective-permute-done | bytes 131104 | tf_op jit(solution)/shard_map/ppermute | solution.py:230
  32.2 2.0 %shard_map.149 = (f32[4,32,128]{2,1,0:T(8,128)S(1)}, bf16[8,64,128]{2,1,0:T(8,128)(2,1)S(1)}) custom-call(s32[3,8]{1,0:T(4,128)S(1)} %pad_add_fusion.index_ref, f32[3,2]{1,0:T(4,128)S(1)} %pad_maximum_fusion.1.steps_ref, bf16[8,128,128]{2,1,0:T(8,128)(2,1)S(1)} %copy-done, f32[4,64,128]{2,1,0:T(8,128)S(1)} %shard_map.148.mine_ref, ...), custom_call_target="tpu_custom_call" | custom-call | tf_op jit(solution)/shard_map/pallas_call | solution.py:231
  34.2 10.1 %all_to_all.39.received_ref = bf16[8,64,128]{2,1,0:T(8,128)(2,1)S(1)} all-to-all(bf16[8,64,128]{2,1,0:T(8,128)(2,1)S(1)} %get-tuple-element.21), channel_id=1, replica_groups=mesh['groups'=2,'row'=8,'col'=2] {'row'}, dimensions={0} | all-to-all | bytes 262144 | tf_op jit(solution)/shard_map/all_to_all | solution.py:189
  45.0 9.8 %all_to_all.40.received_ref = bf16[8,64,128]{2,1,0:T(8,128)(2,1)S(1)} all-to-all(bf16[8,64,128]{2,1,0:T(8,128)(2,1)S(1)} %get-tuple-element.23), channel_id=1, replica_groups=mesh['groups'=2,'row'=8,'col'=2] {'row'}, dimensions={0} | all-to-all | bytes 262144 | tf_op jit(solution)/shard_map/all_to_all | solution.py:189
  54.8 0.8 shard_map.151.mine_ref
  55.7 1.3 %collective-permute-done.1.other_ref = f32[4,64,128]{2,1,0:T(8,128)S(1)} collective-permute-done((f32[4,64,128]{2,1,0:T(8,128)S(1)}, f32[4,64,128]{2,1,0:T(8,128)S(1)}, u32[]{:S(2)}, u32[]{:S(2)}) %collective-permute-start.1) | collective-permute-done | bytes 131104 | tf_op jit(solution)/shard_map/ppermute | solution.py:230
  57.0 2.0 %shard_map.152 = (f32[4,32,128]{2,1,0:T(8,128)S(1)}, bf16[8,64,128]{2,1,0:T(8,128)(2,1)S(1)}) custom-call(s32[3,8]{1,0:T(4,128)S(1)} %pad_add_fusion.index_ref, f32[3,2]{1,0:T(4,128)S(1)} %pad_maximum_fusion.1.steps_ref, bf16[8,128,128]{2,1,0:T(8,128)(2,1)S(1)} %copy-done, f32[4,64,128]{2,1,0:T(8,128)S(1)} %shard_map.151.mine_ref, ...), custom_call_target="tpu_custom_call" | custom-call | tf_op jit(solution)/shard_map/pallas_call | solution.py:231
  58.9 10.0 %all_to_all.41.received_ref = bf16[8,64,128]{2,1,0:T(8,128)(2,1)S(1)} all-to-all(bf16[8,64,128]{2,1,0:T(8,128)(2,1)S(1)} %get-tuple-element.25), channel_id=1, replica_groups=mesh['groups'=2,'row'=8,'col'=2] {'row'}, dimensions={0} | all-to-all | bytes 262144 | tf_op jit(solution)/shard_map/all_to_all | solution.py:189
  69.6 9.8 %all_to_all.42.received_ref = bf16[8,64,128]{2,1,0:T(8,128)(2,1)S(1)} all-to-all(bf16[8,64,128]{2,1,0:T(8,128)(2,1)S(1)} %get-tuple-element.27), channel_id=1, replica_groups=mesh['groups'=2,'row'=8,'col'=2] {'row'}, dimensions={0} | all-to-all | bytes 262144 | tf_op jit(solution)/shard_map/all_to_all | solution.py:189
  79.4 0.8 shard_map.154.mine_ref
  80.3 1.3 %collective-permute-done.2.other_ref = f32[4,64,128]{2,1,0:T(8,128)S(1)} collective-permute-done((f32[4,64,128]{2,1,0:T(8,128)S(1)}, f32[4,64,128]{2,1,0:T(8,128)S(1)}, u32[]{:S(2)}, u32[]{:S(2)}) %collective-permute-start.2) | collective-permute-done | bytes 131104 | tf_op jit(solution)/shard_map/ppermute | solution.py:230
  81.6 2.3 %shard_map.155 = (f32[4,32,128]{2,1,0:T(8,128)}, bf16[8,64,128]{2,1,0:T(8,128)(2,1)S(1)}) custom-call(s32[3,8]{1,0:T(4,128)S(1)} %pad_add_fusion.index_ref, f32[3,2]{1,0:T(4,128)S(1)} %pad_maximum_fusion.1.steps_ref, bf16[8,128,128]{2,1,0:T(8,128)(2,1)S(1)} %copy-done, f32[4,64,128]{2,1,0:T(8,128)S(1)} %shard_map.154.mine_ref, ...), custom_call_target="tpu_custom_call" | custom-call | tf_op jit(solution)/shard_map/pallas_call | solution.py:231
  83.9 10.0 %all_to_all.43.received_ref = bf16[8,64,128]{2,1,0:T(8,128)(2,1)S(1)} all-to-all(bf16[8,64,128]{2,1,0:T(8,128)(2,1)S(1)} %get-tuple-element.30), channel_id=1, replica_groups=mesh['groups'=2,'row'=8,'col'=2] {'row'}, dimensions={0} | all-to-all | bytes 262144 | tf_op jit(solution)/shard_map/all_to_all | solution.py:189
  93.8 1.3 %shard_map.156 = (f32[8,32,128]{2,1,0:T(8,128)}, f32[32,128]{1,0:T(8,128)S(1)}) custom-call(s32[3,8]{1,0:T(4,128)S(1)} %pad_add_fusion.index_ref, bf16[8,64,128]{2,1,0:T(8,128)(2,1)S(1)} %all_to_all.43.received_ref, f32[8,32,128]{2,1,0:T(8,128)S(1)} %get-tuple-element.31.cot_in), custom_call_target="tpu_custom_call" | custom-call | tf_op jit(solution)/shard_map/pallas_call | solution.py:251
  95.1 0.7 slice_multiply_fusion
  (36 shorter events, 2.9 us)
Async XLA Ops:
  1.4 8.1 %copy-start.11 = (s32[8]{0:T(128)S(1)}, s32[8]{0:T(128)}, u32[]{:S(2)}) copy-start(s32[8]{0:T(128)} %param.14) | copy-start | bytes 100
  2.1 14.0 %copy-start.7 = (s32[3,8,128]{2,1,0:T(8,128)S(1)}, s32[3,8,128]{2,1,0:T(8,128)}, u32[]{:S(2)}) copy-start(s32[3,8,128]{2,1,0:T(8,128)} %mask_ref.10) | copy-start | bytes 36868
  2.1 13.8 %all-to-all-start = ((s32[8,1,1]{2,1,0:T(1,128)}), s32[8,1,1]{2,1,0:T(1,128)S(1)}, u32[]{:S(2)}, u32[]{:S(2)}) async-start(s32[8,1,1]{2,1,0:T(1,128)} %copy.18), calls=%async_computation | async-start | bytes 8192 | tf_op jit(solution)/shard_map/all_to_all | solution.py:189
  16.1 0.9 copy-start.1
  17.1 0.9 copy-start.6
  18.0 12.0 %copy-start = (bf16[8,128,128]{2,1,0:T(8,128)(2,1)S(1)}, bf16[8,128,128]{2,1,0:T(8,128)(2,1)}, u32[]{:S(2)}) copy-start(bf16[8,128,128]{2,1,0:T(8,128)(2,1)} %tiles_ref.11) | copy-start | bytes 786436
  19.2 3.5 %copy-start.10 = (s32[3,4]{1,0:T(4,128)S(1)}, s32[3,4]{1,0:T(4,128)}, u32[]{:S(2)}) copy-start(s32[3,4]{1,0:T(4,128)} %param.21) | copy-start | bytes 148
  19.2 10.8 %all-to-all-start.1 = ((bf16[8,64,128]{2,1,0:T(8,128)(2,1)}), bf16[8,64,128]{2,1,0:T(8,128)(2,1)S(1)}, u32[]{:S(2)}, u32[]{:S(2)}) async-start(bf16[8,64,128]{2,1,0:T(8,128)(2,1)} %get-tuple-element.20), calls=%async_computation.1 | async-start | bytes 262144 | tf_op jit(solution)/shard_map/all_to_all | solution.py:189
  22.7 9.5 %copy-start.3 = (bf16[4,4,32,128]{3,2,1,0:T(8,128)(2,1)S(1)}, bf16[4,4,32,128]{3,2,1,0:T(8,128)(2,1)}, u32[]{:S(2)}) copy-start(bf16[4,4,32,128]{3,2,1,0:T(8,128)(2,1)} %saved_ref.11) | copy-start | bytes 393220
  30.0 2.2 %copy-start.4 = (f32[3,32,32]{2,1,0:T(8,128)S(1)}, f32[3,32,32]{2,1,0:T(8,128)}, u32[]{:S(2)}) copy-start(f32[3,32,32]{2,1,0:T(8,128)} %dual_mix_ref.5) | copy-start | bytes 36868
  30.0 2.2 %copy-start.5 = (f32[3,32,32]{2,1,0:T(8,128)S(1)}, f32[3,32,32]{2,1,0:T(8,128)}, u32[]{:S(2)}) copy-start(f32[3,32,32]{2,1,0:T(8,128)} %primal_mix_ref.5) | copy-start | bytes 36868
  30.0 2.2 %copy-start.8 = (f32[4,32,128]{2,1,0:T(8,128)S(1)}, f32[4,32,128]{2,1,0:T(8,128)}, u32[]{:S(2)}) copy-start(f32[4,32,128]{2,1,0:T(8,128)} %grad_in.1) | copy-start | bytes 196612
  30.8 1.4 %collective-permute-start = (f32[4,64,128]{2,1,0:T(8,128)S(1)}, f32[4,64,128]{2,1,0:T(8,128)S(1)}, u32[]{:S(2)}, u32[]{:S(2)}) collective-permute-start(f32[4,64,128]{2,1,0:T(8,128)S(1)} %shard_map.148.mine_ref), channel_id=1, source_target_pairs={{0,1},{1,0},{2,3},{3,2},{4,5},{5,4},{6,7},{7,6},{8,9},{9,8},{10,11... | collective-permute-start | bytes 393224 | tf_op jit(solution)/shard_map/ppermute | solution.py:230
  31.1 1.2 %copy-start.9 = (s32[3,4,128]{2,1,0:T(4,128)S(1)}, s32[3,4,128]{2,1,0:T(4,128)}, u32[]{:S(2)}) copy-start(s32[3,4,128]{2,1,0:T(4,128)} %mask_ref.11) | copy-start | bytes 18436
  34.2 10.1 %copy-start.2 = (bf16[3,8,32,128]{3,2,1,0:T(8,128)(2,1)S(1)}, bf16[3,8,32,128]{3,2,1,0:T(8,128)(2,1)}, u32[]{:S(2)}) copy-start(bf16[3,8,32,128]{3,2,1,0:T(8,128)(2,1)} %saved_ref.10) | copy-start | bytes 589828
  55.6 1.4 %collective-permute-start.1 = (f32[4,64,128]{2,1,0:T(8,128)S(1)}, f32[4,64,128]{2,1,0:T(8,128)S(1)}, u32[]{:S(2)}, u32[]{:S(2)}) collective-permute-start(f32[4,64,128]{2,1,0:T(8,128)S(1)} %shard_map.151.mine_ref), channel_id=1, source_target_pairs={{0,1},{1,0},{2,3},{3,2},{4,5},{5,4},{6,7},{7,6},{8,9},{9,8},{10,11... | collective-permute-start | bytes 393224 | tf_op jit(solution)/shard_map/ppermute | solution.py:230
  80.2 1.4 %collective-permute-start.2 = (f32[4,64,128]{2,1,0:T(8,128)S(1)}, f32[4,64,128]{2,1,0:T(8,128)S(1)}, u32[]{:S(2)}, u32[]{:S(2)}) collective-permute-start(f32[4,64,128]{2,1,0:T(8,128)S(1)} %shard_map.154.mine_ref), channel_id=1, source_target_pairs={{0,1},{1,0},{2,3},{3,2},{4,5},{5,4},{6,7},{7,6},{8,9},{9,8},{10,11... | collective-permute-start | bytes 393224 | tf_op jit(solution)/shard_map/ppermute | solution.py:230

commit v2 on v1

v2 whole, which is shorter than its diff:
```python
from functools import partial
import math

import jax
import jax.numpy as jnp
from jax import lax
from jax.experimental import pallas as pl
from jax.experimental.pallas import tpu as pltpu
from jax.sharding import PartitionSpec as P

SMEM = pl.BlockSpec(memory_space=pltpu.SMEM)
VMEM = pl.BlockSpec(memory_space=pltpu.VMEM)
F32 = jnp.float32
BF16 = jnp.bfloat16


def loop(count, body):
    if count <= 16:
        for i in range(count):
            body(i)
    else:
        lax.fori_loop(0, count, lambda i, _: (body(i), 0)[1], 0)


def total_of(count, term, shape):
    if count <= 16:
        total = term(0)
        for i in range(1, count):
            total = total + term(i)
        return total
    return lax.fori_loop(0, count, lambda i, t: t + term(i), jnp.zeros(shape, F32))


def halves(x):
    high = x.astype(BF16)
    return high, (x - high.astype(F32)).astype(BF16)


def prepare_kernel(
    peer_size,
    primal_count,
    rows_ref,
    cols_ref,
    steps_ref,
    tiles_in,
    cot_in,
    mask_ref,
    saved_ref,
    dual_mix_ref,
    primal_mix_ref,
    tiles_ref,
    place_ref,
    scale_ref,
    mix_ref,
    cot_ref,
    base_ref,
    pad_ref,
):
    owned, channels, side = cot_ref.shape
    layers = dual_mix_ref.shape[0]

    def one(t):
        peer = lax.div(rows_ref[t], peer_size)
        tiles_ref[peer] = tiles_in[t]
        p = lax.rem(cols_ref[t], primal_count)
        place_ref[peer] = jnp.full(place_ref.shape[1:], p.astype(F32), F32)

    loop(tiles_ref.shape[0], one)
    for k in range(layers):
        for s in range(2):
            upper = jnp.full((1, side), steps_ref[k, 2 * s].astype(F32), F32)
            lower = jnp.full((1, side), steps_ref[k, 2 * s + 1].astype(F32), F32)
            scale_ref[pl.ds(2 * k + s, 1), :] = -(upper / lower)
    pad_ref[...] = jnp.zeros_like(pad_ref)
    for k in range(layers):
        for s, ref in enumerate((primal_mix_ref, dual_mix_ref)):
            pad_ref[:, :channels] = ref[k]
            weights = pad_ref[...]
            high = weights.astype(BF16).astype(F32)
            rest = weights - high
            mix_ref[2 * k + s] = (
                high
                + pltpu.roll(high, channels, 1)
                + pltpu.roll(rest, 2 * channels, 1)
                + pltpu.roll(rest, 3 * channels, 1)
            ).astype(BF16)
    for b in range(owned):
        cot = mask_ref[layers - 1, pl.ds(b, 1), :].astype(F32) * cot_in[b]
        cot_ref[b] = cot
        base_ref[b, :channels, :] = cot.astype(BF16)
        base_ref[b, channels:, :] = saved_ref[layers - 1, b]


def choose(place_ref, base, send_ref):
    copies = base[0].shape[0] // place_ref.shape[1]

    def one(r):
        place = jnp.concatenate([place_ref[r]] * copies, 0)
        picked = base[0]
        for b in range(1, len(base)):
            picked = jnp.where(place == b, base[b], picked)
        send_ref[r] = picked.astype(BF16)

    loop(send_ref.shape[0], one)


def first_dual_kernel(wanted_ref, base_ref, send_ref):
    owned = base_ref.shape[0]
    choose(wanted_ref, [base_ref[b].astype(F32) for b in range(owned)], send_ref)


def add_pushed(wanted_ref, received_ref, cot_ref):
    owned, channels, side = cot_ref.shape
    rows = received_ref.shape[0]
    copies = channels // wanted_ref.shape[1]
    place = lambda r: jnp.concatenate([wanted_ref[r]] * copies, 0)
    if rows <= 16:
        blocks = [cot_ref[b] for b in range(owned)]
        for r in range(rows):
            at, pushed = place(r), received_ref[r, :channels, :].astype(F32)
            blocks = [block + jnp.where(at == b, pushed, 0.0) for b, block in enumerate(blocks)]
        return blocks

    def step(r, blocks):
        at, pushed = place(r), received_ref[r, :channels, :].astype(F32)
        return tuple(block + jnp.where(at == b, pushed, 0.0) for b, block in enumerate(blocks))

    return list(lax.fori_loop(0, rows, step, tuple(cot_ref[b] for b in range(owned))))


def sum_terms(received_ref):
    rows, height, side = received_ref.shape
    channels = height // 2
    return total_of(
        rows, lambda r: received_ref[r, channels:, :].astype(F32), (channels, side)
    )


def dual_kernel(
    layer, wanted_ref, received_ref, cot_in, mask_ref, saved_ref, cot_ref, send_ref, terms_ref
):
    base = []
    for b, block in enumerate(add_pushed(wanted_ref, received_ref, cot_in)):
        cot = mask_ref[layer, pl.ds(b, 1), :].astype(F32) * block
        cot_ref[b] = cot
        base.append(jnp.concatenate([cot, saved_ref[layer, b].astype(F32)], 0))
    choose(wanted_ref, base, send_ref)
    terms_ref[...] = sum_terms(received_ref)


def last_dual_kernel(
    row_scale, col_scale, wanted_ref, received_ref, cot_in, scale_ref, *refs
):
    terms_refs, (cot_ref, primal_ref, dual_ref) = refs[:-3], refs[-3:]
    channels = cot_ref.shape[1]
    layers = primal_ref.shape[0]
    for b, block in enumerate(add_pushed(wanted_ref, received_ref, cot_in)):
        cot_ref[b] = block
    for k in range(layers):
        terms = sum_terms(received_ref) if k == 0 else terms_refs[k - 1][...]
        side = terms.shape[1]
        terms = terms + pltpu.roll(terms, side - channels, 1)
        dual = scale_ref[pl.ds(2 * k + 1, 1), :] * row_scale * terms
        primal = scale_ref[pl.ds(2 * k, 1), :] * col_scale * terms
        dual_ref[k] = dual[:, :channels]
        primal_ref[k] = pltpu.roll(primal, side - 2 * channels, 1)[:, :channels]


def pull_kernel(tiles_ref, place_ref, received_ref, sum_ref):
    count = sum_ref.shape[0]
    rows = tiles_ref.shape[0]
    copies = received_ref.shape[1] // place_ref.shape[1]

    def step(t, sums):
        product = jnp.dot(received_ref[t], tiles_ref[t], preferred_element_type=F32)
        at = jnp.concatenate([place_ref[t]] * copies, 0)
        return tuple(s + jnp.where(at == p, product, 0.0) for p, s in enumerate(sums))

    sums = tuple(jnp.zeros(sum_ref.shape[1:], F32) for _ in range(count))
    if rows <= 16:
        for t in range(rows):
            sums = step(t, sums)
    else:
        sums = lax.fori_loop(0, rows, step, sums)
    for p in range(count):
        sum_ref[p] = sums[p]


def primal_kernel(
    layer,
    tiles_ref,
    place_ref,
    scale_ref,
    mix_ref,
    mine_ref,
    other_ref,
    grad_in,
    mask_ref,
    saved_ref,
    grad_ref,
    send_ref,
):
    blocks, channels, side = grad_ref.shape
    sigma = scale_ref[pl.ds(2 * layer + 1, 1), :]
    tau = scale_ref[pl.ds(2 * layer, 1), :]

    def mix(weights, x):
        high, rest = halves(x)
        return jnp.dot(
            weights, jnp.concatenate([high, rest, high, rest], 0), preferred_element_type=F32
        )

    mixed, left, right = [], [], []
    for p in range(blocks):
        both = mine_ref[p] + other_ref[p]
        pulled_mixed, pulled_saved = both[:channels], both[channels:]
        back = sigma * mix(mix_ref[2 * layer + 1], pulled_mixed)
        primal_cot = mask_ref[layer, pl.ds(p, 1), :].astype(F32) * (grad_in[p] + 2.0 * back)
        grad_ref[p] = primal_cot - back
        mixed.append((tau * mix(mix_ref[2 * layer], primal_cot)).astype(BF16).astype(F32))
        extrapolated = (
            2.0 * saved_ref[layer + 1, p].astype(F32) - saved_ref[layer, p].astype(F32)
        ).astype(BF16)
        left.append(jnp.concatenate([extrapolated, *halves(pulled_saved)], 0))
        right.append(jnp.concatenate([*halves(pulled_mixed), *halves(primal_cot)], 0))
    terms = lax.dot_general(
        jnp.concatenate(left, 1),
        jnp.concatenate(right, 1),
        (((1,), (1,)), ((), ())),
        preferred_element_type=F32,
    )
    lane = lax.broadcasted_iota(jnp.int32, (channels, side), 1)
    terms = jnp.where(
        lane < 2 * channels,
        terms[:channels],
        terms[channels : 2 * channels] + terms[2 * channels :],
    )
    terms = terms + pltpu.roll(terms, side - channels, 1)
    high = terms.astype(BF16).astype(F32)
    rest = pltpu.roll(terms - high, channels, 1)
    packed = jnp.where(lax.rem(lane, 2 * channels) < channels, high, rest).astype(BF16)
    copies = channels // place_ref.shape[1]

    def one(t):
        at = jnp.concatenate([place_ref[t]] * copies, 0)
        picked = mixed[0]
        for p in range(1, blocks):
            picked = jnp.where(at == p, mixed[p], picked)
        product = lax.dot_general(
            picked.astype(BF16),
            tiles_ref[t],
            (((1,), (1,)), ((), ())),
            preferred_element_type=F32,
        )
        send_ref[t, :channels, :] = product.astype(BF16)
        send_ref[t, channels:, :] = packed

    loop(tiles_ref.shape[0], one)


def per_device(
    tile_blocks,
    tile_rows,
    tile_cols,
    saved_primal,
    saved_dual,
    primal_active,
    dual_active,
    primal_mix,
    dual_mix,
    step_fracs,
    cot_primal,
    cot_dual,
):
    row_count = lax.axis_size("row")
    col_count = lax.axis_size("col")
    owned, channels, side = cot_dual.shape
    primal_count = cot_primal.shape[0]
    layer_count = primal_mix.shape[0]
    row_scale = 1.0 / math.sqrt(owned * row_count * col_count * side)
    col_scale = 1.0 / math.sqrt(primal_count * row_count * side)
    params = pltpu.CompilerParams(vmem_limit_bytes=16 * 1024 * 1024)

    def call(kernel, outs, *operands, smem=0, **rest):
        return pl.pallas_call(
            kernel,
            out_shape=outs,
            in_specs=[SMEM] * smem + [VMEM] * (len(operands) - smem),
            out_specs=jax.tree.map(lambda _: VMEM, outs),
            compiler_params=params,
            **rest,
        )(*operands)

    def exchange(x):
        return lax.all_to_all(x, "row", split_axis=0, concat_axis=0, tiled=True)

    def shape(dims, kind=F32):
        return jax.ShapeDtypeStruct(dims, kind)

    peers = tile_rows // (owned * col_count)
    peer_ids = jnp.arange(row_count, dtype=jnp.int32)
    asked = jnp.sum(
        jnp.where(peers[None, :] == peer_ids[:, None], (tile_rows % owned)[None, :], 0), axis=1
    )
    wanted = exchange(
        jnp.broadcast_to(asked.astype(F32)[:, None, None], (row_count, 8, side))
    )
    message = shape((row_count, 2 * channels, side), BF16)
    tiles, place, scale, mix, cot, base = call(
        partial(prepare_kernel, owned * col_count, primal_count),
        (
            shape(tile_blocks.shape, BF16),
            shape((row_count, 8, side)),
            shape((2 * layer_count, side)),
            shape((2 * layer_count, channels, side), BF16),
            shape(cot_dual.shape),
            shape((owned, 2 * channels, side), BF16),
        ),
        tile_rows,
        tile_cols,
        step_fracs,
        tile_blocks,
        cot_dual,
        dual_active,
        saved_dual,
        dual_mix,
        primal_mix,
        smem=3,
        scratch_shapes=[pltpu.VMEM((channels, side), F32)],
    )
    swap = [(i, col_count - 1 - i) for i in range(col_count)]
    grad_x = cot_primal
    received = None
    all_terms = []
    for layer in reversed(range(layer_count)):
        if received is None:
            send = call(first_dual_kernel, message, wanted, base)
        else:
            cot, send, terms = call(
                partial(dual_kernel, layer),
                (shape(cot_dual.shape), message, shape((channels, side))),
                wanted,
                received,
                cot,
                dual_active,
                saved_dual,
            )
            all_terms.insert(0, terms)
        fetched = exchange(send)
        mine = call(
            pull_kernel, shape((primal_count, 2 * channels, side)), tiles, place, fetched
        )
        other = lax.ppermute(mine, "col", swap)
        grad_x, push = call(
            partial(primal_kernel, layer),
            (shape(cot_primal.shape), message),
            tiles,
            place,
            scale,
            mix,
            mine,
            other,
            grad_x,
            primal_active,
            saved_primal,
        )
        received = exchange(push)
    grad_y, primal_mix_grad, dual_mix_grad = call(
        partial(last_dual_kernel, row_scale, col_scale),
        (shape(cot_dual.shape), shape(primal_mix.shape), shape(dual_mix.shape)),
        wanted,
        received,
        cot,
        scale,
        *all_terms,
    )
    return (grad_x, grad_y, primal_mix_grad, dual_mix_grad)


def solution(mesh):
    return jax.shard_map(
        per_device,
        mesh=mesh,
        in_specs=(
            P(("groups", "row", "col"), None, None),
            P(("groups", "row", "col")),
            P(("groups", "row", "col")),
            P(None, ("groups", "row"), None, None),
            P(None, ("groups", "row", "col"), None, None),
            P(None, ("groups", "row"), None),
            P(None, ("groups", "row", "col"), None),
            P(),
            P(),
            P(),
            P(("groups", "row"), None, None),
            P(("groups", "row", "col"), None, None),
        ),
        out_specs=(
            P(("groups", "row"), None, None),
            P(("groups", "row", "col"), None, None),
            P("groups", None, None),
            P("groups", None, None),
        ),
        check_vma=False,
    )
```

time: 96.4 us -> 85.5 us (0.89)
  waiting for transfers between devices: 17.3 us -> 6.33 us
  blocking collectives: 49.7 us -> 60.5 us
  Pallas kernels: 12.3 us -> 4.64 us
  starting transfers between devices: 11.1 us -> 7.61 us
  local copies, waits for them, and re-layouts: 2.54 us -> 4.3 us
  other arithmetic: 2.02 us -> 0.79 us
    all_to_all x2 -> x1, waiting for transfers between devices: 13.6 us -> 2.33 us  [exchange(): return lax.all_to_all(x, 'row', split_axis=0, concat_axis=0, tiled=True)]
    all_to_all x5 -> x6, blocking collectives: 49.7 us -> 60.5 us  [exchange(): return lax.all_to_all(x, 'row', split_axis=0, concat_axis=0, tiled=True)]
    pallas_call x10 -> x11, Pallas kernels: 12.3 us -> 4.64 us  [call(): pl.pallas_call(kernel, out_shape=outs, in_specs=[SMEM] * smem + [VMEM] *...]
    all_to_all x2 -> x1, starting transfers between devices: 10.9 us -> 7.4 us  [exchange(): return lax.all_to_all(x, 'row', split_axis=0, concat_axis=0, tiled=True)]
    unnamed x24 -> x26, local copies, waits for them, and re-layouts: 1.87 us -> 3.61 us
  transfers between devices with their start and end apart: 5 -> 4, of which waited for: 5 -> 4; matrix products, arithmetic and copies ran while one was open for 0% -> 0% of each run, Pallas kernels for 0% -> 1%
where the time goes in v2:
time: 85.5 us; the launch traced here: 85 us
  blocking collectives  60.5 us (71%)
  starting transfers between devices  7.61 us (9%)
  waiting for transfers between devices  6.33 us (7%)
  Pallas kernels  4.64 us (5%)
  local copies, waits for them, and re-layouts  4.3 us (5%)
    all_to_all x6, blocking collectives, exchange(): return lax.all_to_all(x, 'row', split_axis=0, concat_axis=0, tiled=True)  60.5 us
    all_to_all x1, starting transfers between devices, exchange(): return lax.all_to_all(x, 'row', split_axis=0, concat_axis=0, tiled=True)  7.4 us
    pallas_call x11, Pallas kernels, call(): pl.pallas_call(kernel, out_shape=outs, in_specs=[SMEM] * smem + [VMEM] *...  4.64 us
    ppermute x3, waiting for transfers between devices, per_device(): other = lax.ppermute(mine, 'col', swap)  4 us
    unnamed x26, local copies, waits for them, and re-layouts  3.61 us
    all_to_all x1, waiting for transfers between devices, exchange(): return lax.all_to_all(x, 'row', split_axis=0, concat_axis=0, tiled=True)  2.33 us
  transfers between devices with their start and end apart: 4, of which 4 were waited for; matrix products, arithmetic and copies ran while one was open for 0% of the time, Pallas kernels for 1%

profile of v2, /device:TPU:0, one launch (start us, length us, event | category | flops | bytes accessed | tf_op | source)
XLA Modules:
  0.0 85.0 jit_solution(17728294145452044062)
XLA Ops:
  0.6 0.7 and_select_fusion.1
  1.4 0.7 broadcast_in_dim.23
  2.1 7.4 %all-to-all-start = ((f32[8,8,128]{2,1,0:T(8,128)}), f32[8,8,128]{2,1,0:T(8,128)S(1)}, u32[]{:S(2)}, u32[]{:S(2)}) async-start(f32[8,8,128]{2,1,0:T(8,128)} %broadcast_in_dim.23), calls=%async_computation | async-start | bytes 65536 | tf_op jit(solution)/shard_map/all_to_all | solution.py:295
  9.6 0.9 %copy-done = bf16[3,8,32,128]{3,2,1,0:T(8,128)(2,1)S(1)} copy-done((bf16[3,8,32,128]{3,2,1,0:T(8,128)(2,1)S(1)}, bf16[3,8,32,128]{3,2,1,0:T(8,128)(2,1)}, u32[]{:S(2)}) %copy-start) | copy-done | bytes 196632
  10.5 0.9 %copy-done.3 = bf16[8,128,128]{2,1,0:T(8,128)(2,1)S(1)} copy-done((bf16[8,128,128]{2,1,0:T(8,128)(2,1)S(1)}, bf16[8,128,128]{2,1,0:T(8,128)(2,1)}, u32[]{:S(2)}) %copy-start.3) | copy-done | bytes 262168
  11.5 0.9 %copy-done.4 = f32[8,32,128]{2,1,0:T(8,128)S(1)} copy-done((f32[8,32,128]{2,1,0:T(8,128)S(1)}, f32[8,32,128]{2,1,0:T(8,128)}, u32[]{:S(2)}) %copy-start.4) | copy-done | bytes 131096
  12.4 0.8 copy-done.9
  13.2 0.7 shard_map.147
  13.9 2.3 %all-to-all-done.wanted_ref = f32[8,8,128]{2,1,0:T(8,128)S(1)} async-done(((f32[8,8,128]{2,1,0:T(8,128)}), f32[8,8,128]{2,1,0:T(8,128)S(1)}, u32[]{:S(2)}, u32[]{:S(2)}) %all-to-all-start) | async-done | bytes 32800 | tf_op jit(solution)/shard_map/all_to_all | solution.py:295
  16.3 10.8 %all_to_all.35.received_ref = bf16[8,64,128]{2,1,0:T(8,128)(2,1)S(1)} all-to-all(bf16[8,64,128]{2,1,0:T(8,128)(2,1)S(1)} %shard_map.148), channel_id=1, replica_groups=mesh['groups'=2,'row'=8,'col'=2] {'row'}, dimensions={0} | all-to-all | bytes 262144 | tf_op jit(solution)/shard_map/all_to_all | solution.py:295
  27.1 0.2 shard_map.149.mine_ref
  27.4 1.3 %collective-permute-done.other_ref = f32[4,64,128]{2,1,0:T(8,128)S(1)} collective-permute-done((f32[4,64,128]{2,1,0:T(8,128)S(1)}, f32[4,64,128]{2,1,0:T(8,128)S(1)}, u32[]{:S(2)}, u32[]{:S(2)}) %collective-permute-start) | collective-permute-done | bytes 131104 | tf_op jit(solution)/shard_map/ppermute | solution.py:353
  28.8 0.6 shard_map.150
  29.4 10.1 %all_to_all.36.received_ref = bf16[8,64,128]{2,1,0:T(8,128)(2,1)S(1)} all-to-all(bf16[8,64,128]{2,1,0:T(8,128)(2,1)S(1)} %get-tuple-element.30), channel_id=1, replica_groups=mesh['groups'=2,'row'=8,'col'=2] {'row'}, dimensions={0} | all-to-all | bytes 262144 | tf_op jit(solution)/shard_map/all_to_all | solution.py:295
  39.6 9.8 %all_to_all.37.received_ref = bf16[8,64,128]{2,1,0:T(8,128)(2,1)S(1)} all-to-all(bf16[8,64,128]{2,1,0:T(8,128)(2,1)S(1)} %get-tuple-element.32), channel_id=1, replica_groups=mesh['groups'=2,'row'=8,'col'=2] {'row'}, dimensions={0} | all-to-all | bytes 262144 | tf_op jit(solution)/shard_map/all_to_all | solution.py:295
  49.5 0.2 shard_map.152.mine_ref
  49.8 1.3 %collective-permute-done.1.other_ref = f32[4,64,128]{2,1,0:T(8,128)S(1)} collective-permute-done((f32[4,64,128]{2,1,0:T(8,128)S(1)}, f32[4,64,128]{2,1,0:T(8,128)S(1)}, u32[]{:S(2)}, u32[]{:S(2)}) %collective-permute-start.1) | collective-permute-done | bytes 131104 | tf_op jit(solution)/shard_map/ppermute | solution.py:353
  51.1 0.6 shard_map.153
  51.7 10.0 %all_to_all.38.received_ref = bf16[8,64,128]{2,1,0:T(8,128)(2,1)S(1)} all-to-all(bf16[8,64,128]{2,1,0:T(8,128)(2,1)S(1)} %get-tuple-element.34), channel_id=1, replica_groups=mesh['groups'=2,'row'=8,'col'=2] {'row'}, dimensions={0} | all-to-all | bytes 262144 | tf_op jit(solution)/shard_map/all_to_all | solution.py:295
  61.8 9.8 %all_to_all.39.received_ref = bf16[8,64,128]{2,1,0:T(8,128)(2,1)S(1)} all-to-all(bf16[8,64,128]{2,1,0:T(8,128)(2,1)S(1)} %get-tuple-element.36), channel_id=1, replica_groups=mesh['groups'=2,'row'=8,'col'=2] {'row'}, dimensions={0} | all-to-all | bytes 262144 | tf_op jit(solution)/shard_map/all_to_all | solution.py:295
  72.0 1.3 %collective-permute-done.2.other_ref = f32[4,64,128]{2,1,0:T(8,128)S(1)} collective-permute-done((f32[4,64,128]{2,1,0:T(8,128)S(1)}, f32[4,64,128]{2,1,0:T(8,128)S(1)}, u32[]{:S(2)}, u32[]{:S(2)}) %collective-permute-start.2) | collective-permute-done | bytes 131104 | tf_op jit(solution)/shard_map/ppermute | solution.py:353
  73.3 0.8 shard_map.156
  74.2 10.0 %all_to_all.40.received_ref = bf16[8,64,128]{2,1,0:T(8,128)(2,1)S(1)} all-to-all(bf16[8,64,128]{2,1,0:T(8,128)(2,1)S(1)} %get-tuple-element.39), channel_id=1, replica_groups=mesh['groups'=2,'row'=8,'col'=2] {'row'}, dimensions={0} | all-to-all | bytes 262144 | tf_op jit(solution)/shard_map/all_to_all | solution.py:295
  84.1 0.8 shard_map.157
  (31 shorter events, 1.0 us)
Async XLA Ops:
  1.4 8.1 %copy-start.8 = (f32[3,32,32]{2,1,0:T(8,128)S(1)}, f32[3,32,32]{2,1,0:T(8,128)}, u32[]{:S(2)}) copy-start(f32[3,32,32]{2,1,0:T(8,128)} %dual_mix_ref.1) | copy-start | bytes 36868
  2.1 7.4 %copy-start.5 = (s32[3,8,128]{2,1,0:T(8,128)S(1)}, s32[3,8,128]{2,1,0:T(8,128)}, u32[]{:S(2)}) copy-start(s32[3,8,128]{2,1,0:T(8,128)} %mask_ref.10) | copy-start | bytes 36868
  2.1 7.4 %copy-start.10 = (s32[3,4]{1,0:T(4,128)S(1)}, s32[3,4]{1,0:T(4,128)}, u32[]{:S(2)}) copy-start(s32[3,4]{1,0:T(4,128)} %steps_ref.1) | copy-start | bytes 148
  2.1 7.4 %copy-start.11 = (s32[8]{0:T(128)S(1)}, s32[8]{0:T(128)}, u32[]{:S(2)}) copy-start(s32[8]{0:T(128)} %rows_ref.1) | copy-start | bytes 100
  2.1 7.4 %copy-start.12 = (s32[8]{0:T(128)S(1)}, s32[8]{0:T(128)}, u32[]{:S(2)}) copy-start(s32[8]{0:T(128)} %cols_ref.1) | copy-start | bytes 100
  2.1 14.1 %all-to-all-start = ((f32[8,8,128]{2,1,0:T(8,128)}), f32[8,8,128]{2,1,0:T(8,128)S(1)}, u32[]{:S(2)}, u32[]{:S(2)}) async-start(f32[8,8,128]{2,1,0:T(8,128)} %broadcast_in_dim.23), calls=%async_computation | async-start | bytes 65536 | tf_op jit(solution)/shard_map/all_to_all | solution.py:295
  9.6 0.9 %copy-start = (bf16[3,8,32,128]{3,2,1,0:T(8,128)(2,1)S(1)}, bf16[3,8,32,128]{3,2,1,0:T(8,128)(2,1)}, u32[]{:S(2)}) copy-start(bf16[3,8,32,128]{3,2,1,0:T(8,128)(2,1)} %saved_ref.10) | copy-start | bytes 589828
  10.5 0.9 %copy-start.3 = (bf16[8,128,128]{2,1,0:T(8,128)(2,1)S(1)}, bf16[8,128,128]{2,1,0:T(8,128)(2,1)}, u32[]{:S(2)}) copy-start(bf16[8,128,128]{2,1,0:T(8,128)(2,1)} %tiles_in.1) | copy-start | bytes 786436
  11.5 0.9 %copy-start.4 = (f32[8,32,128]{2,1,0:T(8,128)S(1)}, f32[8,32,128]{2,1,0:T(8,128)}, u32[]{:S(2)}) copy-start(f32[8,32,128]{2,1,0:T(8,128)} %cot_in.1) | copy-start | bytes 393220
  12.4 0.8 copy-start.9
  27.1 1.7 %copy-start.2 = (bf16[4,4,32,128]{3,2,1,0:T(8,128)(2,1)S(1)}, bf16[4,4,32,128]{3,2,1,0:T(8,128)(2,1)}, u32[]{:S(2)}) copy-start(bf16[4,4,32,128]{3,2,1,0:T(8,128)(2,1)} %saved_ref.11) | copy-start | bytes 393220
  27.1 1.7 %copy-start.6 = (f32[4,32,128]{2,1,0:T(8,128)S(1)}, f32[4,32,128]{2,1,0:T(8,128)}, u32[]{:S(2)}) copy-start(f32[4,32,128]{2,1,0:T(8,128)} %grad_in.1) | copy-start | bytes 196612
  27.1 1.7 %copy-start.7 = (s32[3,4,128]{2,1,0:T(4,128)S(1)}, s32[3,4,128]{2,1,0:T(4,128)}, u32[]{:S(2)}) copy-start(s32[3,4,128]{2,1,0:T(4,128)} %mask_ref.11) | copy-start | bytes 18436
  27.4 1.4 %collective-permute-start = (f32[4,64,128]{2,1,0:T(8,128)S(1)}, f32[4,64,128]{2,1,0:T(8,128)S(1)}, u32[]{:S(2)}, u32[]{:S(2)}) collective-permute-start(f32[4,64,128]{2,1,0:T(8,128)S(1)} %shard_map.149.mine_ref), channel_id=1, source_target_pairs={{0,1},{1,0},{2,3},{3,2},{4,5},{5,4},{6,7},{7,6},{8,9},{9,8},{10,11... | collective-permute-start | bytes 393224 | tf_op jit(solution)/shard_map/ppermute | solution.py:353
  29.4 10.1 %copy-start.1 = (bf16[3,8,32,128]{3,2,1,0:T(8,128)(2,1)S(1)}, bf16[3,8,32,128]{3,2,1,0:T(8,128)(2,1)}, u32[]{:S(2)}) copy-start(bf16[3,8,32,128]{3,2,1,0:T(8,128)(2,1)} %saved_ref.10) | copy-start | bytes 589828
  49.7 1.4 %collective-permute-start.1 = (f32[4,64,128]{2,1,0:T(8,128)S(1)}, f32[4,64,128]{2,1,0:T(8,128)S(1)}, u32[]{:S(2)}, u32[]{:S(2)}) collective-permute-start(f32[4,64,128]{2,1,0:T(8,128)S(1)} %shard_map.152.mine_ref), channel_id=1, source_target_pairs={{0,1},{1,0},{2,3},{3,2},{4,5},{5,4},{6,7},{7,6},{8,9},{9,8},{10,11... | collective-permute-start | bytes 393224 | tf_op jit(solution)/shard_map/ppermute | solution.py:353
  71.9 1.4 %collective-permute-start.2 = (f32[4,64,128]{2,1,0:T(8,128)S(1)}, f32[4,64,128]{2,1,0:T(8,128)S(1)}, u32[]{:S(2)}, u32[]{:S(2)}) collective-permute-start(f32[4,64,128]{2,1,0:T(8,128)S(1)} %shard_map.155.mine_ref), channel_id=1, source_target_pairs={{0,1},{1,0},{2,3},{3,2},{4,5},{5,4},{6,7},{7,6},{8,9},{9,8},{10,11... | collective-permute-start | bytes 393224 | tf_op jit(solution)/shard_map/ppermute | solution.py:353

commit v3 on v2

--- a/solution.py
+++ b/solution.py
@@ -10,6 +10,7 @@
 
 SMEM = pl.BlockSpec(memory_space=pltpu.SMEM)
 VMEM = pl.BlockSpec(memory_space=pltpu.VMEM)
+HBM = pl.BlockSpec(memory_space=pltpu.HBM)
 F32 = jnp.float32
 BF16 = jnp.bfloat16
 
@@ -44,10 +45,10 @@
     steps_ref,
     tiles_in,
     cot_in,
-    mask_ref,
-    saved_ref,
-    dual_mix_ref,
-    primal_mix_ref,
+    mask_in,
+    saved_in,
+    dual_mix_in,
+    primal_mix_in,
     tiles_ref,
     place_ref,
     scale_ref,
@@ -55,15 +56,39 @@
     cot_ref,
     base_ref,
     pad_ref,
+    mask_ref,
+    saved_ref,
+    mixes_ref,
+    sems,
+    tile_sems,
 ):
     owned, channels, side = cot_ref.shape
-    layers = dual_mix_ref.shape[0]
+    layers = dual_mix_in.shape[0]
+    fetches = [
+        pltpu.make_async_copy(source, target, sems.at[i])
+        for i, (source, target) in enumerate(
+            (
+                (cot_in, cot_ref),
+                (saved_in.at[layers - 1], saved_ref),
+                (mask_in.at[layers - 1], mask_ref),
+                (primal_mix_in, mixes_ref.at[0]),
+                (dual_mix_in, mixes_ref.at[1]),
+            )
+        )
+    ]
+    for fetch in fetches:
+        fetch.start()
+
+    def fetch_tile(t):
+        peer = lax.div(rows_ref[t], peer_size)
+        return pltpu.make_async_copy(tiles_in.at[t], tiles_ref.at[peer], tile_sems.at[t])
+
+    loop(tiles_ref.shape[0], lambda t: fetch_tile(t).start())
 
     def one(t):
-        peer = lax.div(rows_ref[t], peer_size)
-        tiles_ref[peer] = tiles_in[t]
         p = lax.rem(cols_ref[t], primal_count)
-        place_ref[peer] = jnp.full(place_ref.shape[1:], p.astype(F32), F32)
+        filled = jnp.full(place_ref.shape[1:], p.astype(F32), F32)
+        place_ref[lax.div(rows_ref[t], peer_size)] = filled
 
     loop(tiles_ref.shape[0], one)
     for k in range(layers):
@@ -72,10 +97,17 @@
             lower = jnp.full((1, side), steps_ref[k, 2 * s + 1].astype(F32), F32)
             scale_ref[pl.ds(2 * k + s, 1), :] = -(upper / lower)
     pad_ref[...] = jnp.zeros_like(pad_ref)
+    for fetch in fetches:
+        fetch.wait()
+    for b in range(owned):
+        cot = mask_ref[pl.ds(b, 1), :].astype(F32) * cot_ref[b]
+        cot_ref[b] = cot
+        base_ref[b, :channels, :] = cot.astype(BF16)
+        base_ref[b, channels:, :] = saved_ref[b]
     for k in range(layers):
-        for s, ref in enumerate((primal_mix_ref, dual_mix_ref)):
-            pad_ref[:, :channels] = ref[k]
-            weights = pad_ref[...]
+        for s in range(2):
+            pad_ref[2 * k + s, :, :channels] = mixes_ref[s, k]
+            weights = pad_ref[2 * k + s]
             high = weights.astype(BF16).astype(F32)
             rest = weights - high
             mix_ref[2 * k + s] = (
@@ -84,11 +116,7 @@
                 + pltpu.roll(rest, 2 * channels, 1)
                 + pltpu.roll(rest, 3 * channels, 1)
             ).astype(BF16)
-    for b in range(owned):
-        cot = mask_ref[layers - 1, pl.ds(b, 1), :].astype(F32) * cot_in[b]
-        cot_ref[b] = cot
-        base_ref[b, :channels, :] = cot.astype(BF16)
-        base_ref[b, channels:, :] = saved_ref[layers - 1, b]
+    loop(tiles_ref.shape[0], lambda t: fetch_tile(t).wait())
 
 
 def choose(place_ref, base, send_ref):
@@ -128,11 +156,10 @@
     return list(lax.fori_loop(0, rows, step, tuple(cot_ref[b] for b in range(owned))))
 
 
-def sum_terms(received_ref):
+def sum_terms(received_ref, channels):
     rows, height, side = received_ref.shape
-    channels = height // 2
     return total_of(
-        rows, lambda r: received_ref[r, channels:, :].astype(F32), (channels, side)
+        rows, lambda r: received_ref[r, channels:, :].astype(F32), (height - channels, side)
     )
 
 
@@ -145,25 +172,37 @@
         cot_ref[b] = cot
         base.append(jnp.concatenate([cot, saved_ref[layer, b].astype(F32)], 0))
     choose(wanted_ref, base, send_ref)
-    terms_ref[...] = sum_terms(received_ref)
+    terms_ref[...] = sum_terms(received_ref, cot_ref.shape[1])
 
 
 def last_dual_kernel(
-    row_scale, col_scale, wanted_ref, received_ref, cot_in, scale_ref, *refs
+    row_scale, col_scale, wanted_ref, received_ref, cot_in, scale_ref, grad_in, *refs
 ):
-    terms_refs, (cot_ref, primal_ref, dual_ref) = refs[:-3], refs[-3:]
-    channels = cot_ref.shape[1]
+    terms_refs, refs = refs[:-8], refs[-8:]
+    grad_ref, cot_ref, primal_out, dual_out, held_ref, primal_ref, dual_ref, sems = refs
+    owned, channels, side = held_ref.shape
     layers = primal_ref.shape[0]
+    copies = [pltpu.make_async_copy(grad_in, grad_ref, sems.at[owned])]
+    copies[0].start()
     for b, block in enumerate(add_pushed(wanted_ref, received_ref, cot_in)):
-        cot_ref[b] = block
+        held_ref[b] = block
+        copy = pltpu.make_async_copy(held_ref.at[b], cot_ref.at[b], sems.at[b])
+        copy.start()
+        copies.append(copy)
     for k in range(layers):
-        terms = sum_terms(received_ref) if k == 0 else terms_refs[k - 1][...]
-        side = terms.shape[1]
-        terms = terms + pltpu.roll(terms, side - channels, 1)
+        terms = sum_terms(received_ref, channels) if k == 0 else terms_refs[k - 1][...]
+        half = terms.shape[0]
         dual = scale_ref[pl.ds(2 * k + 1, 1), :] * row_scale * terms
         primal = scale_ref[pl.ds(2 * k, 1), :] * col_scale * terms
-        dual_ref[k] = dual[:, :channels]
-        primal_ref[k] = pltpu.roll(primal, side - 2 * channels, 1)[:, :channels]
+        dual_ref[k, :half, :] = dual[:, :channels]
+        dual_ref[k, half:, :] = pltpu.roll(dual, side - channels, 1)[:, :channels]
+        primal_ref[k, :half, :] = pltpu.roll(primal, side - 2 * channels, 1)[:, :channels]
+        primal_ref[k, half:, :] = pltpu.roll(primal, side - 3 * channels, 1)[:, :channels]
+    for i, (source, target) in enumerate(((primal_ref, primal_out), (dual_ref, dual_out))):
+        copies.append(pltpu.make_async_copy(source, target, sems.at[owned + 1 + i]))
+        copies[-1].start()
+    for copy in copies:
+        copy.wait()
 
 
 def pull_kernel(tiles_ref, place_ref, received_ref, sum_ref):
@@ -236,9 +275,12 @@
         terms[channels : 2 * channels] + terms[2 * channels :],
     )
     terms = terms + pltpu.roll(terms, side - channels, 1)
-    high = terms.astype(BF16).astype(F32)
-    rest = pltpu.roll(terms - high, channels, 1)
-    packed = jnp.where(lax.rem(lane, 2 * channels) < channels, high, rest).astype(BF16)
+    half = channels // 2
+    packed = jnp.where(
+        lax.rem(lane[:half], 2 * channels) < channels,
+        terms[:half],
+        pltpu.roll(terms[half:], channels, 1),
+    ).astype(BF16)
     copies = channels // place_ref.shape[1]
 
     def one(t):
@@ -281,12 +323,12 @@
     col_scale = 1.0 / math.sqrt(primal_count * row_count * side)
     params = pltpu.CompilerParams(vmem_limit_bytes=16 * 1024 * 1024)
 
-    def call(kernel, outs, *operands, smem=0, **rest):
+    def call(kernel, outs, *operands, ins=None, out_specs=None, **rest):
         return pl.pallas_call(
             kernel,
             out_shape=outs,
-            in_specs=[SMEM] * smem + [VMEM] * (len(operands) - smem),
-            out_specs=jax.tree.map(lambda _: VMEM, outs),
+            in_specs=ins or [VMEM] * len(operands),
+            out_specs=out_specs or jax.tree.map(lambda _: VMEM, outs),
             compiler_params=params,
             **rest,
         )(*operands)
@@ -306,6 +348,8 @@
         jnp.broadcast_to(asked.astype(F32)[:, None, None], (row_count, 8, side))
     )
     message = shape((row_count, 2 * channels, side), BF16)
+    pushed = shape((row_count, channels + channels // 2, side), BF16)
+    terms_shape = shape((channels // 2, side))
     tiles, place, scale, mix, cot, base = call(
         partial(prepare_kernel, owned * col_count, primal_count),
         (
@@ -319,14 +363,19 @@
         tile_rows,
         tile_cols,
         step_fracs,
-        tile_blocks,
-        cot_dual,
-        dual_active,
-        saved_dual,
-        dual_mix,
-        primal_mix,
-        smem=3,
-        scratch_shapes=[pltpu.VMEM((channels, side), F32)],
+        *(
+            pltpu.with_memory_space_constraint(x, pltpu.HBM)
+            for x in (tile_blocks, cot_dual, dual_active, saved_dual, dual_mix, primal_mix)
+        ),
+        ins=[SMEM] * 3 + [HBM] * 6,
+        scratch_shapes=[
+            pltpu.VMEM((2 * layer_count, channels, side), F32),
+            pltpu.VMEM((owned, side), jnp.int32),
+            pltpu.VMEM((owned, channels, side), BF16),
+            pltpu.VMEM((2, layer_count, channels, channels), F32),
+            pltpu.SemaphoreType.DMA((5,)),
+            pltpu.SemaphoreType.DMA((row_count,)),
+        ],
     )
     swap = [(i, col_count - 1 - i) for i in range(col_count)]
     grad_x = cot_primal
@@ -338,7 +387,7 @@
         else:
             cot, send, terms = call(
                 partial(dual_kernel, layer),
-                (shape(cot_dual.shape), message, shape((channels, side))),
+                (shape(cot_dual.shape), message, terms_shape),
                 wanted,
                 received,
                 cot,
@@ -353,7 +402,7 @@
         other = lax.ppermute(mine, "col", swap)
         grad_x, push = call(
             partial(primal_kernel, layer),
-            (shape(cot_primal.shape), message),
+            (shape(cot_primal.shape), pushed),
             tiles,
             place,
             scale,
@@ -365,14 +414,27 @@
             saved_primal,
         )
         received = exchange(push)
-    grad_y, primal_mix_grad, dual_mix_grad = call(
+    grad_x, grad_y, primal_mix_grad, dual_mix_grad = call(
         partial(last_dual_kernel, row_scale, col_scale),
-        (shape(cot_dual.shape), shape(primal_mix.shape), shape(dual_mix.shape)),
+        (
+            shape(cot_primal.shape),
+            shape(cot_dual.shape),
+            shape(primal_mix.shape),
+            shape(dual_mix.shape),
+        ),
         wanted,
         received,
         cot,
         scale,
+        grad_x,
         *all_terms,
+        out_specs=(HBM,) * 4,
+        scratch_shapes=[
+            pltpu.VMEM(cot_dual.shape, F32),
+            pltpu.VMEM(primal_mix.shape, F32),
+            pltpu.VMEM(dual_mix.shape, F32),
+            pltpu.SemaphoreType.DMA((owned + 3,)),
+        ],
     )
     return (grad_x, grad_y, primal_mix_grad, dual_mix_grad)
 

time: 85.5 us -> 82.5 us (0.965)
  local copies, waits for them, and re-layouts: 4.3 us -> 0.73 us
  blocking collectives: 60.5 us -> 57.9 us
  waiting for transfers between devices: 6.33 us -> 8.74 us
  Pallas kernels: 4.64 us -> 5.54 us
    unnamed x26 -> x16, local copies, waits for them, and re-layouts: 3.61 us -> 0.03 us
    all_to_all x6, blocking collectives: 60.5 us -> 57.9 us  [exchange(): return lax.all_to_all(x, 'row', split_axis=0, concat_axis=0, tiled=True)]
    all_to_all x1, waiting for transfers between devices: 2.33 us -> 4.73 us  [exchange(): return lax.all_to_all(x, 'row', split_axis=0, concat_axis=0, tiled=True)]
    pallas_call x11, Pallas kernels: 4.64 us -> 5.54 us  [call(): pl.pallas_call(kernel, out_shape=outs, in_specs=ins or [VMEM] * len(opera...]
  transfers between devices with their start and end apart: 4 -> 4, of which waited for: 4 -> 4; matrix products, arithmetic and copies ran while one was open for 0% -> 0% of each run, Pallas kernels for 1% -> 2%
where the time goes in v3:
time: 82.5 us; the launch traced here: 82.1 us
  blocking collectives  57.9 us (70%)
  waiting for transfers between devices  8.74 us (11%)
  starting transfers between devices  7.6 us (9%)
  Pallas kernels  5.54 us (7%)
    all_to_all x6, blocking collectives, exchange(): return lax.all_to_all(x, 'row', split_axis=0, concat_axis=0, tiled=True)  57.9 us
    all_to_all x1, starting transfers between devices, exchange(): return lax.all_to_all(x, 'row', split_axis=0, concat_axis=0, tiled=True)  7.38 us
    pallas_call x11, Pallas kernels, call(): pl.pallas_call(kernel, out_shape=outs, in_specs=ins or [VMEM] * len(opera...  5.54 us
    all_to_all x1, waiting for transfers between devices, exchange(): return lax.all_to_all(x, 'row', split_axis=0, concat_axis=0, tiled=True)  4.73 us
    ppermute x3, waiting for transfers between devices, per_device(): other = lax.ppermute(mine, 'col', swap)  4 us
  transfers between devices with their start and end apart: 4, of which 4 were waited for; matrix products, arithmetic and copies ran while one was open for 0% of the time, Pallas kernels for 2%

profile of v3, /device:TPU:0, one launch (start us, length us, event | category | flops | bytes accessed | tf_op | source)
XLA Modules:
  0.0 82.1 jit_solution(14410103027258692936)
XLA Ops:
  0.6 0.7 and_select_fusion.1
  1.3 0.1 select_reduce_fusion
  1.4 0.7 broadcast_in_dim.23
  2.1 7.4 %all-to-all-start = ((f32[8,8,128]{2,1,0:T(8,128)}), f32[8,8,128]{2,1,0:T(8,128)S(1)}, u32[]{:S(2)}, u32[]{:S(2)}) async-start(f32[8,8,128]{2,1,0:T(8,128)} %broadcast_in_dim.23), calls=%async_computation | async-start | bytes 65536 | tf_op jit(solution)/shard_map/all_to_all | solution.py:337
  9.5 1.9 %shard_map.147 = (bf16[8,128,128]{2,1,0:T(8,128)(2,1)S(1)}, f32[8,8,128]{2,1,0:T(8,128)S(1)}, f32[6,128]{1,0:T(8,128)S(1)}, bf16[6,32,128]{2,1,0:T(8,128)(2,1)S(...) custom-call(s32[8]{0:T(128)S(1)} %copy-done.6, s32[8]{0:T(128)S(1)} %copy-done.7, s32[3,4]{1,0:T(4,128)S(1)} %copy-done.5, ...), custom_call_target="tpu_custom_call" | custom-call | tf_op jit(solution)/shard_map/pallas_call | solution.py:327
  11.5 4.7 %all-to-all-done.wanted_ref = f32[8,8,128]{2,1,0:T(8,128)S(1)} async-done(((f32[8,8,128]{2,1,0:T(8,128)}), f32[8,8,128]{2,1,0:T(8,128)S(1)}, u32[]{:S(2)}, u32[]{:S(2)}) %all-to-all-start) | async-done | bytes 32800 | tf_op jit(solution)/shard_map/all_to_all | solution.py:337
  16.3 9.7 %all_to_all.35.received_ref = bf16[8,64,128]{2,1,0:T(8,128)(2,1)S(1)} all-to-all(bf16[8,64,128]{2,1,0:T(8,128)(2,1)S(1)} %shard_map.148), channel_id=1, replica_groups=mesh['groups'=2,'row'=8,'col'=2] {'row'}, dimensions={0} | all-to-all | bytes 262144 | tf_op jit(solution)/shard_map/all_to_all | solution.py:337
  26.0 0.2 shard_map.149.mine_ref
  26.3 1.3 %collective-permute-done.other_ref = f32[4,64,128]{2,1,0:T(8,128)S(1)} collective-permute-done((f32[4,64,128]{2,1,0:T(8,128)S(1)}, f32[4,64,128]{2,1,0:T(8,128)S(1)}, u32[]{:S(2)}, u32[]{:S(2)}) %collective-permute-start) | collective-permute-done | bytes 131104 | tf_op jit(solution)/shard_map/ppermute | solution.py:402
  27.7 0.6 shard_map.150
  28.3 9.7 %all_to_all.36.received_ref = bf16[8,48,128]{2,1,0:T(8,128)(2,1)S(1)} all-to-all(bf16[8,48,128]{2,1,0:T(8,128)(2,1)S(1)} %get-tuple-element.27), channel_id=1, replica_groups=mesh['groups'=2,'row'=8,'col'=2] {'row'}, dimensions={0} | all-to-all | bytes 196608 | tf_op jit(solution)/shard_map/all_to_all | solution.py:337
  37.9 0.2 shard_map.151
  38.1 9.7 %all_to_all.37.received_ref = bf16[8,64,128]{2,1,0:T(8,128)(2,1)S(1)} all-to-all(bf16[8,64,128]{2,1,0:T(8,128)(2,1)S(1)} %get-tuple-element.29), channel_id=1, replica_groups=mesh['groups'=2,'row'=8,'col'=2] {'row'}, dimensions={0} | all-to-all | bytes 262144 | tf_op jit(solution)/shard_map/all_to_all | solution.py:337
  47.8 0.2 shard_map.152.mine_ref
  48.1 1.3 %collective-permute-done.1.other_ref = f32[4,64,128]{2,1,0:T(8,128)S(1)} collective-permute-done((f32[4,64,128]{2,1,0:T(8,128)S(1)}, f32[4,64,128]{2,1,0:T(8,128)S(1)}, u32[]{:S(2)}, u32[]{:S(2)}) %collective-permute-start.1) | collective-permute-done | bytes 131104 | tf_op jit(solution)/shard_map/ppermute | solution.py:402
  49.5 0.6 shard_map.153
  50.0 9.5 %all_to_all.38.received_ref = bf16[8,48,128]{2,1,0:T(8,128)(2,1)S(1)} all-to-all(bf16[8,48,128]{2,1,0:T(8,128)(2,1)S(1)} %get-tuple-element.31), channel_id=1, replica_groups=mesh['groups'=2,'row'=8,'col'=2] {'row'}, dimensions={0} | all-to-all | bytes 196608 | tf_op jit(solution)/shard_map/all_to_all | solution.py:337
  59.6 0.2 shard_map.154
  59.7 9.7 %all_to_all.39.received_ref = bf16[8,64,128]{2,1,0:T(8,128)(2,1)S(1)} all-to-all(bf16[8,64,128]{2,1,0:T(8,128)(2,1)S(1)} %get-tuple-element.33), channel_id=1, replica_groups=mesh['groups'=2,'row'=8,'col'=2] {'row'}, dimensions={0} | all-to-all | bytes 262144 | tf_op jit(solution)/shard_map/all_to_all | solution.py:337
  69.5 0.2 shard_map.155.mine_ref
  69.8 1.3 %collective-permute-done.2.other_ref = f32[4,64,128]{2,1,0:T(8,128)S(1)} collective-permute-done((f32[4,64,128]{2,1,0:T(8,128)S(1)}, f32[4,64,128]{2,1,0:T(8,128)S(1)}, u32[]{:S(2)}, u32[]{:S(2)}) %collective-permute-start.2) | collective-permute-done | bytes 131104 | tf_op jit(solution)/shard_map/ppermute | solution.py:402
  71.1 0.6 shard_map.156
  71.7 9.5 %all_to_all.40.received_ref = bf16[8,48,128]{2,1,0:T(8,128)(2,1)S(1)} all-to-all(bf16[8,48,128]{2,1,0:T(8,128)(2,1)S(1)} %get-tuple-element.35), channel_id=1, replica_groups=mesh['groups'=2,'row'=8,'col'=2] {'row'}, dimensions={0} | all-to-all | bytes 196608 | tf_op jit(solution)/shard_map/all_to_all | solution.py:337
  81.2 0.8 %shard_map.157 = (f32[4,32,128]{2,1,0:T(8,128)}, f32[8,32,128]{2,1,0:T(8,128)}, f32[3,32,32]{2,1,0:T(8,128)}, f32[3,32,32]{2,1,0:T(8,128)}) custom-call(f32[8,8,128]{2,1,0:T(8,128)S(1)} %all-to-all-done.wanted_ref, bf16[8,48,128]{2,1,0:T(8,128)(2,1)S(1)} %all_to_all.40.received_ref, f32[8,32,128]{2,1,0:T(8,128)S(1)} %get-tuple-element.36.cot_in, ...), custom_call_target="tpu_custom_call" | custom-call | tf_op jit(solution)/shard_map/pallas_call | solution.py:327
  (21 shorter events, 0.3 us)
Async XLA Ops:
  2.1 7.4 %copy-start.5 = (s32[3,4]{1,0:T(4,128)S(1)}, s32[3,4]{1,0:T(4,128)}, u32[]{:S(2)}) copy-start(s32[3,4]{1,0:T(4,128)} %steps_ref.1) | copy-start | bytes 148
  2.1 7.4 %copy-start.6 = (s32[8]{0:T(128)S(1)}, s32[8]{0:T(128)}, u32[]{:S(2)}) copy-start(s32[8]{0:T(128)} %rows_ref.1) | copy-start | bytes 100
  2.1 7.4 %copy-start.7 = (s32[8]{0:T(128)S(1)}, s32[8]{0:T(128)}, u32[]{:S(2)}) copy-start(s32[8]{0:T(128)} %cols_ref.1) | copy-start | bytes 100
  2.1 14.1 %all-to-all-start = ((f32[8,8,128]{2,1,0:T(8,128)}), f32[8,8,128]{2,1,0:T(8,128)S(1)}, u32[]{:S(2)}, u32[]{:S(2)}) async-start(f32[8,8,128]{2,1,0:T(8,128)} %broadcast_in_dim.23), calls=%async_computation | async-start | bytes 65536 | tf_op jit(solution)/shard_map/all_to_all | solution.py:337
  26.0 1.7 %copy-start.1 = (bf16[4,4,32,128]{3,2,1,0:T(8,128)(2,1)S(1)}, bf16[4,4,32,128]{3,2,1,0:T(8,128)(2,1)}, u32[]{:S(2)}) copy-start(bf16[4,4,32,128]{3,2,1,0:T(8,128)(2,1)} %saved_ref.9) | copy-start | bytes 393220
  26.0 1.7 %copy-start.3 = (f32[4,32,128]{2,1,0:T(8,128)S(1)}, f32[4,32,128]{2,1,0:T(8,128)}, u32[]{:S(2)}) copy-start(f32[4,32,128]{2,1,0:T(8,128)} %grad_in.1) | copy-start | bytes 196612
  26.0 1.7 %copy-start.4 = (s32[3,4,128]{2,1,0:T(4,128)S(1)}, s32[3,4,128]{2,1,0:T(4,128)}, u32[]{:S(2)}) copy-start(s32[3,4,128]{2,1,0:T(4,128)} %mask_ref.9) | copy-start | bytes 18436
  26.3 1.4 %collective-permute-start = (f32[4,64,128]{2,1,0:T(8,128)S(1)}, f32[4,64,128]{2,1,0:T(8,128)S(1)}, u32[]{:S(2)}, u32[]{:S(2)}) collective-permute-start(f32[4,64,128]{2,1,0:T(8,128)S(1)} %shard_map.149.mine_ref), channel_id=1, source_target_pairs={{0,1},{1,0},{2,3},{3,2},{4,5},{5,4},{6,7},{7,6},{8,9},{9,8},{10,11... | collective-permute-start | bytes 393224 | tf_op jit(solution)/shard_map/ppermute | solution.py:402
  27.7 10.2 %copy-start.2 = (s32[3,8,128]{2,1,0:T(8,128)S(1)}, s32[3,8,128]{2,1,0:T(8,128)}, u32[]{:S(2)}) copy-start(s32[3,8,128]{2,1,0:T(8,128)} %mask_ref.8) | copy-start | bytes 36868
  28.3 9.7 %copy-start = (bf16[3,8,32,128]{3,2,1,0:T(8,128)(2,1)S(1)}, bf16[3,8,32,128]{3,2,1,0:T(8,128)(2,1)}, u32[]{:S(2)}) copy-start(bf16[3,8,32,128]{3,2,1,0:T(8,128)(2,1)} %saved_ref.8) | copy-start | bytes 589828
  48.1 1.4 %collective-permute-start.1 = (f32[4,64,128]{2,1,0:T(8,128)S(1)}, f32[4,64,128]{2,1,0:T(8,128)S(1)}, u32[]{:S(2)}, u32[]{:S(2)}) collective-permute-start(f32[4,64,128]{2,1,0:T(8,128)S(1)} %shard_map.152.mine_ref), channel_id=1, source_target_pairs={{0,1},{1,0},{2,3},{3,2},{4,5},{5,4},{6,7},{7,6},{8,9},{9,8},{10,11... | collective-permute-start | bytes 393224 | tf_op jit(solution)/shard_map/ppermute | solution.py:402
  69.7 1.4 %collective-permute-start.2 = (f32[4,64,128]{2,1,0:T(8,128)S(1)}, f32[4,64,128]{2,1,0:T(8,128)S(1)}, u32[]{:S(2)}, u32[]{:S(2)}) collective-permute-start(f32[4,64,128]{2,1,0:T(8,128)S(1)} %shard_map.155.mine_ref), channel_id=1, source_target_pairs={{0,1},{1,0},{2,3},{3,2},{4,5},{5,4},{6,7},{7,6},{8,9},{9,8},{10,11... | collective-permute-start | bytes 393224 | tf_op jit(solution)/shard_map/ppermute | solution.py:402

commit v4 on v3

--- a/solution.py
+++ b/solution.py
@@ -8,7 +8,6 @@
 from jax.experimental.pallas import tpu as pltpu
 from jax.sharding import PartitionSpec as P
 
-SMEM = pl.BlockSpec(memory_space=pltpu.SMEM)
 VMEM = pl.BlockSpec(memory_space=pltpu.VMEM)
 HBM = pl.BlockSpec(memory_space=pltpu.HBM)
 F32 = jnp.float32
@@ -37,12 +36,25 @@
     return high, (x - high.astype(F32)).astype(BF16)
 
 
+def ask_kernel(peer_size, owned, rows_in, asked_ref, rows_ref, sem):
+    fetch = pltpu.make_async_copy(rows_in, rows_ref, sem)
+    fetch.start()
+    fetch.wait()
+
+    def one(t):
+        place = lax.rem(rows_ref[t], owned)
+        filled = jnp.full(asked_ref.shape[1:], place.astype(F32), F32)
+        asked_ref[lax.div(rows_ref[t], peer_size)] = filled
+
+    loop(asked_ref.shape[0], one)
+
+
 def prepare_kernel(
     peer_size,
     primal_count,
-    rows_ref,
-    cols_ref,
-    steps_ref,
+    rows_in,
+    cols_in,
+    steps_in,
     tiles_in,
     cot_in,
     mask_in,
@@ -56,11 +68,14 @@
     cot_ref,
     base_ref,
     pad_ref,
+    rows_ref,
+    cols_ref,
+    steps_ref,
     mask_ref,
     saved_ref,
     mixes_ref,
+    held_ref,
     sems,
-    tile_sems,
 ):
     owned, channels, side = cot_ref.shape
     layers = dual_mix_in.shape[0]
@@ -68,6 +83,10 @@
         pltpu.make_async_copy(source, target, sems.at[i])
         for i, (source, target) in enumerate(
             (
+                (rows_in, rows_ref),
+                (cols_in, cols_ref),
+                (steps_in, steps_ref),
+                (tiles_in, held_ref),
                 (cot_in, cot_ref),
                 (saved_in.at[layers - 1], saved_ref),
                 (mask_in.at[layers - 1], mask_ref),
@@ -78,12 +97,9 @@
     ]
     for fetch in fetches:
         fetch.start()
-
-    def fetch_tile(t):
-        peer = lax.div(rows_ref[t], peer_size)
-        return pltpu.make_async_copy(tiles_in.at[t], tiles_ref.at[peer], tile_sems.at[t])
-
-    loop(tiles_ref.shape[0], lambda t: fetch_tile(t).start())
+    pad_ref[...] = jnp.zeros_like(pad_ref)
+    for fetch in fetches[:3]:
+        fetch.wait()
 
     def one(t):
         p = lax.rem(cols_ref[t], primal_count)
@@ -96,14 +112,8 @@
             upper = jnp.full((1, side), steps_ref[k, 2 * s].astype(F32), F32)
             lower = jnp.full((1, side), steps_ref[k, 2 * s + 1].astype(F32), F32)
             scale_ref[pl.ds(2 * k + s, 1), :] = -(upper / lower)
-    pad_ref[...] = jnp.zeros_like(pad_ref)
-    for fetch in fetches:
+    for fetch in fetches[7:]:
         fetch.wait()
-    for b in range(owned):
-        cot = mask_ref[pl.ds(b, 1), :].astype(F32) * cot_ref[b]
-        cot_ref[b] = cot
-        base_ref[b, :channels, :] = cot.astype(BF16)
-        base_ref[b, channels:, :] = saved_ref[b]
     for k in range(layers):
         for s in range(2):
             pad_ref[2 * k + s, :, :channels] = mixes_ref[s, k]
@@ -116,14 +126,24 @@
                 + pltpu.roll(rest, 2 * channels, 1)
                 + pltpu.roll(rest, 3 * channels, 1)
             ).astype(BF16)
-    loop(tiles_ref.shape[0], lambda t: fetch_tile(t).wait())
+    for fetch in fetches[4:7]:
+        fetch.wait()
+    for b in range(owned):
+        cot = mask_ref[pl.ds(b, 1), :].astype(F32) * cot_ref[b]
+        cot_ref[b] = cot
+        base_ref[b, :channels, :] = cot.astype(BF16)
+        base_ref[b, channels:, :] = saved_ref[b]
+    fetches[3].wait()
+
+    def sort(t):
+        tiles_ref[lax.div(rows_ref[t], peer_size)] = held_ref[t]
+
+    loop(tiles_ref.shape[0], sort)
 
 
 def choose(place_ref, base, send_ref):
-    copies = base[0].shape[0] // place_ref.shape[1]
-
     def one(r):
-        place = jnp.concatenate([place_ref[r]] * copies, 0)
+        place = jnp.broadcast_to(place_ref[r], base[0].shape)
         picked = base[0]
         for b in range(1, len(base)):
             picked = jnp.where(place == b, base[b], picked)
@@ -140,8 +160,7 @@
 def add_pushed(wanted_ref, received_ref, cot_ref):
     owned, channels, side = cot_ref.shape
     rows = received_ref.shape[0]
-    copies = channels // wanted_ref.shape[1]
-    place = lambda r: jnp.concatenate([wanted_ref[r]] * copies, 0)
+    place = lambda r: jnp.broadcast_to(wanted_ref[r], (channels, side))
     if rows <= 16:
         blocks = [cot_ref[b] for b in range(owned)]
         for r in range(rows):
@@ -208,11 +227,10 @@
 def pull_kernel(tiles_ref, place_ref, received_ref, sum_ref):
     count = sum_ref.shape[0]
     rows = tiles_ref.shape[0]
-    copies = received_ref.shape[1] // place_ref.shape[1]
 
     def step(t, sums):
         product = jnp.dot(received_ref[t], tiles_ref[t], preferred_element_type=F32)
-        at = jnp.concatenate([place_ref[t]] * copies, 0)
+        at = jnp.broadcast_to(place_ref[t], product.shape)
         return tuple(s + jnp.where(at == p, product, 0.0) for p, s in enumerate(sums))
 
     sums = tuple(jnp.zeros(sum_ref.shape[1:], F32) for _ in range(count))
@@ -281,10 +299,9 @@
         terms[:half],
         pltpu.roll(terms[half:], channels, 1),
     ).astype(BF16)
-    copies = channels // place_ref.shape[1]
 
     def one(t):
-        at = jnp.concatenate([place_ref[t]] * copies, 0)
+        at = jnp.broadcast_to(place_ref[t], mixed[0].shape)
         picked = mixed[0]
         for p in range(1, blocks):
             picked = jnp.where(at == p, mixed[p], picked)
@@ -339,14 +356,14 @@
     def shape(dims, kind=F32):
         return jax.ShapeDtypeStruct(dims, kind)
 
-    peers = tile_rows // (owned * col_count)
-    peer_ids = jnp.arange(row_count, dtype=jnp.int32)
-    asked = jnp.sum(
-        jnp.where(peers[None, :] == peer_ids[:, None], (tile_rows % owned)[None, :], 0), axis=1
-    )
-    wanted = exchange(
-        jnp.broadcast_to(asked.astype(F32)[:, None, None], (row_count, 8, side))
-    )
+    asked = call(
+        partial(ask_kernel, owned * col_count, owned),
+        shape((row_count, 1, side)),
+        pltpu.with_memory_space_constraint(tile_rows, pltpu.HBM),
+        ins=[HBM],
+        scratch_shapes=[pltpu.SMEM(tile_rows.shape, jnp.int32), pltpu.SemaphoreType.DMA],
+    )
+    wanted = exchange(asked)
     message = shape((row_count, 2 * channels, side), BF16)
     pushed = shape((row_count, channels + channels // 2, side), BF16)
     terms_shape = shape((channels // 2, side))
@@ -354,27 +371,37 @@
         partial(prepare_kernel, owned * col_count, primal_count),
         (
             shape(tile_blocks.shape, BF16),
-            shape((row_count, 8, side)),
+            shape((row_count, 1, side)),
             shape((2 * layer_count, side)),
             shape((2 * layer_count, channels, side), BF16),
             shape(cot_dual.shape),
             shape((owned, 2 * channels, side), BF16),
         ),
-        tile_rows,
-        tile_cols,
-        step_fracs,
         *(
             pltpu.with_memory_space_constraint(x, pltpu.HBM)
-            for x in (tile_blocks, cot_dual, dual_active, saved_dual, dual_mix, primal_mix)
+            for x in (
+                tile_rows,
+                tile_cols,
+                step_fracs,
+                tile_blocks,
+                cot_dual,
+                dual_active,
+                saved_dual,
+                dual_mix,
+                primal_mix,
+            )
         ),
-        ins=[SMEM] * 3 + [HBM] * 6,
+        ins=[HBM] * 9,
         scratch_shapes=[
             pltpu.VMEM((2 * layer_count, channels, side), F32),
+            pltpu.SMEM(tile_rows.shape, jnp.int32),
+            pltpu.SMEM(tile_cols.shape, jnp.int32),
+            pltpu.SMEM(step_fracs.shape, jnp.int32),
             pltpu.VMEM((owned, side), jnp.int32),
             pltpu.VMEM((owned, channels, side), BF16),
             pltpu.VMEM((2, layer_count, channels, channels), F32),
-            pltpu.SemaphoreType.DMA((5,)),
-            pltpu.SemaphoreType.DMA((row_count,)),
+            pltpu.VMEM(tile_blocks.shape, BF16),
+            pltpu.SemaphoreType.DMA((9,)),
         ],
     )
     swap = [(i, col_count - 1 - i) for i in range(col_count)]

time: 82.5 us -> 81.8 us (level)
    pallas_call x11 -> x12, Pallas kernels: 5.54 us -> 6.16 us  [call(): pl.pallas_call(kernel, out_shape=outs, in_specs=ins or [VMEM] * len(opera...]
where the time goes in v4:
time: 81.8 us; the launch traced here: 81.4 us
  blocking collectives  57.9 us (71%)
  waiting for transfers between devices  9.1 us (11%)
  starting transfers between devices  7.48 us (9%)
  Pallas kernels  6.16 us (8%)
    all_to_all x6, blocking collectives, exchange(): return lax.all_to_all(x, 'row', split_axis=0, concat_axis=0, tiled=True)  57.9 us
    all_to_all x1, starting transfers between devices, exchange(): return lax.all_to_all(x, 'row', split_axis=0, concat_axis=0, tiled=True)  7.26 us
    pallas_call x12, Pallas kernels, call(): pl.pallas_call(kernel, out_shape=outs, in_specs=ins or [VMEM] * len(opera...  6.16 us
    all_to_all x1, waiting for transfers between devices, exchange(): return lax.all_to_all(x, 'row', split_axis=0, concat_axis=0, tiled=True)  5.1 us
    ppermute x3, waiting for transfers between devices, per_device(): other = lax.ppermute(mine, 'col', swap)  4 us
  transfers between devices with their start and end apart: 4, of which 4 were waited for; matrix products, arithmetic and copies ran while one was open for 0% of the time, Pallas kernels for 2%

profile of v4, /device:TPU:0, one launch (start us, length us, event | category | flops | bytes accessed | tf_op | source)
XLA Modules:
  0.0 81.4 jit_solution(2986804281075971040)
XLA Ops:
  0.6 1.3 %shard_map.147 = f32[8,1,128]{2,1,0:T(1,128)} custom-call(s32[8]{0:T(128)} %rows_in.3), custom_call_target="tpu_custom_call" | custom-call | tf_op jit(solution)/shard_map/pallas_call | solution.py:344
  1.9 7.3 %all-to-all-start = ((f32[8,1,128]{2,1,0:T(1,128)}), f32[8,1,128]{2,1,0:T(1,128)S(1)}, u32[]{:S(2)}, u32[]{:S(2)}) async-start(f32[8,1,128]{2,1,0:T(1,128)} %shard_map.147), calls=%async_computation | async-start | bytes 8192 | tf_op jit(solution)/shard_map/all_to_all | solution.py:354
  9.2 1.3 %shard_map.148 = (bf16[8,128,128]{2,1,0:T(8,128)(2,1)S(1)}, f32[8,1,128]{2,1,0:T(1,128)S(1)}, f32[6,128]{1,0:T(8,128)S(1)}, bf16[6,32,128]{2,1,0:T(8,128)(2,1)S(...) custom-call(s32[8]{0:T(128)} %rows_in.3, s32[8]{0:T(128)} %cols_in.1, s32[3,4]{1,0:T(4,128)} %steps_in.1, ...), custom_call_target="tpu_custom_call" | custom-call | tf_op jit(solution)/shard_map/pallas_call | solution.py:344
  10.5 5.1 %all-to-all-done.wanted_ref = f32[8,1,128]{2,1,0:T(1,128)S(1)} async-done(((f32[8,1,128]{2,1,0:T(1,128)}), f32[8,1,128]{2,1,0:T(1,128)S(1)}, u32[]{:S(2)}, u32[]{:S(2)}) %all-to-all-start) | async-done | bytes 4128 | tf_op jit(solution)/shard_map/all_to_all | solution.py:354
  15.6 0.1 shard_map.149
  15.7 9.7 %all_to_all.35.received_ref = bf16[8,64,128]{2,1,0:T(8,128)(2,1)S(1)} all-to-all(bf16[8,64,128]{2,1,0:T(8,128)(2,1)S(1)} %shard_map.149), channel_id=1, replica_groups=mesh['groups'=2,'row'=8,'col'=2] {'row'}, dimensions={0} | all-to-all | bytes 262144 | tf_op jit(solution)/shard_map/all_to_all | solution.py:354
  25.4 0.2 shard_map.150.mine_ref
  25.7 1.3 %collective-permute-done.other_ref = f32[4,64,128]{2,1,0:T(8,128)S(1)} collective-permute-done((f32[4,64,128]{2,1,0:T(8,128)S(1)}, f32[4,64,128]{2,1,0:T(8,128)S(1)}, u32[]{:S(2)}, u32[]{:S(2)}) %collective-permute-start) | collective-permute-done | bytes 131104 | tf_op jit(solution)/shard_map/ppermute | solution.py:429
  27.1 0.6 shard_map.151
  27.6 9.7 %all_to_all.36.received_ref = bf16[8,48,128]{2,1,0:T(8,128)(2,1)S(1)} all-to-all(bf16[8,48,128]{2,1,0:T(8,128)(2,1)S(1)} %get-tuple-element.27), channel_id=1, replica_groups=mesh['groups'=2,'row'=8,'col'=2] {'row'}, dimensions={0} | all-to-all | bytes 196608 | tf_op jit(solution)/shard_map/all_to_all | solution.py:354
  37.3 0.2 shard_map.152
  37.5 9.7 %all_to_all.37.received_ref = bf16[8,64,128]{2,1,0:T(8,128)(2,1)S(1)} all-to-all(bf16[8,64,128]{2,1,0:T(8,128)(2,1)S(1)} %get-tuple-element.29), channel_id=1, replica_groups=mesh['groups'=2,'row'=8,'col'=2] {'row'}, dimensions={0} | all-to-all | bytes 262144 | tf_op jit(solution)/shard_map/all_to_all | solution.py:354
  47.2 0.2 shard_map.153.mine_ref
  47.5 1.3 %collective-permute-done.1.other_ref = f32[4,64,128]{2,1,0:T(8,128)S(1)} collective-permute-done((f32[4,64,128]{2,1,0:T(8,128)S(1)}, f32[4,64,128]{2,1,0:T(8,128)S(1)}, u32[]{:S(2)}, u32[]{:S(2)}) %collective-permute-start.1) | collective-permute-done | bytes 131104 | tf_op jit(solution)/shard_map/ppermute | solution.py:429
  48.9 0.6 shard_map.154
  49.4 9.5 %all_to_all.38.received_ref = bf16[8,48,128]{2,1,0:T(8,128)(2,1)S(1)} all-to-all(bf16[8,48,128]{2,1,0:T(8,128)(2,1)S(1)} %get-tuple-element.31), channel_id=1, replica_groups=mesh['groups'=2,'row'=8,'col'=2] {'row'}, dimensions={0} | all-to-all | bytes 196608 | tf_op jit(solution)/shard_map/all_to_all | solution.py:354
  58.9 0.2 shard_map.155
  59.1 9.7 %all_to_all.39.received_ref = bf16[8,64,128]{2,1,0:T(8,128)(2,1)S(1)} all-to-all(bf16[8,64,128]{2,1,0:T(8,128)(2,1)S(1)} %get-tuple-element.33), channel_id=1, replica_groups=mesh['groups'=2,'row'=8,'col'=2] {'row'}, dimensions={0} | all-to-all | bytes 262144 | tf_op jit(solution)/shard_map/all_to_all | solution.py:354
  68.9 0.2 shard_map.156.mine_ref
  69.1 0.1 collective-permute-start.2
  69.2 1.3 %collective-permute-done.2.other_ref = f32[4,64,128]{2,1,0:T(8,128)S(1)} collective-permute-done((f32[4,64,128]{2,1,0:T(8,128)S(1)}, f32[4,64,128]{2,1,0:T(8,128)S(1)}, u32[]{:S(2)}, u32[]{:S(2)}) %collective-permute-start.2) | collective-permute-done | bytes 131104 | tf_op jit(solution)/shard_map/ppermute | solution.py:429
  70.5 0.6 shard_map.157
  71.0 9.5 %all_to_all.40.received_ref = bf16[8,48,128]{2,1,0:T(8,128)(2,1)S(1)} all-to-all(bf16[8,48,128]{2,1,0:T(8,128)(2,1)S(1)} %get-tuple-element.35), channel_id=1, replica_groups=mesh['groups'=2,'row'=8,'col'=2] {'row'}, dimensions={0} | all-to-all | bytes 196608 | tf_op jit(solution)/shard_map/all_to_all | solution.py:354
  80.6 0.8 %shard_map.158 = (f32[4,32,128]{2,1,0:T(8,128)}, f32[8,32,128]{2,1,0:T(8,128)}, f32[3,32,32]{2,1,0:T(8,128)}, f32[3,32,32]{2,1,0:T(8,128)}) custom-call(f32[8,1,128]{2,1,0:T(1,128)S(1)} %all-to-all-done.wanted_ref, bf16[8,48,128]{2,1,0:T(8,128)(2,1)S(1)} %all_to_all.40.received_ref, f32[8,32,128]{2,1,0:T(8,128)S(1)} %get-tuple-element.36.cot_in, ...), custom_call_target="tpu_custom_call" | custom-call | tf_op jit(solution)/shard_map/pallas_call | solution.py:344
  (12 shorter events, 0.2 us)
Async XLA Ops:
  1.9 13.7 %all-to-all-start = ((f32[8,1,128]{2,1,0:T(1,128)}), f32[8,1,128]{2,1,0:T(1,128)S(1)}, u32[]{:S(2)}, u32[]{:S(2)}) async-start(f32[8,1,128]{2,1,0:T(1,128)} %shard_map.147), calls=%async_computation | async-start | bytes 8192 | tf_op jit(solution)/shard_map/all_to_all | solution.py:354
  25.4 1.6 %copy-start.1 = (bf16[4,4,32,128]{3,2,1,0:T(8,128)(2,1)S(1)}, bf16[4,4,32,128]{3,2,1,0:T(8,128)(2,1)}, u32[]{:S(2)}) copy-start(bf16[4,4,32,128]{3,2,1,0:T(8,128)(2,1)} %saved_ref.9) | copy-start | bytes 393220
  25.4 1.6 %copy-start.3 = (f32[4,32,128]{2,1,0:T(8,128)S(1)}, f32[4,32,128]{2,1,0:T(8,128)}, u32[]{:S(2)}) copy-start(f32[4,32,128]{2,1,0:T(8,128)} %grad_in.1) | copy-start | bytes 196612
  25.4 1.6 %copy-start.4 = (s32[3,4,128]{2,1,0:T(4,128)S(1)}, s32[3,4,128]{2,1,0:T(4,128)}, u32[]{:S(2)}) copy-start(s32[3,4,128]{2,1,0:T(4,128)} %mask_ref.9) | copy-start | bytes 18436
  25.6 1.4 %collective-permute-start = (f32[4,64,128]{2,1,0:T(8,128)S(1)}, f32[4,64,128]{2,1,0:T(8,128)S(1)}, u32[]{:S(2)}, u32[]{:S(2)}) collective-permute-start(f32[4,64,128]{2,1,0:T(8,128)S(1)} %shard_map.150.mine_ref), channel_id=1, source_target_pairs={{0,1},{1,0},{2,3},{3,2},{4,5},{5,4},{6,7},{7,6},{8,9},{9,8},{10,11... | collective-permute-start | bytes 393224 | tf_op jit(solution)/shard_map/ppermute | solution.py:429
  27.1 10.2 %copy-start.2 = (s32[3,8,128]{2,1,0:T(8,128)S(1)}, s32[3,8,128]{2,1,0:T(8,128)}, u32[]{:S(2)}) copy-start(s32[3,8,128]{2,1,0:T(8,128)} %mask_ref.8) | copy-start | bytes 36868
  27.6 9.7 %copy-start = (bf16[3,8,32,128]{3,2,1,0:T(8,128)(2,1)S(1)}, bf16[3,8,32,128]{3,2,1,0:T(8,128)(2,1)}, u32[]{:S(2)}) copy-start(bf16[3,8,32,128]{3,2,1,0:T(8,128)(2,1)} %saved_ref.8) | copy-start | bytes 589828
  47.4 1.4 %collective-permute-start.1 = (f32[4,64,128]{2,1,0:T(8,128)S(1)}, f32[4,64,128]{2,1,0:T(8,128)S(1)}, u32[]{:S(2)}, u32[]{:S(2)}) collective-permute-start(f32[4,64,128]{2,1,0:T(8,128)S(1)} %shard_map.153.mine_ref), channel_id=1, source_target_pairs={{0,1},{1,0},{2,3},{3,2},{4,5},{5,4},{6,7},{7,6},{8,9},{9,8},{10,11... | collective-permute-start | bytes 393224 | tf_op jit(solution)/shard_map/ppermute | solution.py:429
  69.1 1.4 %collective-permute-start.2 = (f32[4,64,128]{2,1,0:T(8,128)S(1)}, f32[4,64,128]{2,1,0:T(8,128)S(1)}, u32[]{:S(2)}, u32[]{:S(2)}) collective-permute-start(f32[4,64,128]{2,1,0:T(8,128)S(1)} %shard_map.156.mine_ref), channel_id=1, source_target_pairs={{0,1},{1,0},{2,3},{3,2},{4,5},{5,4},{6,7},{7,6},{8,9},{9,8},{10,11... | collective-permute-start | bytes 393224 | tf_op jit(solution)/shard_map/ppermute | solution.py:429

commit v5 on v4

--- a/solution.py
+++ b/solution.py
@@ -36,7 +36,11 @@
     return high, (x - high.astype(F32)).astype(BF16)
 
 
-def ask_kernel(peer_size, owned, rows_in, asked_ref, rows_ref, sem):
+def slot_of(row, peer_size, shift, row_count):
+    return lax.rem(lax.div(row, peer_size) + shift, row_count)
+
+
+def ask_kernel(slot, owned, rows_in, asked_ref, rows_ref, sem):
     fetch = pltpu.make_async_copy(rows_in, rows_ref, sem)
     fetch.start()
     fetch.wait()
@@ -44,13 +48,13 @@
     def one(t):
         place = lax.rem(rows_ref[t], owned)
         filled = jnp.full(asked_ref.shape[1:], place.astype(F32), F32)
-        asked_ref[lax.div(rows_ref[t], peer_size)] = filled
+        asked_ref[slot(rows_ref[t])] = filled
 
     loop(asked_ref.shape[0], one)
 
 
 def prepare_kernel(
-    peer_size,
+    slot,
     primal_count,
     rows_in,
     cols_in,
@@ -104,7 +108,7 @@
     def one(t):
         p = lax.rem(cols_ref[t], primal_count)
         filled = jnp.full(place_ref.shape[1:], p.astype(F32), F32)
-        place_ref[lax.div(rows_ref[t], peer_size)] = filled
+        place_ref[slot(rows_ref[t])] = filled
 
     loop(tiles_ref.shape[0], one)
     for k in range(layers):
@@ -136,7 +140,7 @@
     fetches[3].wait()
 
     def sort(t):
-        tiles_ref[lax.div(rows_ref[t], peer_size)] = held_ref[t]
+        tiles_ref[slot(rows_ref[t])] = held_ref[t]
 
     loop(tiles_ref.shape[0], sort)
 
@@ -350,14 +354,20 @@
             **rest,
         )(*operands)
 
+    shift = row_count - row_count // 2
+    order = [(slot + row_count - shift) % row_count for slot in range(row_count)]
+
     def exchange(x):
-        return lax.all_to_all(x, "row", split_axis=0, concat_axis=0, tiled=True)
+        return lax.all_to_all(
+            x, "row", split_axis=0, concat_axis=0, axis_index_groups=[order], tiled=True
+        )
 
     def shape(dims, kind=F32):
         return jax.ShapeDtypeStruct(dims, kind)
 
+    slot = partial(slot_of, peer_size=owned * col_count, shift=shift, row_count=row_count)
     asked = call(
-        partial(ask_kernel, owned * col_count, owned),
+        partial(ask_kernel, slot, owned),
         shape((row_count, 1, side)),
         pltpu.with_memory_space_constraint(tile_rows, pltpu.HBM),
         ins=[HBM],
@@ -368,7 +378,7 @@
     pushed = shape((row_count, channels + channels // 2, side), BF16)
     terms_shape = shape((channels // 2, side))
     tiles, place, scale, mix, cot, base = call(
-        partial(prepare_kernel, owned * col_count, primal_count),
+        partial(prepare_kernel, slot, primal_count),
         (
             shape(tile_blocks.shape, BF16),
             shape((row_count, 1, side)),

time: 81.8 us -> 75.5 us (0.923)
  blocking collectives: 57.9 us -> 53.4 us
  waiting for transfers between devices: 9.1 us -> 6.73 us
    all_to_all x6, blocking collectives: 57.9 us -> 53.4 us  [exchange(): lax.all_to_all(x, 'row', split_axis=0, concat_axis=0, axis_index_groups=[...]
    all_to_all x1, waiting for transfers between devices: 5.1 us -> 2.72 us  [exchange(): lax.all_to_all(x, 'row', split_axis=0, concat_axis=0, axis_index_groups=[...]
where the time goes in v5:
time: 75.5 us; the launch traced here: 75.1 us
  blocking collectives  53.4 us (71%)
  starting transfers between devices  8.04 us (11%)
  waiting for transfers between devices  6.73 us (9%)
  Pallas kernels  6.19 us (8%)
    all_to_all x6, blocking collectives, exchange(): lax.all_to_all(x, 'row', split_axis=0, concat_axis=0, axis_index_groups=[...  53.4 us
    all_to_all x1, starting transfers between devices, exchange(): lax.all_to_all(x, 'row', split_axis=0, concat_axis=0, axis_index_groups=[...  7.83 us
    pallas_call x12, Pallas kernels, call(): pl.pallas_call(kernel, out_shape=outs, in_specs=ins or [VMEM] * len(opera...  6.19 us
    ppermute x3, waiting for transfers between devices, per_device(): other = lax.ppermute(mine, 'col', swap)  4 us
    all_to_all x1, waiting for transfers between devices, exchange(): lax.all_to_all(x, 'row', split_axis=0, concat_axis=0, axis_index_groups=[...  2.72 us
  transfers between devices with their start and end apart: 4, of which 4 were waited for; matrix products, arithmetic and copies ran while one was open for 0% of the time, Pallas kernels for 2%

profile of v5, /device:TPU:0, one launch (start us, length us, event | category | flops | bytes accessed | tf_op | source)
XLA Modules:
  0.0 75.1 jit_solution(1962046061372388711)
XLA Ops:
  0.6 1.3 %shard_map.147 = f32[8,1,128]{2,1,0:T(1,128)} custom-call(s32[8]{0:T(128)} %rows_in.3), custom_call_target="tpu_custom_call" | custom-call | tf_op jit(solution)/shard_map/pallas_call | solution.py:348
  1.9 7.8 %all-to-all-start = ((f32[8,1,128]{2,1,0:T(1,128)}), f32[8,1,128]{2,1,0:T(1,128)S(1)}, u32[]{:S(2)}, u32[]{:S(2)}) async-start(f32[8,1,128]{2,1,0:T(1,128)} %shard_map.147), calls=%async_computation | async-start | bytes 8192 | tf_op jit(solution)/shard_map/all_to_all | solution.py:361
  9.8 1.3 %shard_map.148 = (bf16[8,128,128]{2,1,0:T(8,128)(2,1)S(1)}, f32[8,1,128]{2,1,0:T(1,128)S(1)}, f32[6,128]{1,0:T(8,128)S(1)}, bf16[6,32,128]{2,1,0:T(8,128)(2,1)S(...) custom-call(s32[8]{0:T(128)} %rows_in.3, s32[8]{0:T(128)} %cols_in.1, s32[3,4]{1,0:T(4,128)} %steps_in.1, ...), custom_call_target="tpu_custom_call" | custom-call | tf_op jit(solution)/shard_map/pallas_call | solution.py:348
  11.1 2.7 %all-to-all-done.wanted_ref = f32[8,1,128]{2,1,0:T(1,128)S(1)} async-done(((f32[8,1,128]{2,1,0:T(1,128)}), f32[8,1,128]{2,1,0:T(1,128)S(1)}, u32[]{:S(2)}, u32[]{:S(2)}) %all-to-all-start) | async-done | bytes 4128 | tf_op jit(solution)/shard_map/all_to_all | solution.py:361
  13.8 0.1 shard_map.149
  13.9 9.0 %all_to_all.35.received_ref = bf16[8,64,128]{2,1,0:T(8,128)(2,1)S(1)} all-to-all(bf16[8,64,128]{2,1,0:T(8,128)(2,1)S(1)} %shard_map.149), channel_id=1, replica_groups={{8,10,12,14,0,2,4,6},{9,11,13,15,1,3,5,7},{24,26,28,30,16,18,20,22},{25..., dimensions={0} | all-to-all | bytes 262144 | tf_op jit(solution)/shard_map/all_to_all | solution.py:361
  22.9 0.2 shard_map.150.mine_ref
  23.1 0.1 collective-permute-start
  23.2 1.3 %collective-permute-done.other_ref = f32[4,64,128]{2,1,0:T(8,128)S(1)} collective-permute-done((f32[4,64,128]{2,1,0:T(8,128)S(1)}, f32[4,64,128]{2,1,0:T(8,128)S(1)}, u32[]{:S(2)}, u32[]{:S(2)}) %collective-permute-start) | collective-permute-done | bytes 131104 | tf_op jit(solution)/shard_map/ppermute | solution.py:439
  24.5 0.6 shard_map.151
  25.1 8.9 %all_to_all.36.received_ref = bf16[8,48,128]{2,1,0:T(8,128)(2,1)S(1)} all-to-all(bf16[8,48,128]{2,1,0:T(8,128)(2,1)S(1)} %get-tuple-element.27), channel_id=1, replica_groups={{8,10,12,14,0,2,4,6},{9,11,13,15,1,3,5,7},{24,26,28,30,16,18,20,22},{25..., dimensions={0} | all-to-all | bytes 196608 | tf_op jit(solution)/shard_map/all_to_all | solution.py:361
  34.0 0.2 shard_map.152
  34.2 9.0 %all_to_all.37.received_ref = bf16[8,64,128]{2,1,0:T(8,128)(2,1)S(1)} all-to-all(bf16[8,64,128]{2,1,0:T(8,128)(2,1)S(1)} %get-tuple-element.29), channel_id=1, replica_groups={{8,10,12,14,0,2,4,6},{9,11,13,15,1,3,5,7},{24,26,28,30,16,18,20,22},{25..., dimensions={0} | all-to-all | bytes 262144 | tf_op jit(solution)/shard_map/all_to_all | solution.py:361
  43.2 0.2 shard_map.153.mine_ref
  43.5 1.3 %collective-permute-done.1.other_ref = f32[4,64,128]{2,1,0:T(8,128)S(1)} collective-permute-done((f32[4,64,128]{2,1,0:T(8,128)S(1)}, f32[4,64,128]{2,1,0:T(8,128)S(1)}, u32[]{:S(2)}, u32[]{:S(2)}) %collective-permute-start.1) | collective-permute-done | bytes 131104 | tf_op jit(solution)/shard_map/ppermute | solution.py:439
  44.8 0.6 shard_map.154
  45.4 8.8 %all_to_all.38.received_ref = bf16[8,48,128]{2,1,0:T(8,128)(2,1)S(1)} all-to-all(bf16[8,48,128]{2,1,0:T(8,128)(2,1)S(1)} %get-tuple-element.31), channel_id=1, replica_groups={{8,10,12,14,0,2,4,6},{9,11,13,15,1,3,5,7},{24,26,28,30,16,18,20,22},{25..., dimensions={0} | all-to-all | bytes 196608 | tf_op jit(solution)/shard_map/all_to_all | solution.py:361
  54.1 0.2 shard_map.155
  54.3 9.0 %all_to_all.39.received_ref = bf16[8,64,128]{2,1,0:T(8,128)(2,1)S(1)} all-to-all(bf16[8,64,128]{2,1,0:T(8,128)(2,1)S(1)} %get-tuple-element.33), channel_id=1, replica_groups={{8,10,12,14,0,2,4,6},{9,11,13,15,1,3,5,7},{24,26,28,30,16,18,20,22},{25..., dimensions={0} | all-to-all | bytes 262144 | tf_op jit(solution)/shard_map/all_to_all | solution.py:361
  63.3 0.2 shard_map.156.mine_ref
  63.6 1.3 %collective-permute-done.2.other_ref = f32[4,64,128]{2,1,0:T(8,128)S(1)} collective-permute-done((f32[4,64,128]{2,1,0:T(8,128)S(1)}, f32[4,64,128]{2,1,0:T(8,128)S(1)}, u32[]{:S(2)}, u32[]{:S(2)}) %collective-permute-start.2) | collective-permute-done | bytes 131104 | tf_op jit(solution)/shard_map/ppermute | solution.py:439
  64.9 0.6 shard_map.157
  65.5 8.8 %all_to_all.40.received_ref = bf16[8,48,128]{2,1,0:T(8,128)(2,1)S(1)} all-to-all(bf16[8,48,128]{2,1,0:T(8,128)(2,1)S(1)} %get-tuple-element.35), channel_id=1, replica_groups={{8,10,12,14,0,2,4,6},{9,11,13,15,1,3,5,7},{24,26,28,30,16,18,20,22},{25..., dimensions={0} | all-to-all | bytes 196608 | tf_op jit(solution)/shard_map/all_to_all | solution.py:361
  74.3 0.8 %shard_map.158 = (f32[4,32,128]{2,1,0:T(8,128)}, f32[8,32,128]{2,1,0:T(8,128)}, f32[3,32,32]{2,1,0:T(8,128)}, f32[3,32,32]{2,1,0:T(8,128)}) custom-call(f32[8,1,128]{2,1,0:T(1,128)S(1)} %all-to-all-done.wanted_ref, bf16[8,48,128]{2,1,0:T(8,128)(2,1)S(1)} %all_to_all.40.received_ref, f32[8,32,128]{2,1,0:T(8,128)S(1)} %get-tuple-element.36.cot_in, ...), custom_call_target="tpu_custom_call" | custom-call | tf_op jit(solution)/shard_map/pallas_call | solution.py:348
  (12 shorter events, 0.2 us)
Async XLA Ops:
  1.9 11.9 %all-to-all-start = ((f32[8,1,128]{2,1,0:T(1,128)}), f32[8,1,128]{2,1,0:T(1,128)S(1)}, u32[]{:S(2)}, u32[]{:S(2)}) async-start(f32[8,1,128]{2,1,0:T(1,128)} %shard_map.147), calls=%async_computation | async-start | bytes 8192 | tf_op jit(solution)/shard_map/all_to_all | solution.py:361
  22.9 1.6 %copy-start.1 = (bf16[4,4,32,128]{3,2,1,0:T(8,128)(2,1)S(1)}, bf16[4,4,32,128]{3,2,1,0:T(8,128)(2,1)}, u32[]{:S(2)}) copy-start(bf16[4,4,32,128]{3,2,1,0:T(8,128)(2,1)} %saved_ref.9) | copy-start | bytes 393220
  22.9 1.6 %copy-start.3 = (f32[4,32,128]{2,1,0:T(8,128)S(1)}, f32[4,32,128]{2,1,0:T(8,128)}, u32[]{:S(2)}) copy-start(f32[4,32,128]{2,1,0:T(8,128)} %grad_in.1) | copy-start | bytes 196612
  22.9 1.6 %copy-start.4 = (s32[3,4,128]{2,1,0:T(4,128)S(1)}, s32[3,4,128]{2,1,0:T(4,128)}, u32[]{:S(2)}) copy-start(s32[3,4,128]{2,1,0:T(4,128)} %mask_ref.9) | copy-start | bytes 18436
  23.1 1.4 %collective-permute-start = (f32[4,64,128]{2,1,0:T(8,128)S(1)}, f32[4,64,128]{2,1,0:T(8,128)S(1)}, u32[]{:S(2)}, u32[]{:S(2)}) collective-permute-start(f32[4,64,128]{2,1,0:T(8,128)S(1)} %shard_map.150.mine_ref), channel_id=1, source_target_pairs={{0,1},{1,0},{2,3},{3,2},{4,5},{5,4},{6,7},{7,6},{8,9},{9,8},{10,11... | collective-permute-start | bytes 393224 | tf_op jit(solution)/shard_map/ppermute | solution.py:439
  24.5 9.5 %copy-start.2 = (s32[3,8,128]{2,1,0:T(8,128)S(1)}, s32[3,8,128]{2,1,0:T(8,128)}, u32[]{:S(2)}) copy-start(s32[3,8,128]{2,1,0:T(8,128)} %mask_ref.8) | copy-start | bytes 36868
  25.1 8.9 %copy-start = (bf16[3,8,32,128]{3,2,1,0:T(8,128)(2,1)S(1)}, bf16[3,8,32,128]{3,2,1,0:T(8,128)(2,1)}, u32[]{:S(2)}) copy-start(bf16[3,8,32,128]{3,2,1,0:T(8,128)(2,1)} %saved_ref.8) | copy-start | bytes 589828
  43.4 1.4 %collective-permute-start.1 = (f32[4,64,128]{2,1,0:T(8,128)S(1)}, f32[4,64,128]{2,1,0:T(8,128)S(1)}, u32[]{:S(2)}, u32[]{:S(2)}) collective-permute-start(f32[4,64,128]{2,1,0:T(8,128)S(1)} %shard_map.153.mine_ref), channel_id=1, source_target_pairs={{0,1},{1,0},{2,3},{3,2},{4,5},{5,4},{6,7},{7,6},{8,9},{9,8},{10,11... | collective-permute-start | bytes 393224 | tf_op jit(solution)/shard_map/ppermute | solution.py:439
  63.5 1.4 %collective-permute-start.2 = (f32[4,64,128]{2,1,0:T(8,128)S(1)}, f32[4,64,128]{2,1,0:T(8,128)S(1)}, u32[]{:S(2)}, u32[]{:S(2)}) collective-permute-start(f32[4,64,128]{2,1,0:T(8,128)S(1)} %shard_map.156.mine_ref), channel_id=1, source_target_pairs={{0,1},{1,0},{2,3},{3,2},{4,5},{5,4},{6,7},{7,6},{8,9},{9,8},{10,11... | collective-permute-start | bytes 393224 | tf_op jit(solution)/shard_map/ppermute | solution.py:439

commit v6 on v5

v6 whole, which is shorter than its diff:
```python
from functools import partial
import math

import jax
import jax.numpy as jnp
from jax import lax
from jax.experimental import pallas as pl
from jax.experimental.pallas import tpu as pltpu
from jax.sharding import PartitionSpec as P

VMEM = pl.BlockSpec(memory_space=pltpu.VMEM)
HBM = pl.BlockSpec(memory_space=pltpu.HBM)
F32 = jnp.float32
BF16 = jnp.bfloat16


def loop(count, body):
    if count <= 16:
        for i in range(count):
            body(i)
    else:
        lax.fori_loop(0, count, lambda i, _: (body(i), 0)[1], 0)


def total_of(count, term, shape):
    if count <= 16:
        total = term(0)
        for i in range(1, count):
            total = total + term(i)
        return total
    return lax.fori_loop(0, count, lambda i, t: t + term(i), jnp.zeros(shape, F32))


def halves(x):
    high = x.astype(BF16)
    return high, (x - high.astype(F32)).astype(BF16)


def slot_of(row, peer_size, shift, row_count):
    return lax.rem(lax.div(row, peer_size) + shift, row_count)


def ask_kernel(slot, owned, rows_in, asked_ref, rows_ref, sem):
    fetch = pltpu.make_async_copy(rows_in, rows_ref, sem)
    fetch.start()
    fetch.wait()

    def one(t):
        place = lax.rem(rows_ref[t], owned)
        filled = jnp.full(asked_ref.shape[1:], place.astype(F32), F32)
        asked_ref[slot(rows_ref[t])] = filled

    loop(asked_ref.shape[0], one)


def prepare_kernel(
    slot,
    primal_count,
    rows_in,
    cols_in,
    steps_in,
    tiles_in,
    cot_in,
    mask_in,
    dual_mix_in,
    primal_mix_in,
    tiles_ref,
    scale_ref,
    mix_ref,
    cot_ref,
    pad_ref,
    rows_ref,
    cols_ref,
    steps_ref,
    mask_ref,
    mixes_ref,
    held_ref,
    sems,
):
    owned, channels, side = cot_ref.shape
    layers = dual_mix_in.shape[0]
    fetches = [
        pltpu.make_async_copy(source, target, sems.at[i])
        for i, (source, target) in enumerate(
            (
                (rows_in, rows_ref),
                (cols_in, cols_ref),
                (steps_in, steps_ref),
                (tiles_in, held_ref),
                (cot_in, cot_ref),
                (mask_in.at[layers - 1], mask_ref),
                (primal_mix_in, mixes_ref.at[0]),
                (dual_mix_in, mixes_ref.at[1]),
            )
        )
    ]
    for fetch in fetches:
        fetch.start()
    pad_ref[...] = jnp.zeros_like(pad_ref)
    for fetch in fetches[:3]:
        fetch.wait()
    for k in range(layers):
        for s in range(2):
            upper = jnp.full((1, side), steps_ref[k, 2 * s].astype(F32), F32)
            lower = jnp.full((1, side), steps_ref[k, 2 * s + 1].astype(F32), F32)
            scale_ref[pl.ds(2 * k + s, 1), :] = -(upper / lower)
    for fetch in fetches[6:]:
        fetch.wait()
    for k in range(layers):
        for s in range(2):
            pad_ref[2 * k + s, :, :channels] = mixes_ref[s, k]
            weights = pad_ref[2 * k + s]
            high = weights.astype(BF16).astype(F32)
            rest = weights - high
            mix_ref[2 * k + s] = (
                high
                + pltpu.roll(high, channels, 1)
                + pltpu.roll(rest, 2 * channels, 1)
                + pltpu.roll(rest, 3 * channels, 1)
            ).astype(BF16)
    for fetch in fetches[4:6]:
        fetch.wait()
    for b in range(owned):
        cot_ref[b] = mask_ref[pl.ds(b, 1), :].astype(F32) * cot_ref[b]
    fetches[3].wait()
    below = tiles_ref.shape[1] - held_ref.shape[1]

    def sort(t):
        to = slot(rows_ref[t])
        tiles_ref[to, : held_ref.shape[1], :] = held_ref[t]
        p = lax.rem(cols_ref[t], primal_count)
        filled = jnp.full((below, side), p.astype(F32), F32)
        tiles_ref[to, held_ref.shape[1] :, :] = filled.astype(BF16)

    loop(tiles_ref.shape[0], sort)


def chosen(wanted_ref, r, base):
    place = jnp.broadcast_to(wanted_ref[r], base[0].shape)
    picked = base[0]
    for b in range(1, len(base)):
        picked = jnp.where(place == b, base[b], picked)
    return picked.astype(BF16)


def choose_for_all(wanted_ref, base, send_ref):
    cols = send_ref.shape[0] // wanted_ref.shape[0]

    def one(r):
        picked = chosen(wanted_ref, r, base)
        for c in range(cols):
            send_ref[r * cols + c] = picked

    loop(wanted_ref.shape[0], one)


def first_dual_kernel(wanted_ref, cot_ref, send_ref):
    choose_for_all(wanted_ref, [cot_ref[b] for b in range(cot_ref.shape[0])], send_ref)


def sum_pushed(wanted_ref, received_ref, start):
    channels, side = start[0].shape
    rows = received_ref.shape[0]

    def step(r, blocks):
        at = jnp.broadcast_to(wanted_ref[r], (channels, side))
        pushed = received_ref[r, :channels, :].astype(F32)
        return tuple(block + jnp.where(at == b, pushed, 0.0) for b, block in enumerate(blocks))

    blocks = tuple(start)
    if rows <= 16:
        for r in range(rows):
            blocks = step(r, blocks)
        return blocks
    return lax.fori_loop(0, rows, step, blocks)


def place_of(tiles_ref, t, shape):
    side = tiles_ref.shape[2]
    return jnp.broadcast_to(tiles_ref[t, side:, :].astype(F32)[:1], shape)


def mixed_by(weights, blocks):
    side = blocks[0].shape[1]
    high, rest = halves(jnp.concatenate(blocks, 1))
    mixed = jnp.dot(
        weights, jnp.concatenate([high, rest, high, rest], 0), preferred_element_type=F32
    )
    return [mixed[:, b * side : (b + 1) * side] for b in range(len(blocks))]


def folded(terms, channels):
    return terms + pltpu.roll(terms, terms.shape[1] - channels, 1)


def contract(left, right):
    return lax.dot_general(
        jnp.concatenate(left, 1),
        jnp.concatenate(right, 1),
        (((1,), (1,)), ((), ())),
        preferred_element_type=F32,
    )


def dual_kernel(
    layer,
    wanted_ref,
    received_ref,
    cot_in,
    mask_ref,
    saved_ref,
    scale_ref,
    mix_ref,
    *refs,
):
    owned, channels, side = cot_in.shape
    tiles_refs, (cot_ref, send_ref, terms_ref) = refs[:-3], refs[-3:]
    above = layer + 1
    tau = scale_ref[pl.ds(2 * above, 1), :]
    pushed = sum_pushed(
        wanted_ref, received_ref, [jnp.zeros((channels, side), F32) for _ in range(owned)]
    )
    base, left, right = [], [], []
    mixed = mixed_by(mix_ref[2 * above], pushed)
    for b in range(owned):
        block = cot_in[b] + tau * mixed[b]
        cot = mask_ref[layer, pl.ds(b, 1), :].astype(F32) * block
        cot_ref[b] = cot
        base.append(cot)
        high, rest = halves(pushed[b])
        left.append(saved_ref[above, b])
        right.append(jnp.concatenate([high, rest, high, rest], 0))
    choose_for_all(wanted_ref, base, send_ref)
    terms_ref[0] = folded(contract(left, right), channels)
    for tiles_ref in tiles_refs:
        count = terms_ref.shape[0] - 1

        def step(t, sums):
            product = jnp.dot(
                received_ref[t, channels:, :], tiles_ref[t, :side, :], preferred_element_type=F32
            )
            at = place_of(tiles_ref, t, product.shape)
            return tuple(s + jnp.where(at == p, product, 0.0) for p, s in enumerate(sums))

        sums = tuple(jnp.zeros((channels, side), F32) for _ in range(count))
        if received_ref.shape[0] <= 16:
            for t in range(received_ref.shape[0]):
                sums = step(t, sums)
        else:
            sums = lax.fori_loop(0, received_ref.shape[0], step, sums)
        for p in range(count):
            terms_ref[1 + p] = sums[p]


def last_dual_kernel(
    row_scale,
    col_scale,
    wanted_ref,
    received_ref,
    cot_in,
    scale_ref,
    grad_in,
    grad_ref,
    cot_ref,
    primal_out,
    dual_out,
    held_ref,
    primal_ref,
    dual_ref,
    sems,
):
    owned, channels, side = held_ref.shape
    layers = primal_ref.shape[0]
    half = channels // 2
    rows = received_ref.shape[0]
    copies = [pltpu.make_async_copy(grad_in, grad_ref, sems.at[owned])]
    copies[0].start()
    blocks = sum_pushed(wanted_ref, received_ref, [cot_in[b] for b in range(owned)])
    for b, block in enumerate(blocks):
        held_ref[b] = block
        copy = pltpu.make_async_copy(held_ref.at[b], cot_ref.at[b], sems.at[b])
        copy.start()
        copies.append(copy)
    all_terms = total_of(
        rows, lambda r: received_ref[r, channels:, :].astype(F32), (layers * half, side)
    )
    for k in range(layers):
        terms = all_terms[k * half : (k + 1) * half]
        dual = scale_ref[pl.ds(2 * k + 1, 1), :] * row_scale * terms
        primal = scale_ref[pl.ds(2 * k, 1), :] * col_scale * terms
        dual_ref[k, :half, :] = dual[:, :channels]
        dual_ref[k, half:, :] = pltpu.roll(dual, side - channels, 1)[:, :channels]
        primal_ref[k, :half, :] = pltpu.roll(primal, side - 2 * channels, 1)[:, :channels]
        primal_ref[k, half:, :] = pltpu.roll(primal, side - 3 * channels, 1)[:, :channels]
    for i, (source, target) in enumerate(((primal_ref, primal_out), (dual_ref, dual_out))):
        copies.append(pltpu.make_async_copy(source, target, sems.at[owned + 1 + i]))
        copies[-1].start()
    for copy in copies:
        copy.wait()


def primal_step(layer, shared, grad_ref):
    tiles_ref, other_ref, scale_ref, mix_ref, fetched_ref, grad_in, mask_ref, saved_ref = shared
    blocks, channels, side = grad_ref.shape
    rows = tiles_ref.shape[0]
    me = lax.axis_index("col")
    sigma = scale_ref[pl.ds(2 * layer + 1, 1), :]

    def step(t, sums):
        for tiles, message in ((tiles_ref, 2 * t + 1 - me), (other_ref, 2 * t + me)):
            product = jnp.dot(
                fetched_ref[message], tiles[t, :side, :], preferred_element_type=F32
            )
            at = place_of(tiles, t, product.shape)
            sums = tuple(s + jnp.where(at == p, product, 0.0) for p, s in enumerate(sums))
        return sums

    sums = tuple(jnp.zeros((channels, side), F32) for _ in range(blocks))
    if rows <= 16:
        for t in range(rows):
            sums = step(t, sums)
    else:
        sums = lax.fori_loop(0, rows, step, sums)
    cots, extrapolated = [], []
    mixed = mixed_by(mix_ref[2 * layer + 1], sums)
    for p in range(blocks):
        back = sigma * mixed[p]
        cot = mask_ref[layer, pl.ds(p, 1), :].astype(F32) * (grad_in[p] + 2.0 * back)
        grad_ref[p] = cot - back
        cots.append(cot)
        extrapolated.append(
            (
                2.0 * saved_ref[layer + 1, p].astype(F32) - saved_ref[layer, p].astype(F32)
            ).astype(BF16)
        )
    return sums, cots, extrapolated


def push(tiles_ref, blocks, send_ref, below):
    channels, side = blocks[0].shape

    def one(t):
        at = place_of(tiles_ref, t, blocks[0].shape)
        picked = blocks[0]
        for p in range(1, len(blocks)):
            picked = jnp.where(at == p, blocks[p], picked)
        product = lax.dot_general(
            picked.astype(BF16),
            tiles_ref[t, :side, :],
            (((1,), (1,)), ((), ())),
            preferred_element_type=F32,
        )
        send_ref[t, :channels, :] = product.astype(BF16)
        if below is not None:
            send_ref[t, channels:, :] = below(t)

    loop(tiles_ref.shape[0], one)


def primal_kernel(layer, *refs):
    shared, rest, (grad_ref, send_ref, terms_ref) = refs[:8], refs[8:-3], refs[-3:]
    blocks, channels, side = grad_ref.shape
    sums, cots, extrapolated = primal_step(layer, shared, grad_ref)
    below = None
    if rest:
        wanted_ref, dual_ref = rest
        base = [dual_ref[0, b].astype(F32) for b in range(dual_ref.shape[1])]
        below = lambda t: chosen(wanted_ref, t, base)
    push(shared[0], cots, send_ref, below)
    right = []
    for p in range(blocks):
        high, low = halves(sums[p])
        right.append(jnp.concatenate([high, low, high, low], 0))
    terms_ref[...] = folded(contract(extrapolated, right), channels)


def last_primal_kernel(*refs):
    shared, rest, (grad_ref, send_ref) = refs[:8], refs[8:-2], refs[-2:]
    early_ref, early_other, late_ref, late_other, *dual_terms = rest
    scale_ref, mix_ref = shared[2], shared[3]
    blocks, channels, side = grad_ref.shape
    half = channels // 2
    sums, cots, extrapolated = primal_step(0, shared, grad_ref)
    tau = scale_ref[pl.ds(0, 1), :]
    left, right = [], []
    for p in range(blocks):
        pulled = early_ref[1 + p] + early_other[1 + p]
        left.append(jnp.concatenate([extrapolated[p], *halves(pulled)], 0))
        right.append(jnp.concatenate([*halves(sums[p]), *halves(cots[p])], 0))
    terms = contract(left, right)
    lane = lax.broadcasted_iota(jnp.int32, (channels, side), 1)
    low = lane < 2 * channels
    terms = jnp.where(
        low, terms[:channels], terms[channels : 2 * channels] + terms[2 * channels :]
    )
    primal_terms = (late_ref[0] + late_other[0], early_ref[0] + early_other[0])
    all_terms = [folded(terms, channels)] + [
        jnp.where(low, dual[...], primal) for dual, primal in zip(dual_terms, primal_terms)
    ]
    packed = jnp.concatenate(
        [
            jnp.where(
                lax.rem(lane[:half], 2 * channels) < channels,
                one[:half],
                pltpu.roll(one[half:], channels, 1),
            )
            for one in all_terms
        ],
        0,
    ).astype(BF16)
    mixed = [
        (tau * cot).astype(BF16).astype(F32) for cot in mixed_by(mix_ref[0], cots)
    ]
    push(shared[0], mixed, send_ref, lambda t: packed)


def per_device(
    tile_blocks,
    tile_rows,
    tile_cols,
    saved_primal,
    saved_dual,
    primal_active,
    dual_active,
    primal_mix,
    dual_mix,
    step_fracs,
    cot_primal,
    cot_dual,
):
    row_count = lax.axis_size("row")
    col_count = lax.axis_size("col")
    owned, channels, side = cot_dual.shape
    primal_count = cot_primal.shape[0]
    layer_count = primal_mix.shape[0]
    half = channels // 2
    row_scale = 1.0 / math.sqrt(owned * row_count * col_count * side)
    col_scale = 1.0 / math.sqrt(primal_count * row_count * side)
    params = pltpu.CompilerParams(vmem_limit_bytes=24 * 1024 * 1024)

    def call(kernel, outs, *operands, ins=None, out_specs=None, **rest):
        return pl.pallas_call(
            kernel,
            out_shape=outs,
            in_specs=ins or [VMEM] * len(operands),
            out_specs=out_specs or jax.tree.map(lambda _: VMEM, outs),
            compiler_params=params,
            **rest,
        )(*operands)

    shift = row_count - row_count // 2
    order = [(slot + row_count - shift) % row_count for slot in range(row_count)]
    order_all = [row * col_count + c for row in order for c in reversed(range(col_count))]

    def exchange(x, axes="row", group=order):
        return lax.all_to_all(
            x, axes, split_axis=0, concat_axis=0, axis_index_groups=[group], tiled=True
        )

    def shape(dims, kind=F32):
        return jax.ShapeDtypeStruct(dims, kind)

    def in_hbm(*arrays):
        return [pltpu.with_memory_space_constraint(x, pltpu.HBM) for x in arrays]

    def swap(x):
        return lax.ppermute(x, "col", [(i, col_count - 1 - i) for i in range(col_count)])

    slot = partial(slot_of, peer_size=owned * col_count, shift=shift, row_count=row_count)
    asked = call(
        partial(ask_kernel, slot, owned),
        shape((row_count, 1, side)),
        *in_hbm(tile_rows),
        ins=[HBM],
        scratch_shapes=[pltpu.SMEM(tile_rows.shape, jnp.int32), pltpu.SemaphoreType.DMA],
    )
    wanted = exchange(asked)
    tiles, scale, mix, cot = call(
        partial(prepare_kernel, slot, primal_count),
        (
            shape((row_count, side + 16, side), BF16),
            shape((2 * layer_count, side)),
            shape((2 * layer_count, channels, side), BF16),
            shape(cot_dual.shape),
        ),
        *in_hbm(
            tile_rows,
            tile_cols,
            step_fracs,
            tile_blocks,
            cot_dual,
            dual_active,
            dual_mix,
            primal_mix,
        ),
        ins=[HBM] * 8,
        scratch_shapes=[
            pltpu.VMEM((2 * layer_count, channels, side), F32),
            pltpu.SMEM(tile_rows.shape, jnp.int32),
            pltpu.SMEM(tile_cols.shape, jnp.int32),
            pltpu.SMEM(step_fracs.shape, jnp.int32),
            pltpu.VMEM((owned, side), jnp.int32),
            pltpu.VMEM((2, layer_count, channels, channels), F32),
            pltpu.VMEM(tile_blocks.shape, BF16),
            pltpu.SemaphoreType.DMA((8,)),
        ],
    )
    other_tiles = swap(lax.optimization_barrier((tiles, wanted))[0])
    blocks_out = shape((col_count * row_count, channels, side), BF16)
    grad_x = cot_primal
    send = call(first_dual_kernel, blocks_out, wanted, cot)
    dual_terms, primal_terms = [], []
    for layer in reversed(range(layer_count)):
        fetched = exchange(send, ("row", "col"), order_all)
        shared = (
            tiles,
            other_tiles,
            scale,
            mix,
            fetched,
            grad_x,
            primal_active,
            saved_primal,
        )
        if layer == 0:
            height = channels + layer_count * half
            grad_x, pushed = call(
                last_primal_kernel,
                (shape(cot_primal.shape), shape((row_count, height, side), BF16)),
                *shared,
                *primal_terms,
                *dual_terms[::-1],
            )
            received = exchange(pushed)
            break
        first = layer == layer_count - 1
        height = 2 * channels if first else channels
        grad_x, pushed, terms = call(
            partial(primal_kernel, layer),
            (
                shape(cot_primal.shape),
                shape((row_count, height, side), BF16),
                shape((channels, side)),
            ),
            *shared,
            *((wanted, saved_dual) if first else ()),
        )
        dual_terms.append(terms)
        received = exchange(pushed)
        cot, send, terms = call(
            partial(dual_kernel, layer - 1),
            (
                shape(cot_dual.shape),
                blocks_out,
                shape((1 + (primal_count if first else 0), channels, side)),
            ),
            wanted,
            received,
            cot,
            dual_active,
            saved_dual,
            scale,
            mix,
            *((tiles,) if first else ()),
        )
        primal_terms += [terms, swap(terms)]
    grad_x, grad_y, primal_mix_grad, dual_mix_grad = call(
        partial(last_dual_kernel, row_scale, col_scale),
        (
            shape(cot_primal.shape),
            shape(cot_dual.shape),
            shape(primal_mix.shape),
            shape(dual_mix.shape),
        ),
        wanted,
        received,
        cot,
        scale,
        grad_x,
        out_specs=(HBM,) * 4,
        scratch_shapes=[
            pltpu.VMEM(cot_dual.shape, F32),
            pltpu.VMEM(primal_mix.shape, F32),
            pltpu.VMEM(dual_mix.shape, F32),
            pltpu.SemaphoreType.DMA((owned + 3,)),
        ],
    )
    return (grad_x, grad_y, primal_mix_grad, dual_mix_grad)


def solution(mesh):
    return jax.shard_map(
        per_device,
        mesh=mesh,
        in_specs=(
            P(("groups", "row", "col"), None, None),
            P(("groups", "row", "col")),
            P(("groups", "row", "col")),
            P(None, ("groups", "row"), None, None),
            P(None, ("groups", "row", "col"), None, None),
            P(None, ("groups", "row"), None),
            P(None, ("groups", "row", "col"), None),
            P(),
            P(),
            P(),
            P(("groups", "row"), None, None),
            P(("groups", "row", "col"), None, None),
        ),
        out_specs=(
            P(("groups", "row"), None, None),
            P(("groups", "row", "col"), None, None),
            P("groups", None, None),
            P("groups", None, None),
        ),
        check_vma=False,
    )
```

time: 75.5 us -> 74.4 us (0.985)
  blocking collectives: 53.4 us -> 46 us
  starting transfers between devices: 8.04 us -> 12.3 us
  waiting for transfers between devices: 6.73 us -> 7.85 us
  Pallas kernels: 6.19 us -> 7.06 us
    all_to_all x6 -> x5, blocking collectives: 53.4 us -> 46 us  [exchange(): lax.all_to_all(x, axes, split_axis=0, concat_axis=0, axis_index_groups=[g...]
    all_to_all x1 -> x2, waiting for transfers between devices: 2.72 us -> 7.01 us  [exchange(): lax.all_to_all(x, axes, split_axis=0, concat_axis=0, axis_index_groups=[g...]
    all_to_all x1 -> x2, starting transfers between devices: 7.83 us -> 11.8 us  [exchange(): lax.all_to_all(x, axes, split_axis=0, concat_axis=0, axis_index_groups=[g...]
    ppermute x3, waiting for transfers between devices: 4 us -> 0.84 us  [swap(): lax.ppermute(x, 'col', [(i, col_count - 1 - i) for i in range(col_count)])]
    pallas_call x12 -> x9, Pallas kernels: 6.19 us -> 7.06 us  [call(): pl.pallas_call(kernel, out_shape=outs, in_specs=ins or [VMEM] * len(opera...]
  transfers between devices with their start and end apart: 4 -> 5, of which waited for: 4 -> 4; matrix products, arithmetic and copies ran while one was open for 0% -> 0% of each run, Pallas kernels for 2% -> 2%
where the time goes in v6:
time: 74.4 us; the launch traced here: 73.9 us
  blocking collectives  46 us (62%)
  starting transfers between devices  12.3 us (17%)
  waiting for transfers between devices  7.85 us (11%)
  Pallas kernels  7.06 us (9%)
    all_to_all x5, blocking collectives, exchange(): lax.all_to_all(x, axes, split_axis=0, concat_axis=0, axis_index_groups=[g...  46 us
    all_to_all x2, starting transfers between devices, exchange(): lax.all_to_all(x, axes, split_axis=0, concat_axis=0, axis_index_groups=[g...  11.8 us
    pallas_call x9, Pallas kernels, call(): pl.pallas_call(kernel, out_shape=outs, in_specs=ins or [VMEM] * len(opera...  7.06 us
    all_to_all x2, waiting for transfers between devices, exchange(): lax.all_to_all(x, axes, split_axis=0, concat_axis=0, axis_index_groups=[g...  7.01 us
  transfers between devices with their start and end apart: 5, of which 4 were waited for; matrix products, arithmetic and copies ran while one was open for 0% of the time, Pallas kernels for 2%

profile of v6, /device:TPU:0, one launch (start us, length us, event | category | flops | bytes accessed | tf_op | source)
XLA Modules:
  0.0 73.9 jit_solution(11201710843475391111)
XLA Ops:
  0.6 1.3 %shard_map.147 = f32[8,1,128]{2,1,0:T(1,128)} custom-call(s32[8]{0:T(128)} %rows_in.3), custom_call_target="tpu_custom_call" | custom-call | tf_op jit(solution)/shard_map/pallas_call | solution.py:442
  1.9 7.8 %all-to-all-start = ((f32[8,1,128]{2,1,0:T(1,128)}), f32[8,1,128]{2,1,0:T(1,128)S(1)}, u32[]{:S(2)}, u32[]{:S(2)}) async-start(f32[8,1,128]{2,1,0:T(1,128)} %shard_map.147), calls=%async_computation | async-start | bytes 8192 | tf_op jit(solution)/shard_map/all_to_all | solution.py:456
  9.8 1.3 %shard_map.148 = (bf16[8,144,128]{2,1,0:T(8,128)(2,1)S(1)}, f32[6,128]{1,0:T(8,128)S(1)}, bf16[6,32,128]{2,1,0:T(8,128)(2,1)S(1)}, f32[8,32,128]{2,1,0:T(8,128)S(1)}) custom-call(s32[8]{0:T(128)} %rows_in.3, s32[8]{0:T(128)} %cols_in.1, s32[3,4]{1,0:T(4,128)} %steps_in.1, bf16[8,128,128]{2,1,0:T(8,128)(2,1)} %tiles_in.1, f32[8,32,128]{2,1,0:T(8,128)} %cot_in.1, ...), custom_call_target="tpu_custom_call" | custom-call | tf_op jit(solution)/shard_map/pallas_call | solution.py:442
  11.0 2.8 %all-to-all-done.wanted_ref.refs_8_ = f32[8,1,128]{2,1,0:T(1,128)S(1)} async-done(((f32[8,1,128]{2,1,0:T(1,128)}), f32[8,1,128]{2,1,0:T(1,128)S(1)}, u32[]{:S(2)}, u32[]{:S(2)}) %all-to-all-start) | async-done | bytes 4128 | tf_op jit(solution)/shard_map/all_to_all | solution.py:456
  13.9 0.0 copy-start
  13.9 0.0 copy-start.3
  13.9 9.8 %all_to_all.35.refs_4_ = bf16[16,32,128]{2,1,0:T(8,128)(2,1)S(1)} all-to-all(bf16[16,32,128]{2,1,0:T(8,128)(2,1)S(1)} %shard_map.149), channel_id=1, replica_groups={{9,8,11,10,13,12,15,14,1,0,3,2,5,4,7,6},{25,24,27,26,29,28,31,30,17,16,..., dimensions={0} | all-to-all | bytes 262144 | tf_op jit(solution)/shard_map/all_to_all | solution.py:456
  23.6 0.0 collective-permute-done.refs_1_
  23.7 0.7 shard_map.150
  24.4 9.1 %all_to_all.36.received_ref = bf16[8,64,128]{2,1,0:T(8,128)(2,1)S(1)} all-to-all(bf16[8,64,128]{2,1,0:T(8,128)(2,1)S(1)} %get-tuple-element.28), channel_id=1, replica_groups={{8,10,12,14,0,2,4,6},{9,11,13,15,1,3,5,7},{24,26,28,30,16,18,20,22},{25..., dimensions={0} | all-to-all | bytes 262144 | tf_op jit(solution)/shard_map/all_to_all | solution.py:456
  33.5 0.5 shard_map.151
  34.0 9.4 %all_to_all.37.refs_4_ = bf16[16,32,128]{2,1,0:T(8,128)(2,1)S(1)} all-to-all(bf16[16,32,128]{2,1,0:T(8,128)(2,1)S(1)} %get-tuple-element.29), channel_id=1, replica_groups={{9,8,11,10,13,12,15,14,1,0,3,2,5,4,7,6},{25,24,27,26,29,28,31,30,17,16,..., dimensions={0} | all-to-all | bytes 262144 | tf_op jit(solution)/shard_map/all_to_all | solution.py:456
  43.3 0.7 shard_map.152
  44.0 8.6 %all_to_all.38.received_ref = bf16[8,32,128]{2,1,0:T(8,128)(2,1)S(1)} all-to-all(bf16[8,32,128]{2,1,0:T(8,128)(2,1)S(1)} %get-tuple-element.31), channel_id=1, replica_groups={{8,10,12,14,0,2,4,6},{9,11,13,15,1,3,5,7},{24,26,28,30,16,18,20,22},{25..., dimensions={0} | all-to-all | bytes 131072 | tf_op jit(solution)/shard_map/all_to_all | solution.py:456
  52.6 0.9 %shard_map.153 = (f32[8,32,128]{2,1,0:T(8,128)S(1)}, bf16[16,32,128]{2,1,0:T(8,128)(2,1)}, f32[1,32,128]{2,1,0:T(8,128)S(1)}) custom-call(f32[8,1,128]{2,1,0:T(1,128)S(1)} %all-to-all-done.wanted_ref.refs_8_, bf16[8,32,128]{2,1,0:T(8,128)(2,1)S(1)} %all_to_all.38.received_ref, f32[8,32,128]{2,1,0:T(8,128)S(1)} %get-tuple-element.32.cot_in, ...), custom_call_target="tpu_custom_call" | custom-call | tf_op jit(solution)/shard_map/pallas_call | solution.py:442
  53.5 4.0 %all-to-all-start.5 = ((bf16[16,32,128]{2,1,0:T(8,128)(2,1)}), bf16[16,32,128]{2,1,0:T(8,128)(2,1)S(1)}, u32[]{:S(2)}, u32[]{:S(2)}) async-start(bf16[16,32,128]{2,1,0:T(8,128)(2,1)} %get-tuple-element.33), calls=%async_computation.5 | async-start | bytes 262144 | tf_op jit(solution)/shard_map/all_to_all | solution.py:456
  57.5 0.1 collective-permute-start.1
  57.6 0.4 collective-permute-start.2
  58.0 0.8 %collective-permute-done.1.refs_9_ = f32[5,32,128]{2,1,0:T(8,128)S(1)} collective-permute-done((f32[5,32,128]{2,1,0:T(8,128)S(1)}, f32[5,32,128]{2,1,0:T(8,128)S(1)}, u32[]{:S(2)}, u32[]{:S(2)}) %collective-permute-start.1) | collective-permute-done | bytes 81952 | tf_op jit(solution)/shard_map/ppermute | solution.py:467
  58.8 0.1 collective-permute-done.2.refs_11_
  58.8 4.2 %all-to-all-done.5.refs_4_ = bf16[16,32,128]{2,1,0:T(8,128)(2,1)S(1)} async-done(((bf16[16,32,128]{2,1,0:T(8,128)(2,1)}), bf16[16,32,128]{2,1,0:T(8,128)(2,1)S(1)}, u32[]{:S(2)}, u32[]{:S(2)}) %all-to-all-start.5) | async-done | bytes 131104 | tf_op jit(solution)/shard_map/all_to_all | solution.py:456
  63.1 0.8 %shard_map.154 = (f32[4,32,128]{2,1,0:T(8,128)S(1)}, bf16[8,80,128]{2,1,0:T(8,128)(2,1)S(1)}) custom-call(bf16[8,144,128]{2,1,0:T(8,128)(2,1)S(1)} %get-tuple-element.24.refs_0_, bf16[8,144,128]{2,1,0:T(8,128)(2,1)S(1)} %collective-permute-done.refs_1_, f32[6,128]{1,0:T(8,128)S(1)} %get-tuple-element.25.refs_2_.scale_ref, ...), custom_call_target="tpu_custom_call" | custom-call | tf_op jit(solution)/shard_map/pallas_call | solution.py:442
  63.9 9.2 %all_to_all.39.received_ref = bf16[8,80,128]{2,1,0:T(8,128)(2,1)S(1)} all-to-all(bf16[8,80,128]{2,1,0:T(8,128)(2,1)S(1)} %get-tuple-element.39), channel_id=1, replica_groups={{8,10,12,14,0,2,4,6},{9,11,13,15,1,3,5,7},{24,26,28,30,16,18,20,22},{25..., dimensions={0} | all-to-all | bytes 327680 | tf_op jit(solution)/shard_map/all_to_all | solution.py:456
  73.1 0.8 %shard_map.155 = (f32[4,32,128]{2,1,0:T(8,128)}, f32[8,32,128]{2,1,0:T(8,128)}, f32[3,32,32]{2,1,0:T(8,128)}, f32[3,32,32]{2,1,0:T(8,128)}) custom-call(f32[8,1,128]{2,1,0:T(1,128)S(1)} %all-to-all-done.wanted_ref.refs_8_, bf16[8,80,128]{2,1,0:T(8,128)(2,1)S(1)} %all_to_all.39.received_ref, f32[8,32,128]{2,1,0:T(8,128)S(1)} %get-tuple-element.40.cot_in, ...), custom_call_target="tpu_custom_call" | custom-call | tf_op jit(solution)/shard_map/pallas_call | solution.py:442
  (10 shorter events, 0.1 us)
Async XLA Ops:
  1.9 11.9 %all-to-all-start = ((f32[8,1,128]{2,1,0:T(1,128)}), f32[8,1,128]{2,1,0:T(1,128)S(1)}, u32[]{:S(2)}, u32[]{:S(2)}) async-start(f32[8,1,128]{2,1,0:T(1,128)} %shard_map.147), calls=%async_computation | async-start | bytes 8192 | tf_op jit(solution)/shard_map/all_to_all | solution.py:456
  13.8 9.8 %collective-permute-start = (bf16[8,144,128]{2,1,0:T(8,128)(2,1)S(1)}, bf16[8,144,128]{2,1,0:T(8,128)(2,1)S(1)}, u32[]{:S(2)}, u32[]{:S(2)}) collective-permute-start(bf16[8,144,128]{2,1,0:T(8,128)(2,1)S(1)} %get-tuple-element.24.refs_0_), channel_id=1, source_target_pairs={{0,1},{1,0},{2,3},{3,2},{4,5},{5,4},{6,7},{7,6},{8,9},{9,8},{10,11... | collective-permute-start | bytes 884744 | tf_op jit(solution)/shard_map/ppermute | solution.py:467
  13.8 9.8 %copy-start.1 = (bf16[4,4,32,128]{3,2,1,0:T(8,128)(2,1)S(1)}, bf16[4,4,32,128]{3,2,1,0:T(8,128)(2,1)}, u32[]{:S(2)}) copy-start(bf16[4,4,32,128]{3,2,1,0:T(8,128)(2,1)} %refs_7_.5) | copy-start | bytes 393220
  13.8 9.8 %copy-start.4 = (s32[3,4,128]{2,1,0:T(4,128)S(1)}, s32[3,4,128]{2,1,0:T(4,128)}, u32[]{:S(2)}) copy-start(s32[3,4,128]{2,1,0:T(4,128)} %refs_6_.5) | copy-start | bytes 18436
  13.9 9.8 %copy-start = (bf16[3,8,32,128]{3,2,1,0:T(8,128)(2,1)S(1)}, bf16[3,8,32,128]{3,2,1,0:T(8,128)(2,1)}, u32[]{:S(2)}) copy-start(bf16[3,8,32,128]{3,2,1,0:T(8,128)(2,1)} %saved_ref.3) | copy-start | bytes 589828
  13.9 9.8 %copy-start.3 = (f32[4,32,128]{2,1,0:T(8,128)S(1)}, f32[4,32,128]{2,1,0:T(8,128)}, u32[]{:S(2)}) copy-start(f32[4,32,128]{2,1,0:T(8,128)} %refs_5_.1) | copy-start | bytes 196612
  24.4 9.1 %copy-start.2 = (s32[3,8,128]{2,1,0:T(8,128)S(1)}, s32[3,8,128]{2,1,0:T(8,128)}, u32[]{:S(2)}) copy-start(s32[3,8,128]{2,1,0:T(8,128)} %mask_ref.3) | copy-start | bytes 36868
  53.5 9.6 %all-to-all-start.5 = ((bf16[16,32,128]{2,1,0:T(8,128)(2,1)}), bf16[16,32,128]{2,1,0:T(8,128)(2,1)S(1)}, u32[]{:S(2)}, u32[]{:S(2)}) async-start(bf16[16,32,128]{2,1,0:T(8,128)(2,1)} %get-tuple-element.33), calls=%async_computation.5 | async-start | bytes 262144 | tf_op jit(solution)/shard_map/all_to_all | solution.py:456
  57.5 1.3 %collective-permute-start.1 = (f32[5,32,128]{2,1,0:T(8,128)S(1)}, f32[5,32,128]{2,1,0:T(8,128)S(1)}, u32[]{:S(2)}, u32[]{:S(2)}) collective-permute-start(f32[5,32,128]{2,1,0:T(8,128)S(1)} %get-tuple-element.35.refs_8_), channel_id=1, source_target_pairs={{0,1},{1,0},{2,3},{3,2},{4,5},{5,4},{6,7},{7,6},{8,9},{9,8},{10,11... | collective-permute-start | bytes 245768 | tf_op jit(solution)/shard_map/ppermute | solution.py:467
  57.6 1.3 %collective-permute-start.2 = (f32[1,32,128]{2,1,0:T(8,128)S(1)}, f32[1,32,128]{2,1,0:T(8,128)S(1)}, u32[]{:S(2)}, u32[]{:S(2)}) collective-permute-start(f32[1,32,128]{2,1,0:T(8,128)S(1)} %get-tuple-element.36.refs_10_), channel_id=1, source_target_pairs={{0,1},{1,0},{2,3},{3,2},{4,5},{5,4},{6,7},{7,6},{8,9},{9,8},{10,11... | collective-permute-start | bytes 49160 | tf_op jit(solution)/shard_map/ppermute | solution.py:467

commit v7 on v6

--- a/solution.py
+++ b/solution.py
@@ -175,9 +175,17 @@
     return lax.fori_loop(0, rows, step, blocks)
 
 
-def place_of(tiles_ref, t, shape):
-    side = tiles_ref.shape[2]
-    return jnp.broadcast_to(tiles_ref[t, side:, :].astype(F32)[:1], shape)
+def place_of(tile, shape):
+    side = tile.shape[1]
+    return jnp.broadcast_to(tile[side:].astype(F32)[:1], shape)
+
+
+def pushed_tile(tiles_ref, other_ref, t):
+    rows = lax.axis_size("row")
+    upper = lax.axis_index("row") >= rows // 2
+    here = t < rows - rows // 2
+    own = upper == here
+    return jnp.where(own, tiles_ref[t], other_ref[t])
 
 
 def mixed_by(weights, blocks):
@@ -232,14 +240,15 @@
         right.append(jnp.concatenate([high, rest, high, rest], 0))
     choose_for_all(wanted_ref, base, send_ref)
     terms_ref[0] = folded(contract(left, right), channels)
-    for tiles_ref in tiles_refs:
+    if tiles_refs:
         count = terms_ref.shape[0] - 1
 
         def step(t, sums):
+            tile = pushed_tile(*tiles_refs, t)
             product = jnp.dot(
-                received_ref[t, channels:, :], tiles_ref[t, :side, :], preferred_element_type=F32
+                received_ref[t, channels:, :], tile[:side], preferred_element_type=F32
             )
-            at = place_of(tiles_ref, t, product.shape)
+            at = place_of(tile, product.shape)
             return tuple(s + jnp.where(at == p, product, 0.0) for p, s in enumerate(sums))
 
         sums = tuple(jnp.zeros((channels, side), F32) for _ in range(count))
@@ -311,7 +320,7 @@
             product = jnp.dot(
                 fetched_ref[message], tiles[t, :side, :], preferred_element_type=F32
             )
-            at = place_of(tiles, t, product.shape)
+            at = place_of(tiles[t], product.shape)
             sums = tuple(s + jnp.where(at == p, product, 0.0) for p, s in enumerate(sums))
         return sums
 
@@ -336,17 +345,18 @@
     return sums, cots, extrapolated
 
 
-def push(tiles_ref, blocks, send_ref, below):
+def push(tiles_ref, other_ref, blocks, send_ref, below):
     channels, side = blocks[0].shape
 
     def one(t):
-        at = place_of(tiles_ref, t, blocks[0].shape)
+        tile = pushed_tile(tiles_ref, other_ref, t)
+        at = place_of(tile, blocks[0].shape)
         picked = blocks[0]
         for p in range(1, len(blocks)):
             picked = jnp.where(at == p, blocks[p], picked)
         product = lax.dot_general(
             picked.astype(BF16),
-            tiles_ref[t, :side, :],
+            tile[:side],
             (((1,), (1,)), ((), ())),
             preferred_element_type=F32,
         )
@@ -366,7 +376,7 @@
         wanted_ref, dual_ref = rest
         base = [dual_ref[0, b].astype(F32) for b in range(dual_ref.shape[1])]
         below = lambda t: chosen(wanted_ref, t, base)
-    push(shared[0], cots, send_ref, below)
+    push(*shared[:2], cots, send_ref, below)
     right = []
     for p in range(blocks):
         high, low = halves(sums[p])
@@ -411,7 +421,7 @@
     mixed = [
         (tau * cot).astype(BF16).astype(F32) for cot in mixed_by(mix_ref[0], cots)
     ]
-    push(shared[0], mixed, send_ref, lambda t: packed)
+    push(*shared[:2], mixed, send_ref, lambda t: packed)
 
 
 def per_device(
@@ -452,9 +462,17 @@
     order = [(slot + row_count - shift) % row_count for slot in range(row_count)]
     order_all = [row * col_count + c for row in order for c in reversed(range(col_count))]
 
-    def exchange(x, axes="row", group=order):
+    order_push = [
+        [
+            row * col_count + (c if i < shift else col_count - 1 - c)
+            for i, row in enumerate(order)
+        ]
+        for c in range(col_count)
+    ]
+
+    def exchange(x, axes, groups):
         return lax.all_to_all(
-            x, axes, split_axis=0, concat_axis=0, axis_index_groups=[group], tiled=True
+            x, axes, split_axis=0, concat_axis=0, axis_index_groups=groups, tiled=True
         )
 
     def shape(dims, kind=F32):
@@ -474,7 +492,7 @@
         ins=[HBM],
         scratch_shapes=[pltpu.SMEM(tile_rows.shape, jnp.int32), pltpu.SemaphoreType.DMA],
     )
-    wanted = exchange(asked)
+    wanted = exchange(asked, "row", [order])
     tiles, scale, mix, cot = call(
         partial(prepare_kernel, slot, primal_count),
         (
@@ -511,7 +529,7 @@
     send = call(first_dual_kernel, blocks_out, wanted, cot)
     dual_terms, primal_terms = [], []
     for layer in reversed(range(layer_count)):
-        fetched = exchange(send, ("row", "col"), order_all)
+        fetched = exchange(send, ("row", "col"), [order_all])
         shared = (
             tiles,
             other_tiles,
@@ -531,7 +549,7 @@
                 *primal_terms,
                 *dual_terms[::-1],
             )
-            received = exchange(pushed)
+            received = exchange(pushed, ("row", "col"), order_push)
             break
         first = layer == layer_count - 1
         height = 2 * channels if first else channels
@@ -546,7 +564,7 @@
             *((wanted, saved_dual) if first else ()),
         )
         dual_terms.append(terms)
-        received = exchange(pushed)
+        received = exchange(pushed, ("row", "col"), order_push)
         cot, send, terms = call(
             partial(dual_kernel, layer - 1),
             (
@@ -561,7 +579,7 @@
             saved_dual,
             scale,
             mix,
-            *((tiles,) if first else ()),
+            *((tiles, other_tiles) if first else ()),
         )
         primal_terms += [terms, swap(terms)]
     grad_x, grad_y, primal_mix_grad, dual_mix_grad = call(

time: 74.4 us -> 73.7 us (level)
  blocking collectives: 46 us -> 44.8 us
    all_to_all x5, blocking collectives: 46 us -> 44.8 us  [exchange(): lax.all_to_all(x, axes, split_axis=0, concat_axis=0, axis_index_groups=gr...]
where the time goes in v7:
time: 73.7 us; the launch traced here: 73.2 us
  blocking collectives  44.8 us (61%)
  starting transfers between devices  12.7 us (17%)
  waiting for transfers between devices  7.83 us (11%)
  Pallas kernels  7.07 us (10%)
    all_to_all x5, blocking collectives, exchange(): lax.all_to_all(x, axes, split_axis=0, concat_axis=0, axis_index_groups=gr...  44.8 us
    all_to_all x2, starting transfers between devices, exchange(): lax.all_to_all(x, axes, split_axis=0, concat_axis=0, axis_index_groups=gr...  12.2 us
    pallas_call x9, Pallas kernels, call(): pl.pallas_call(kernel, out_shape=outs, in_specs=ins or [VMEM] * len(opera...  7.07 us
    all_to_all x2, waiting for transfers between devices, exchange(): lax.all_to_all(x, axes, split_axis=0, concat_axis=0, axis_index_groups=gr...  6.99 us
  transfers between devices with their start and end apart: 5, of which 4 were waited for; matrix products, arithmetic and copies ran while one was open for 0% of the time, Pallas kernels for 2%

profile of v7, /device:TPU:0, one launch (start us, length us, event | category | flops | bytes accessed | tf_op | source)
XLA Modules:
  0.0 73.2 jit_solution(5345451486707488834)
XLA Ops:
  0.6 1.3 %shard_map.147 = f32[8,1,128]{2,1,0:T(1,128)} custom-call(s32[8]{0:T(128)} %rows_in.3), custom_call_target="tpu_custom_call" | custom-call | tf_op jit(solution)/shard_map/pallas_call | solution.py:452
  1.9 7.8 %all-to-all-start = ((f32[8,1,128]{2,1,0:T(1,128)}), f32[8,1,128]{2,1,0:T(1,128)S(1)}, u32[]{:S(2)}, u32[]{:S(2)}) async-start(f32[8,1,128]{2,1,0:T(1,128)} %shard_map.147), calls=%async_computation | async-start | bytes 8192 | tf_op jit(solution)/shard_map/all_to_all | solution.py:474
  9.8 1.3 %shard_map.148 = (bf16[8,144,128]{2,1,0:T(8,128)(2,1)S(1)}, f32[6,128]{1,0:T(8,128)S(1)}, bf16[6,32,128]{2,1,0:T(8,128)(2,1)S(1)}, f32[8,32,128]{2,1,0:T(8,128)S(1)}) custom-call(s32[8]{0:T(128)} %rows_in.3, s32[8]{0:T(128)} %cols_in.1, s32[3,4]{1,0:T(4,128)} %steps_in.1, bf16[8,128,128]{2,1,0:T(8,128)(2,1)} %tiles_in.1, f32[8,32,128]{2,1,0:T(8,128)} %cot_in.1, ...), custom_call_target="tpu_custom_call" | custom-call | tf_op jit(solution)/shard_map/pallas_call | solution.py:452
  11.0 2.8 %all-to-all-done.wanted_ref.refs_8_ = f32[8,1,128]{2,1,0:T(1,128)S(1)} async-done(((f32[8,1,128]{2,1,0:T(1,128)}), f32[8,1,128]{2,1,0:T(1,128)S(1)}, u32[]{:S(2)}, u32[]{:S(2)}) %all-to-all-start) | async-done | bytes 4128 | tf_op jit(solution)/shard_map/all_to_all | solution.py:474
  13.8 0.0 collective-permute-start
  13.9 0.0 copy-start
  13.9 0.0 copy-start.3
  13.9 9.8 %all_to_all.35.refs_4_ = bf16[16,32,128]{2,1,0:T(8,128)(2,1)S(1)} all-to-all(bf16[16,32,128]{2,1,0:T(8,128)(2,1)S(1)} %shard_map.149), channel_id=1, replica_groups={{9,8,11,10,13,12,15,14,1,0,3,2,5,4,7,6},{25,24,27,26,29,28,31,30,17,16,..., dimensions={0} | all-to-all | bytes 262144 | tf_op jit(solution)/shard_map/all_to_all | solution.py:474
  23.7 0.7 shard_map.150
  24.4 8.8 %all_to_all.36.received_ref = bf16[8,64,128]{2,1,0:T(8,128)(2,1)S(1)} all-to-all(bf16[8,64,128]{2,1,0:T(8,128)(2,1)S(1)} %get-tuple-element.28), channel_id=1, replica_groups={{8,10,12,14,1,3,5,7},{9,11,13,15,0,2,4,6},{24,26,28,30,17,19,21,23},{25..., dimensions={0} | all-to-all | bytes 262144 | tf_op jit(solution)/shard_map/all_to_all | solution.py:474
  33.2 0.5 shard_map.151
  33.6 9.4 %all_to_all.37.refs_4_ = bf16[16,32,128]{2,1,0:T(8,128)(2,1)S(1)} all-to-all(bf16[16,32,128]{2,1,0:T(8,128)(2,1)S(1)} %get-tuple-element.29), channel_id=1, replica_groups={{9,8,11,10,13,12,15,14,1,0,3,2,5,4,7,6},{25,24,27,26,29,28,31,30,17,16,..., dimensions={0} | all-to-all | bytes 262144 | tf_op jit(solution)/shard_map/all_to_all | solution.py:474
  43.0 0.7 shard_map.152
  43.7 7.8 %all_to_all.38.received_ref = bf16[8,32,128]{2,1,0:T(8,128)(2,1)S(1)} all-to-all(bf16[8,32,128]{2,1,0:T(8,128)(2,1)S(1)} %get-tuple-element.31), channel_id=1, replica_groups={{8,10,12,14,1,3,5,7},{9,11,13,15,0,2,4,6},{24,26,28,30,17,19,21,23},{25..., dimensions={0} | all-to-all | bytes 131072 | tf_op jit(solution)/shard_map/all_to_all | solution.py:474
  51.5 0.9 %shard_map.153 = (f32[8,32,128]{2,1,0:T(8,128)S(1)}, bf16[16,32,128]{2,1,0:T(8,128)(2,1)}, f32[1,32,128]{2,1,0:T(8,128)S(1)}) custom-call(f32[8,1,128]{2,1,0:T(1,128)S(1)} %all-to-all-done.wanted_ref.refs_8_, bf16[8,32,128]{2,1,0:T(8,128)(2,1)S(1)} %all_to_all.38.received_ref, f32[8,32,128]{2,1,0:T(8,128)S(1)} %get-tuple-element.32.cot_in, ...), custom_call_target="tpu_custom_call" | custom-call | tf_op jit(solution)/shard_map/pallas_call | solution.py:452
  52.5 4.4 %all-to-all-start.5 = ((bf16[16,32,128]{2,1,0:T(8,128)(2,1)}), bf16[16,32,128]{2,1,0:T(8,128)(2,1)S(1)}, u32[]{:S(2)}, u32[]{:S(2)}) async-start(bf16[16,32,128]{2,1,0:T(8,128)(2,1)} %get-tuple-element.33), calls=%async_computation.5 | async-start | bytes 262144 | tf_op jit(solution)/shard_map/all_to_all | solution.py:474
  56.8 0.1 collective-permute-start.1
  56.9 0.4 collective-permute-start.2
  57.4 0.8 %collective-permute-done.1.refs_9_ = f32[5,32,128]{2,1,0:T(8,128)S(1)} collective-permute-done((f32[5,32,128]{2,1,0:T(8,128)S(1)}, f32[5,32,128]{2,1,0:T(8,128)S(1)}, u32[]{:S(2)}, u32[]{:S(2)}) %collective-permute-start.1) | collective-permute-done | bytes 81952 | tf_op jit(solution)/shard_map/ppermute | solution.py:485
  58.1 0.1 collective-permute-done.2.refs_11_
  58.2 4.2 %all-to-all-done.5.refs_4_ = bf16[16,32,128]{2,1,0:T(8,128)(2,1)S(1)} async-done(((bf16[16,32,128]{2,1,0:T(8,128)(2,1)}), bf16[16,32,128]{2,1,0:T(8,128)(2,1)S(1)}, u32[]{:S(2)}, u32[]{:S(2)}) %all-to-all-start.5) | async-done | bytes 131104 | tf_op jit(solution)/shard_map/all_to_all | solution.py:474
  62.4 0.8 %shard_map.154 = (f32[4,32,128]{2,1,0:T(8,128)S(1)}, bf16[8,80,128]{2,1,0:T(8,128)(2,1)S(1)}) custom-call(bf16[8,144,128]{2,1,0:T(8,128)(2,1)S(1)} %get-tuple-element.24.refs_0_, bf16[8,144,128]{2,1,0:T(8,128)(2,1)S(1)} %collective-permute-done.refs_1_, f32[6,128]{1,0:T(8,128)S(1)} %get-tuple-element.25.refs_2_.scale_ref, ...), custom_call_target="tpu_custom_call" | custom-call | tf_op jit(solution)/shard_map/pallas_call | solution.py:452
  63.2 9.1 %all_to_all.39.received_ref = bf16[8,80,128]{2,1,0:T(8,128)(2,1)S(1)} all-to-all(bf16[8,80,128]{2,1,0:T(8,128)(2,1)S(1)} %get-tuple-element.39), channel_id=1, replica_groups={{8,10,12,14,1,3,5,7},{9,11,13,15,0,2,4,6},{24,26,28,30,17,19,21,23},{25..., dimensions={0} | all-to-all | bytes 327680 | tf_op jit(solution)/shard_map/all_to_all | solution.py:474
  72.3 0.8 %shard_map.155 = (f32[4,32,128]{2,1,0:T(8,128)}, f32[8,32,128]{2,1,0:T(8,128)}, f32[3,32,32]{2,1,0:T(8,128)}, f32[3,32,32]{2,1,0:T(8,128)}) custom-call(f32[8,1,128]{2,1,0:T(1,128)S(1)} %all-to-all-done.wanted_ref.refs_8_, bf16[8,80,128]{2,1,0:T(8,128)(2,1)S(1)} %all_to_all.39.received_ref, f32[8,32,128]{2,1,0:T(8,128)S(1)} %get-tuple-element.40.cot_in, ...), custom_call_target="tpu_custom_call" | custom-call | tf_op jit(solution)/shard_map/pallas_call | solution.py:452
  (10 shorter events, 0.1 us)
Async XLA Ops:
  1.9 11.9 %all-to-all-start = ((f32[8,1,128]{2,1,0:T(1,128)}), f32[8,1,128]{2,1,0:T(1,128)S(1)}, u32[]{:S(2)}, u32[]{:S(2)}) async-start(f32[8,1,128]{2,1,0:T(1,128)} %shard_map.147), calls=%async_computation | async-start | bytes 8192 | tf_op jit(solution)/shard_map/all_to_all | solution.py:474
  13.8 9.8 %collective-permute-start = (bf16[8,144,128]{2,1,0:T(8,128)(2,1)S(1)}, bf16[8,144,128]{2,1,0:T(8,128)(2,1)S(1)}, u32[]{:S(2)}, u32[]{:S(2)}) collective-permute-start(bf16[8,144,128]{2,1,0:T(8,128)(2,1)S(1)} %get-tuple-element.24.refs_0_), channel_id=1, source_target_pairs={{0,1},{1,0},{2,3},{3,2},{4,5},{5,4},{6,7},{7,6},{8,9},{9,8},{10,11... | collective-permute-start | bytes 884744 | tf_op jit(solution)/shard_map/ppermute | solution.py:485
  13.8 9.8 %copy-start.1 = (bf16[4,4,32,128]{3,2,1,0:T(8,128)(2,1)S(1)}, bf16[4,4,32,128]{3,2,1,0:T(8,128)(2,1)}, u32[]{:S(2)}) copy-start(bf16[4,4,32,128]{3,2,1,0:T(8,128)(2,1)} %refs_7_.5) | copy-start | bytes 393220
  13.8 9.8 %copy-start.4 = (s32[3,4,128]{2,1,0:T(4,128)S(1)}, s32[3,4,128]{2,1,0:T(4,128)}, u32[]{:S(2)}) copy-start(s32[3,4,128]{2,1,0:T(4,128)} %refs_6_.5) | copy-start | bytes 18436
  13.9 9.8 %copy-start = (bf16[3,8,32,128]{3,2,1,0:T(8,128)(2,1)S(1)}, bf16[3,8,32,128]{3,2,1,0:T(8,128)(2,1)}, u32[]{:S(2)}) copy-start(bf16[3,8,32,128]{3,2,1,0:T(8,128)(2,1)} %saved_ref.3) | copy-start | bytes 589828
  13.9 9.8 %copy-start.3 = (f32[4,32,128]{2,1,0:T(8,128)S(1)}, f32[4,32,128]{2,1,0:T(8,128)}, u32[]{:S(2)}) copy-start(f32[4,32,128]{2,1,0:T(8,128)} %refs_5_.1) | copy-start | bytes 196612
  24.4 8.8 %copy-start.2 = (s32[3,8,128]{2,1,0:T(8,128)S(1)}, s32[3,8,128]{2,1,0:T(8,128)}, u32[]{:S(2)}) copy-start(s32[3,8,128]{2,1,0:T(8,128)} %mask_ref.3) | copy-start | bytes 36868
  52.5 10.0 %all-to-all-start.5 = ((bf16[16,32,128]{2,1,0:T(8,128)(2,1)}), bf16[16,32,128]{2,1,0:T(8,128)(2,1)S(1)}, u32[]{:S(2)}, u32[]{:S(2)}) async-start(bf16[16,32,128]{2,1,0:T(8,128)(2,1)} %get-tuple-element.33), calls=%async_computation.5 | async-start | bytes 262144 | tf_op jit(solution)/shard_map/all_to_all | solution.py:474
  56.8 1.3 %collective-permute-start.1 = (f32[5,32,128]{2,1,0:T(8,128)S(1)}, f32[5,32,128]{2,1,0:T(8,128)S(1)}, u32[]{:S(2)}, u32[]{:S(2)}) collective-permute-start(f32[5,32,128]{2,1,0:T(8,128)S(1)} %get-tuple-element.35.refs_8_), channel_id=1, source_target_pairs={{0,1},{1,0},{2,3},{3,2},{4,5},{5,4},{6,7},{7,6},{8,9},{9,8},{10,11... | collective-permute-start | bytes 245768 | tf_op jit(solution)/shard_map/ppermute | solution.py:485
  56.9 1.3 %collective-permute-start.2 = (f32[1,32,128]{2,1,0:T(8,128)S(1)}, f32[1,32,128]{2,1,0:T(8,128)S(1)}, u32[]{:S(2)}, u32[]{:S(2)}) collective-permute-start(f32[1,32,128]{2,1,0:T(8,128)S(1)} %get-tuple-element.36.refs_10_), channel_id=1, source_target_pairs={{0,1},{1,0},{2,3},{3,2},{4,5},{5,4},{6,7},{7,6},{8,9},{9,8},{10,11... | collective-permute-start | bytes 49160 | tf_op jit(solution)/shard_map/ppermute | solution.py:485

commit v8 on v7

--- a/solution.py
+++ b/solution.py
@@ -210,55 +210,100 @@
     )
 
 
-def dual_kernel(
-    layer,
+def dual_step(layer, pushed, cot_in, mask_ref, scale_ref, mix_ref, wanted_ref, cot_ref, send_ref):
+    above = layer + 1
+    tau = scale_ref[pl.ds(2 * above, 1), :]
+    mixed = mixed_by(mix_ref[2 * above], pushed)
+    base = []
+    for b in range(len(pushed)):
+        cot = mask_ref[layer, pl.ds(b, 1), :].astype(F32) * (cot_in[b] + tau * mixed[b])
+        cot_ref[b] = cot
+        base.append(cot)
+    choose_for_all(wanted_ref, base, send_ref)
+
+
+def all_pushed(wanted_ref, received_ref, pushed_ref):
+    owned, channels, side = pushed_ref.shape
+    pushed = sum_pushed(
+        wanted_ref, received_ref, [jnp.zeros((channels, side), F32) for _ in range(owned)]
+    )
+    for b in range(owned):
+        pushed_ref[b] = pushed[b]
+    return pushed
+
+
+def dual_kernel(layer, received_ref, *refs):
+    *refs, pushed_ref = refs
+    wanted_ref = refs[4]
+    dual_step(layer, all_pushed(wanted_ref, received_ref, pushed_ref), *refs)
+
+
+def last_layer_dual_kernel(pushed_ref, *refs):
+    dual_step(0, [pushed_ref[b] for b in range(pushed_ref.shape[0])], *refs)
+
+
+def doubled_halves(x):
+    high, rest = halves(x)
+    return jnp.concatenate([high, rest, high, rest], 0)
+
+
+def extrapolate(saved_ref, layer, p):
+    return (
+        2.0 * saved_ref[layer + 1, p].astype(F32) - saved_ref[layer, p].astype(F32)
+    ).astype(BF16)
+
+
+def terms_kernel(
     wanted_ref,
+    last_received_ref,
+    saved_dual_ref,
+    saved_primal_ref,
+    tiles_ref,
+    other_ref,
     received_ref,
-    cot_in,
-    mask_ref,
-    saved_ref,
-    scale_ref,
-    mix_ref,
     *refs,
 ):
-    owned, channels, side = cot_in.shape
-    tiles_refs, (cot_ref, send_ref, terms_ref) = refs[:-3], refs[-3:]
-    above = layer + 1
-    tau = scale_ref[pl.ds(2 * above, 1), :]
-    pushed = sum_pushed(
-        wanted_ref, received_ref, [jnp.zeros((channels, side), F32) for _ in range(owned)]
-    )
-    base, left, right = [], [], []
-    mixed = mixed_by(mix_ref[2 * above], pushed)
-    for b in range(owned):
-        block = cot_in[b] + tau * mixed[b]
-        cot = mask_ref[layer, pl.ds(b, 1), :].astype(F32) * block
-        cot_ref[b] = cot
-        base.append(cot)
-        high, rest = halves(pushed[b])
-        left.append(saved_ref[above, b])
-        right.append(jnp.concatenate([high, rest, high, rest], 0))
-    choose_for_all(wanted_ref, base, send_ref)
-    terms_ref[0] = folded(contract(left, right), channels)
-    if tiles_refs:
-        count = terms_ref.shape[0] - 1
-
-        def step(t, sums):
-            tile = pushed_tile(*tiles_refs, t)
-            product = jnp.dot(
-                received_ref[t, channels:, :], tile[:side], preferred_element_type=F32
-            )
-            at = place_of(tile, product.shape)
-            return tuple(s + jnp.where(at == p, product, 0.0) for p, s in enumerate(sums))
-
-        sums = tuple(jnp.zeros((channels, side), F32) for _ in range(count))
-        if received_ref.shape[0] <= 16:
-            for t in range(received_ref.shape[0]):
-                sums = step(t, sums)
-        else:
-            sums = lax.fori_loop(0, received_ref.shape[0], step, sums)
-        for p in range(count):
-            terms_ref[1 + p] = sums[p]
+    last_sums_ref, last_pushed_ref, part_ref, dual_ref = refs[-4:]
+    refs = (*refs[:-4], last_pushed_ref, last_sums_ref)
+    early, channels, side = dual_ref.shape
+    owned, blocks = saved_dual_ref.shape[1], saved_primal_ref.shape[1]
+    all_pushed(wanted_ref, last_received_ref, last_pushed_ref)
+    for i in range(early):
+        pushed_ref, sums_ref = refs[2 * i], refs[2 * i + 1]
+        layer = early - i
+        part_ref[layer - 1] = folded(
+            contract(
+                [saved_dual_ref[layer, b] for b in range(owned)],
+                [doubled_halves(pushed_ref[b]) for b in range(owned)],
+            ),
+            channels,
+        )
+        dual_ref[layer - 1] = folded(
+            contract(
+                [extrapolate(saved_primal_ref, layer, p) for p in range(blocks)],
+                [doubled_halves(sums_ref[p]) for p in range(blocks)],
+            ),
+            channels,
+        )
+
+    def step(t, sums):
+        tile = pushed_tile(tiles_ref, other_ref, t)
+        product = jnp.dot(
+            received_ref[t, channels:, :], tile[:side], preferred_element_type=F32
+        )
+        at = place_of(tile, product.shape)
+        return tuple(s + jnp.where(at == p, product, 0.0) for p, s in enumerate(sums))
+
+    sums = tuple(jnp.zeros((channels, side), F32) for _ in range(blocks))
+    if received_ref.shape[0] <= 16:
+        for t in range(received_ref.shape[0]):
+            sums = step(t, sums)
+    else:
+        sums = lax.fori_loop(0, received_ref.shape[0], step, sums)
+    for p in range(blocks):
+        part_ref[early + p] = sums[p]
+    for i in range(early + blocks, part_ref.shape[0]):
+        part_ref[i] = jnp.zeros((channels, side), F32)
 
 
 def last_dual_kernel(
@@ -309,7 +354,7 @@
 
 
 def primal_step(layer, shared, grad_ref):
-    tiles_ref, other_ref, scale_ref, mix_ref, fetched_ref, grad_in, mask_ref, saved_ref = shared
+    tiles_ref, other_ref, scale_ref, mix_ref, fetched_ref, grad_in, mask_ref = shared
     blocks, channels, side = grad_ref.shape
     rows = tiles_ref.shape[0]
     me = lax.axis_index("col")
@@ -330,19 +375,14 @@
             sums = step(t, sums)
     else:
         sums = lax.fori_loop(0, rows, step, sums)
-    cots, extrapolated = [], []
+    cots = []
     mixed = mixed_by(mix_ref[2 * layer + 1], sums)
     for p in range(blocks):
         back = sigma * mixed[p]
         cot = mask_ref[layer, pl.ds(p, 1), :].astype(F32) * (grad_in[p] + 2.0 * back)
         grad_ref[p] = cot - back
         cots.append(cot)
-        extrapolated.append(
-            (
-                2.0 * saved_ref[layer + 1, p].astype(F32) - saved_ref[layer, p].astype(F32)
-            ).astype(BF16)
-        )
-    return sums, cots, extrapolated
+    return sums, cots
 
 
 def push(tiles_ref, other_ref, blocks, send_ref, below):
@@ -368,34 +408,31 @@
 
 
 def primal_kernel(layer, *refs):
-    shared, rest, (grad_ref, send_ref, terms_ref) = refs[:8], refs[8:-3], refs[-3:]
-    blocks, channels, side = grad_ref.shape
-    sums, cots, extrapolated = primal_step(layer, shared, grad_ref)
+    shared, rest, (grad_ref, send_ref, sums_ref) = refs[:7], refs[7:-3], refs[-3:]
+    sums, cots = primal_step(layer, shared, grad_ref)
     below = None
     if rest:
         wanted_ref, dual_ref = rest
         base = [dual_ref[0, b].astype(F32) for b in range(dual_ref.shape[1])]
         below = lambda t: chosen(wanted_ref, t, base)
     push(*shared[:2], cots, send_ref, below)
-    right = []
-    for p in range(blocks):
-        high, low = halves(sums[p])
-        right.append(jnp.concatenate([high, low, high, low], 0))
-    terms_ref[...] = folded(contract(extrapolated, right), channels)
+    for p, total in enumerate(sums):
+        sums_ref[p] = total
 
 
 def last_primal_kernel(*refs):
-    shared, rest, (grad_ref, send_ref) = refs[:8], refs[8:-2], refs[-2:]
-    early_ref, early_other, late_ref, late_other, *dual_terms = rest
+    shared, rest, (grad_ref, send_ref) = refs[:7], refs[7:-2], refs[-2:]
+    saved_ref, part_ref, part_other, dual_ref = rest
     scale_ref, mix_ref = shared[2], shared[3]
     blocks, channels, side = grad_ref.shape
+    early = dual_ref.shape[0]
     half = channels // 2
-    sums, cots, extrapolated = primal_step(0, shared, grad_ref)
+    sums, cots = primal_step(0, shared, grad_ref)
     tau = scale_ref[pl.ds(0, 1), :]
     left, right = [], []
     for p in range(blocks):
-        pulled = early_ref[1 + p] + early_other[1 + p]
-        left.append(jnp.concatenate([extrapolated[p], *halves(pulled)], 0))
+        pulled = part_ref[early + p] + part_other[early + p]
+        left.append(jnp.concatenate([extrapolate(saved_ref, 0, p), *halves(pulled)], 0))
         right.append(jnp.concatenate([*halves(sums[p]), *halves(cots[p])], 0))
     terms = contract(left, right)
     lane = lax.broadcasted_iota(jnp.int32, (channels, side), 1)
@@ -403,9 +440,8 @@
     terms = jnp.where(
         low, terms[:channels], terms[channels : 2 * channels] + terms[2 * channels :]
     )
-    primal_terms = (late_ref[0] + late_other[0], early_ref[0] + early_other[0])
     all_terms = [folded(terms, channels)] + [
-        jnp.where(low, dual[...], primal) for dual, primal in zip(dual_terms, primal_terms)
+        jnp.where(low, dual_ref[i], part_ref[i] + part_other[i]) for i in range(early)
     ]
     packed = jnp.concatenate(
         [
@@ -527,61 +563,70 @@
     blocks_out = shape((col_count * row_count, channels, side), BF16)
     grad_x = cot_primal
     send = call(first_dual_kernel, blocks_out, wanted, cot)
-    dual_terms, primal_terms = [], []
+    carried = []
+    first_received = None
+    spread = 16
     for layer in reversed(range(layer_count)):
         fetched = exchange(send, ("row", "col"), [order_all])
-        shared = (
-            tiles,
-            other_tiles,
-            scale,
-            mix,
-            fetched,
-            grad_x,
-            primal_active,
-            saved_primal,
-        )
+        shared = (tiles, other_tiles, scale, mix, fetched, grad_x, primal_active)
         if layer == 0:
             height = channels + layer_count * half
             grad_x, pushed = call(
                 last_primal_kernel,
                 (shape(cot_primal.shape), shape((row_count, height, side), BF16)),
                 *shared,
-                *primal_terms,
-                *dual_terms[::-1],
+                saved_primal,
+                part,
+                part_other,
+                dual_terms,
             )
             received = exchange(pushed, ("row", "col"), order_push)
             break
         first = layer == layer_count - 1
         height = 2 * channels if first else channels
-        grad_x, pushed, terms = call(
+        grad_x, pushed, sums = call(
             partial(primal_kernel, layer),
             (
                 shape(cot_primal.shape),
                 shape((row_count, height, side), BF16),
-                shape((channels, side)),
+                shape(cot_primal.shape),
             ),
             *shared,
             *((wanted, saved_dual) if first else ()),
         )
-        dual_terms.append(terms)
         received = exchange(pushed, ("row", "col"), order_push)
-        cot, send, terms = call(
-            partial(dual_kernel, layer - 1),
+        if first:
+            first_received = received
+        state = (cot, dual_active, scale, mix, wanted)
+        dual_shape = shape(cot_dual.shape)
+        if layer > 1:
+            cot, send, sums_pushed = call(
+                partial(dual_kernel, layer - 1),
+                (dual_shape, blocks_out, dual_shape),
+                received,
+                *state,
+            )
+            carried += [sums_pushed, sums]
+            continue
+        sums_pushed, part, dual_terms = call(
+            terms_kernel,
             (
-                shape(cot_dual.shape),
-                blocks_out,
-                shape((1 + (primal_count if first else 0), channels, side)),
+                dual_shape,
+                shape((max(spread, layer_count - 1 + primal_count), channels, side)),
+                shape((layer_count - 1, channels, side)),
             ),
             wanted,
             received,
-            cot,
-            dual_active,
             saved_dual,
-            scale,
-            mix,
-            *((tiles, other_tiles) if first else ()),
-        )
-        primal_terms += [terms, swap(terms)]
+            saved_primal,
+            tiles,
+            other_tiles,
+            first_received,
+            *carried,
+            sums,
+        )
+        part_other = swap(part)
+        cot, send = call(last_layer_dual_kernel, (dual_shape, blocks_out), sums_pushed, *state)
     grad_x, grad_y, primal_mix_grad, dual_mix_grad = call(
         partial(last_dual_kernel, row_scale, col_scale),
         (

time: 73.7 us -> 72.8 us (0.988)
  blocking collectives: 44.8 us -> 54.3 us
  waiting for transfers between devices: 7.83 us -> 2.76 us
  starting transfers between devices: 12.7 us -> 8.14 us
    all_to_all x5 -> x6, blocking collectives: 44.8 us -> 54.3 us  [exchange(): lax.all_to_all(x, axes, split_axis=0, concat_axis=0, axis_index_groups=gr...]
    all_to_all x2 -> x1, starting transfers between devices: 12.2 us -> 7.83 us  [exchange(): lax.all_to_all(x, axes, split_axis=0, concat_axis=0, axis_index_groups=gr...]
    all_to_all x2 -> x1, waiting for transfers between devices: 6.99 us -> 2.76 us  [exchange(): lax.all_to_all(x, axes, split_axis=0, concat_axis=0, axis_index_groups=gr...]
    ppermute x3 -> x2, waiting for transfers between devices: 0.84 us -> 0.01 us  [swap(): lax.ppermute(x, 'col', [(i, col_count - 1 - i) for i in range(col_count)])]
    pallas_call x9 -> x10, Pallas kernels: 7.07 us -> 6.42 us  [call(): pl.pallas_call(kernel, out_shape=outs, in_specs=ins or [VMEM] * len(opera...]
  transfers between devices with their start and end apart: 5 -> 3, of which waited for: 4 -> 1; matrix products, arithmetic and copies ran while one was open for 0% -> 0% of each run, Pallas kernels for 2% -> 2%
where the time goes in v8:
time: 72.8 us; the launch traced here: 72.4 us
  blocking collectives  54.3 us (75%)
  starting transfers between devices  8.14 us (11%)
  Pallas kernels  6.42 us (9%)
  waiting for transfers between devices  2.76 us (4%)
    all_to_all x6, blocking collectives, exchange(): lax.all_to_all(x, axes, split_axis=0, concat_axis=0, axis_index_groups=gr...  54.3 us
    all_to_all x1, starting transfers between devices, exchange(): lax.all_to_all(x, axes, split_axis=0, concat_axis=0, axis_index_groups=gr...  7.83 us
    pallas_call x10, Pallas kernels, call(): pl.pallas_call(kernel, out_shape=outs, in_specs=ins or [VMEM] * len(opera...  6.42 us
    all_to_all x1, waiting for transfers between devices, exchange(): lax.all_to_all(x, axes, split_axis=0, concat_axis=0, axis_index_groups=gr...  2.76 us
  transfers between devices with their start and end apart: 3, of which 1 were waited for; matrix products, arithmetic and copies ran while one was open for 0% of the time, Pallas kernels for 2%

profile of v8, /device:TPU:0, one launch (start us, length us, event | category | flops | bytes accessed | tf_op | source)
XLA Modules:
  0.0 72.4 jit_solution(1698397327420794786)
XLA Ops:
  0.6 1.3 %shard_map.147 = f32[8,1,128]{2,1,0:T(1,128)} custom-call(s32[8]{0:T(128)} %rows_in.3), custom_call_target="tpu_custom_call" | custom-call | tf_op jit(solution)/shard_map/pallas_call | solution.py:488
  1.9 7.8 %all-to-all-start = ((f32[8,1,128]{2,1,0:T(1,128)}), f32[8,1,128]{2,1,0:T(1,128)S(1)}, u32[]{:S(2)}, u32[]{:S(2)}) async-start(f32[8,1,128]{2,1,0:T(1,128)} %shard_map.147), calls=%async_computation | async-start | bytes 8192 | tf_op jit(solution)/shard_map/all_to_all | solution.py:510
  9.8 1.3 %shard_map.148 = (bf16[8,144,128]{2,1,0:T(8,128)(2,1)S(1)}, f32[6,128]{1,0:T(8,128)S(1)}, bf16[6,32,128]{2,1,0:T(8,128)(2,1)S(1)}, f32[8,32,128]{2,1,0:T(8,128)S(1)}) custom-call(s32[8]{0:T(128)} %rows_in.3, s32[8]{0:T(128)} %cols_in.1, s32[3,4]{1,0:T(4,128)} %steps_in.1, bf16[8,128,128]{2,1,0:T(8,128)(2,1)} %tiles_in.1, f32[8,32,128]{2,1,0:T(8,128)} %cot_in.1, ...), custom_call_target="tpu_custom_call" | custom-call | tf_op jit(solution)/shard_map/pallas_call | solution.py:488
  11.0 2.8 %all-to-all-done.wanted_ref.refs_7_.refs_4_ = f32[8,1,128]{2,1,0:T(1,128)S(1)} async-done(((f32[8,1,128]{2,1,0:T(1,128)}), f32[8,1,128]{2,1,0:T(1,128)S(1)}, u32[]{:S(2)}, u32[]{:S(2)}) %all-to-all-start) | async-done | bytes 4128 | tf_op jit(solution)/shard_map/all_to_all | solution.py:510
  13.8 0.0 collective-permute-start
  13.9 0.0 copy-start
  13.9 0.0 copy-start.3
  13.9 9.8 %all_to_all.35.refs_4_ = bf16[16,32,128]{2,1,0:T(8,128)(2,1)S(1)} all-to-all(bf16[16,32,128]{2,1,0:T(8,128)(2,1)S(1)} %shard_map.149), channel_id=1, replica_groups={{9,8,11,10,13,12,15,14,1,0,3,2,5,4,7,6},{25,24,27,26,29,28,31,30,17,16,..., dimensions={0} | all-to-all | bytes 262144 | tf_op jit(solution)/shard_map/all_to_all | solution.py:510
  23.6 0.0 collective-permute-done.refs_1_.other_ref
  23.6 0.0 copy-done
  23.7 0.6 shard_map.150
  24.3 8.8 %all_to_all.36.received_ref = bf16[8,64,128]{2,1,0:T(8,128)(2,1)S(1)} all-to-all(bf16[8,64,128]{2,1,0:T(8,128)(2,1)S(1)} %get-tuple-element.30), channel_id=1, replica_groups={{8,10,12,14,1,3,5,7},{9,11,13,15,0,2,4,6},{24,26,28,30,17,19,21,23},{25..., dimensions={0} | all-to-all | bytes 262144 | tf_op jit(solution)/shard_map/all_to_all | solution.py:510
  33.1 0.3 shard_map.151
  33.4 9.4 %all_to_all.37.refs_4_ = bf16[16,32,128]{2,1,0:T(8,128)(2,1)S(1)} all-to-all(bf16[16,32,128]{2,1,0:T(8,128)(2,1)S(1)} %get-tuple-element.31), channel_id=1, replica_groups={{9,8,11,10,13,12,15,14,1,0,3,2,5,4,7,6},{25,24,27,26,29,28,31,30,17,16,..., dimensions={0} | all-to-all | bytes 262144 | tf_op jit(solution)/shard_map/all_to_all | solution.py:510
  42.7 0.6 shard_map.152
  43.3 7.9 %all_to_all.38.last_received_ref = bf16[8,32,128]{2,1,0:T(8,128)(2,1)S(1)} all-to-all(bf16[8,32,128]{2,1,0:T(8,128)(2,1)S(1)} %get-tuple-element.33), channel_id=1, replica_groups={{8,10,12,14,1,3,5,7},{9,11,13,15,0,2,4,6},{24,26,28,30,17,19,21,23},{25..., dimensions={0} | all-to-all | bytes 131072 | tf_op jit(solution)/shard_map/all_to_all | solution.py:510
  51.3 0.5 shard_map.153
  51.7 0.3 collective-permute-start.1
  52.0 0.2 shard_map.154
  52.3 9.4 %all_to_all.39.refs_4_ = bf16[16,32,128]{2,1,0:T(8,128)(2,1)S(1)} all-to-all(bf16[16,32,128]{2,1,0:T(8,128)(2,1)S(1)} %get-tuple-element.39), channel_id=1, replica_groups={{9,8,11,10,13,12,15,14,1,0,3,2,5,4,7,6},{25,24,27,26,29,28,31,30,17,16,..., dimensions={0} | all-to-all | bytes 262144 | tf_op jit(solution)/shard_map/all_to_all | solution.py:510
  61.6 0.0 collective-permute-done.1.refs_9_
  61.6 0.8 %shard_map.155 = (f32[4,32,128]{2,1,0:T(8,128)S(1)}, bf16[8,80,128]{2,1,0:T(8,128)(2,1)S(1)}) custom-call(bf16[8,144,128]{2,1,0:T(8,128)(2,1)S(1)} %get-tuple-element.26.refs_0_.tiles_ref, bf16[8,144,128]{2,1,0:T(8,128)(2,1)S(1)} %collective-permute-done.refs_1_.other_ref, f32[6,128]{1,0:T(8,128)S(1)} %get-tuple-element.27.refs_2_.scale_ref, ...), custom_call_target="tpu_custom_call" | custom-call | tf_op jit(solution)/shard_map/pallas_call | solution.py:488
  62.4 9.1 %all_to_all.40.received_ref = bf16[8,80,128]{2,1,0:T(8,128)(2,1)S(1)} all-to-all(bf16[8,80,128]{2,1,0:T(8,128)(2,1)S(1)} %get-tuple-element.43), channel_id=1, replica_groups={{8,10,12,14,1,3,5,7},{9,11,13,15,0,2,4,6},{24,26,28,30,17,19,21,23},{25..., dimensions={0} | all-to-all | bytes 327680 | tf_op jit(solution)/shard_map/all_to_all | solution.py:510
  71.5 0.8 %shard_map.156 = (f32[4,32,128]{2,1,0:T(8,128)}, f32[8,32,128]{2,1,0:T(8,128)}, f32[3,32,32]{2,1,0:T(8,128)}, f32[3,32,32]{2,1,0:T(8,128)}) custom-call(f32[8,1,128]{2,1,0:T(1,128)S(1)} %all-to-all-done.wanted_ref.refs_7_.refs_4_, bf16[8,80,128]{2,1,0:T(8,128)(2,1)S(1)} %all_to_all.40.received_ref, f32[8,32,128]{2,1,0:T(8,128)S(1)} %get-tuple-element.44.cot_in, ...), custom_call_target="tpu_custom_call" | custom-call | tf_op jit(solution)/shard_map/pallas_call | solution.py:488
  (8 shorter events, 0.1 us)
Async XLA Ops:
  1.9 11.9 %all-to-all-start = ((f32[8,1,128]{2,1,0:T(1,128)}), f32[8,1,128]{2,1,0:T(1,128)S(1)}, u32[]{:S(2)}, u32[]{:S(2)}) async-start(f32[8,1,128]{2,1,0:T(1,128)} %shard_map.147), calls=%async_computation | async-start | bytes 8192 | tf_op jit(solution)/shard_map/all_to_all | solution.py:510
  13.8 9.8 %collective-permute-start = (bf16[8,144,128]{2,1,0:T(8,128)(2,1)S(1)}, bf16[8,144,128]{2,1,0:T(8,128)(2,1)S(1)}, u32[]{:S(2)}, u32[]{:S(2)}) collective-permute-start(bf16[8,144,128]{2,1,0:T(8,128)(2,1)S(1)} %get-tuple-element.26.refs_0_.tiles_ref), channel_id=1, source_target_pairs={{0,1},{1,0},{2,3},{3,2},{4,5},{5,4},{6,7},{7,6},{8,9},{9,8},{10,11... | collective-permute-start | bytes 884744 | tf_op jit(solution)/shard_map/ppermute | solution.py:521
  13.8 9.8 %copy-start.4 = (s32[3,4,128]{2,1,0:T(4,128)S(1)}, s32[3,4,128]{2,1,0:T(4,128)}, u32[]{:S(2)}) copy-start(s32[3,4,128]{2,1,0:T(4,128)} %refs_6_.5) | copy-start | bytes 18436
  13.9 9.8 %copy-start = (bf16[3,8,32,128]{3,2,1,0:T(8,128)(2,1)S(1)}, bf16[3,8,32,128]{3,2,1,0:T(8,128)(2,1)}, u32[]{:S(2)}) copy-start(bf16[3,8,32,128]{3,2,1,0:T(8,128)(2,1)} %saved_dual_ref.1) | copy-start | bytes 589828
  13.9 9.8 %copy-start.3 = (f32[4,32,128]{2,1,0:T(8,128)S(1)}, f32[4,32,128]{2,1,0:T(8,128)}, u32[]{:S(2)}) copy-start(f32[4,32,128]{2,1,0:T(8,128)} %refs_5_.1) | copy-start | bytes 196612
  24.3 8.8 %copy-start.2 = (s32[3,8,128]{2,1,0:T(8,128)S(1)}, s32[3,8,128]{2,1,0:T(8,128)}, u32[]{:S(2)}) copy-start(s32[3,8,128]{2,1,0:T(8,128)} %refs_1_.3) | copy-start | bytes 36868
  43.3 7.9 %copy-start.1 = (bf16[4,4,32,128]{3,2,1,0:T(8,128)(2,1)S(1)}, bf16[4,4,32,128]{3,2,1,0:T(8,128)(2,1)}, u32[]{:S(2)}) copy-start(bf16[4,4,32,128]{3,2,1,0:T(8,128)(2,1)} %refs_7_.1) | copy-start | bytes 393220
  51.7 9.9 %collective-permute-start.1 = (f32[16,32,128]{2,1,0:T(8,128)S(1)}, f32[16,32,128]{2,1,0:T(8,128)S(1)}, u32[]{:S(2)}, u32[]{:S(2)}) collective-permute-start(f32[16,32,128]{2,1,0:T(8,128)S(1)} %get-tuple-element.41.refs_8_), channel_id=1, source_target_pairs={{0,1},{1,0},{2,3},{3,2},{4,5},{5,4},{6,7},{7,6},{8,9},{9,8},{10,11... | collective-permute-start | bytes 786440 | tf_op jit(solution)/shard_map/ppermute | solution.py:521

commit v9 on v8

--- a/solution.py
+++ b/solution.py
@@ -38,6 +38,15 @@
 
 def slot_of(row, peer_size, shift, row_count):
     return lax.rem(lax.div(row, peer_size) + shift, row_count)
+
+
+def spot_of(order, order_all, col_count, slot, col):
+    if not isinstance(slot, int):
+        return slot * col_count + col_count - 1 - col
+    spots = [order_all.index(order[slot] * col_count + c) for c in range(col_count)]
+    if isinstance(col, int):
+        return spots[col]
+    return sum(jnp.where(col == c, spot, 0) for c, spot in enumerate(spots))
 
 
 def ask_kernel(slot, owned, rows_in, asked_ref, rows_ref, sem):
@@ -143,19 +152,19 @@
     return picked.astype(BF16)
 
 
-def choose_for_all(wanted_ref, base, send_ref):
+def choose_for_all(spot, wanted_ref, base, send_ref):
     cols = send_ref.shape[0] // wanted_ref.shape[0]
 
     def one(r):
         picked = chosen(wanted_ref, r, base)
         for c in range(cols):
-            send_ref[r * cols + c] = picked
+            send_ref[spot(r, c)] = picked
 
     loop(wanted_ref.shape[0], one)
 
 
-def first_dual_kernel(wanted_ref, cot_ref, send_ref):
-    choose_for_all(wanted_ref, [cot_ref[b] for b in range(cot_ref.shape[0])], send_ref)
+def first_dual_kernel(spot, wanted_ref, cot_ref, send_ref):
+    choose_for_all(spot, wanted_ref, [cot_ref[b] for b in range(cot_ref.shape[0])], send_ref)
 
 
 def sum_pushed(wanted_ref, received_ref, start):
@@ -210,7 +219,9 @@
     )
 
 
-def dual_step(layer, pushed, cot_in, mask_ref, scale_ref, mix_ref, wanted_ref, cot_ref, send_ref):
+def dual_step(
+    spot, layer, pushed, cot_in, mask_ref, scale_ref, mix_ref, wanted_ref, cot_ref, send_ref
+):
     above = layer + 1
     tau = scale_ref[pl.ds(2 * above, 1), :]
     mixed = mixed_by(mix_ref[2 * above], pushed)
@@ -219,7 +230,7 @@
         cot = mask_ref[layer, pl.ds(b, 1), :].astype(F32) * (cot_in[b] + tau * mixed[b])
         cot_ref[b] = cot
         base.append(cot)
-    choose_for_all(wanted_ref, base, send_ref)
+    choose_for_all(spot, wanted_ref, base, send_ref)
 
 
 def all_pushed(wanted_ref, received_ref, pushed_ref):
@@ -232,14 +243,14 @@
     return pushed
 
 
-def dual_kernel(layer, received_ref, *refs):
+def dual_kernel(spot, layer, received_ref, *refs):
     *refs, pushed_ref = refs
     wanted_ref = refs[4]
-    dual_step(layer, all_pushed(wanted_ref, received_ref, pushed_ref), *refs)
-
-
-def last_layer_dual_kernel(pushed_ref, *refs):
-    dual_step(0, [pushed_ref[b] for b in range(pushed_ref.shape[0])], *refs)
+    dual_step(spot, layer, all_pushed(wanted_ref, received_ref, pushed_ref), *refs)
+
+
+def last_layer_dual_kernel(spot, pushed_ref, *refs):
+    dual_step(spot, 0, [pushed_ref[b] for b in range(pushed_ref.shape[0])], *refs)
 
 
 def doubled_halves(x):
@@ -353,7 +364,7 @@
         copy.wait()
 
 
-def primal_step(layer, shared, grad_ref):
+def primal_step(spot, layer, shared, grad_ref):
     tiles_ref, other_ref, scale_ref, mix_ref, fetched_ref, grad_in, mask_ref = shared
     blocks, channels, side = grad_ref.shape
     rows = tiles_ref.shape[0]
@@ -361,7 +372,7 @@
     sigma = scale_ref[pl.ds(2 * layer + 1, 1), :]
 
     def step(t, sums):
-        for tiles, message in ((tiles_ref, 2 * t + 1 - me), (other_ref, 2 * t + me)):
+        for tiles, message in ((tiles_ref, spot(t, me)), (other_ref, spot(t, 1 - me))):
             product = jnp.dot(
                 fetched_ref[message], tiles[t, :side, :], preferred_element_type=F32
             )
@@ -407,9 +418,9 @@
     loop(tiles_ref.shape[0], one)
 
 
-def primal_kernel(layer, *refs):
+def primal_kernel(spot, layer, *refs):
     shared, rest, (grad_ref, send_ref, sums_ref) = refs[:7], refs[7:-3], refs[-3:]
-    sums, cots = primal_step(layer, shared, grad_ref)
+    sums, cots = primal_step(spot, layer, shared, grad_ref)
     below = None
     if rest:
         wanted_ref, dual_ref = rest
@@ -420,14 +431,14 @@
         sums_ref[p] = total
 
 
-def last_primal_kernel(*refs):
+def last_primal_kernel(spot, *refs):
     shared, rest, (grad_ref, send_ref) = refs[:7], refs[7:-2], refs[-2:]
     saved_ref, part_ref, part_other, dual_ref = rest
     scale_ref, mix_ref = shared[2], shared[3]
     blocks, channels, side = grad_ref.shape
     early = dual_ref.shape[0]
     half = channels // 2
-    sums, cots = primal_step(0, shared, grad_ref)
+    sums, cots = primal_step(spot, 0, shared, grad_ref)
     tau = scale_ref[pl.ds(0, 1), :]
     left, right = [], []
     for p in range(blocks):
@@ -497,6 +508,9 @@
     shift = row_count - row_count // 2
     order = [(slot + row_count - shift) % row_count for slot in range(row_count)]
     order_all = [row * col_count + c for row in order for c in reversed(range(col_count))]
+    if (row_count, col_count) == (8, 2):
+        order_all = [9, 3, 4, 8, 13, 7, 1, 14, 12, 5, 15, 0, 11, 6, 10, 2]
+    spot = partial(spot_of, order, order_all, col_count)
 
     order_push = [
         [
@@ -562,7 +576,7 @@
     other_tiles = swap(lax.optimization_barrier((tiles, wanted))[0])
     blocks_out = shape((col_count * row_count, channels, side), BF16)
     grad_x = cot_primal
-    send = call(first_dual_kernel, blocks_out, wanted, cot)
+    send = call(partial(first_dual_kernel, spot), blocks_out, wanted, cot)
     carried = []
     first_received = None
     spread = 16
@@ -572,7 +586,7 @@
         if layer == 0:
             height = channels + layer_count * half
             grad_x, pushed = call(
-                last_primal_kernel,
+                partial(last_primal_kernel, spot),
                 (shape(cot_primal.shape), shape((row_count, height, side), BF16)),
                 *shared,
                 saved_primal,
@@ -585,7 +599,7 @@
         first = layer == layer_count - 1
         height = 2 * channels if first else channels
         grad_x, pushed, sums = call(
-            partial(primal_kernel, layer),
+            partial(primal_kernel, spot, layer),
             (
                 shape(cot_primal.shape),
                 shape((row_count, height, side), BF16),
@@ -601,7 +615,7 @@
         dual_shape = shape(cot_dual.shape)
         if layer > 1:
             cot, send, sums_pushed = call(
-                partial(dual_kernel, layer - 1),
+                partial(dual_kernel, spot, layer - 1),
                 (dual_shape, blocks_out, dual_shape),
                 received,
                 *state,
@@ -626,7 +640,9 @@
             sums,
         )
         part_other = swap(part)
-        cot, send = call(last_layer_dual_kernel, (dual_shape, blocks_out), sums_pushed, *state)
+        cot, send = call(
+            partial(last_layer_dual_kernel, spot), (dual_shape, blocks_out), sums_pushed, *state
+        )
     grad_x, grad_y, primal_mix_grad, dual_mix_grad = call(
         partial(last_dual_kernel, row_scale, col_scale),
         (

time: 72.8 us -> 72.3 us (level)
  blocking collectives: 54.3 us -> 52.9 us
    all_to_all x6, blocking collectives: 54.3 us -> 52.9 us  [exchange(): lax.all_to_all(x, axes, split_axis=0, concat_axis=0, axis_index_groups=gr...]
where the time goes in v9:
time: 72.3 us; the launch traced here: 71.4 us
  blocking collectives  52.9 us (73%)
  starting transfers between devices  8.56 us (12%)
  Pallas kernels  6.42 us (9%)
  waiting for transfers between devices  2.76 us (4%)
    all_to_all x6, blocking collectives, exchange(): lax.all_to_all(x, axes, split_axis=0, concat_axis=0, axis_index_groups=gr...  52.9 us
    all_to_all x1, starting transfers between devices, exchange(): lax.all_to_all(x, axes, split_axis=0, concat_axis=0, axis_index_groups=gr...  7.83 us
    pallas_call x10, Pallas kernels, call(): pl.pallas_call(kernel, out_shape=outs, in_specs=ins or [VMEM] * len(opera...  6.42 us
    all_to_all x1, waiting for transfers between devices, exchange(): lax.all_to_all(x, axes, split_axis=0, concat_axis=0, axis_index_groups=gr...  2.76 us
  transfers between devices with their start and end apart: 3, of which 1 were waited for; matrix products, arithmetic and copies ran while one was open for 0% of the time, Pallas kernels for 2%

profile of v9, /device:TPU:0, one launch (start us, length us, event | category | flops | bytes accessed | tf_op | source)
XLA Modules:
  0.0 71.4 jit_solution(6667287402636752182)
XLA Ops:
  0.6 1.3 %shard_map.147 = f32[8,1,128]{2,1,0:T(1,128)} custom-call(s32[8]{0:T(128)} %rows_in.3), custom_call_target="tpu_custom_call" | custom-call | tf_op jit(solution)/shard_map/pallas_call | solution.py:499
  1.9 7.8 %all-to-all-start = ((f32[8,1,128]{2,1,0:T(1,128)}), f32[8,1,128]{2,1,0:T(1,128)S(1)}, u32[]{:S(2)}, u32[]{:S(2)}) async-start(f32[8,1,128]{2,1,0:T(1,128)} %shard_map.147), calls=%async_computation | async-start | bytes 8192 | tf_op jit(solution)/shard_map/all_to_all | solution.py:524
  9.8 1.3 %shard_map.148 = (bf16[8,144,128]{2,1,0:T(8,128)(2,1)S(1)}, f32[6,128]{1,0:T(8,128)S(1)}, bf16[6,32,128]{2,1,0:T(8,128)(2,1)S(1)}, f32[8,32,128]{2,1,0:T(8,128)S(1)}) custom-call(s32[8]{0:T(128)} %rows_in.3, s32[8]{0:T(128)} %cols_in.1, s32[3,4]{1,0:T(4,128)} %steps_in.1, bf16[8,128,128]{2,1,0:T(8,128)(2,1)} %tiles_in.1, f32[8,32,128]{2,1,0:T(8,128)} %cot_in.1, ...), custom_call_target="tpu_custom_call" | custom-call | tf_op jit(solution)/shard_map/pallas_call | solution.py:499
  11.0 2.8 %all-to-all-done.wanted_ref.refs_7_.refs_4_ = f32[8,1,128]{2,1,0:T(1,128)S(1)} async-done(((f32[8,1,128]{2,1,0:T(1,128)}), f32[8,1,128]{2,1,0:T(1,128)S(1)}, u32[]{:S(2)}, u32[]{:S(2)}) %all-to-all-start) | async-done | bytes 4128 | tf_op jit(solution)/shard_map/all_to_all | solution.py:524
  13.8 0.0 collective-permute-start
  13.9 0.0 copy-start
  13.9 0.0 copy-start.3
  13.9 9.3 %all_to_all.35.refs_4_ = bf16[16,32,128]{2,1,0:T(8,128)(2,1)S(1)} all-to-all(bf16[16,32,128]{2,1,0:T(8,128)(2,1)S(1)} %shard_map.149), channel_id=1, replica_groups={{9,3,4,8,13,7,1,14,12,5,15,0,11,6,10,2},{25,19,20,24,29,23,17,30,28,21,..., dimensions={0} | all-to-all | bytes 262144 | tf_op jit(solution)/shard_map/all_to_all | solution.py:524
  23.1 0.0 collective-permute-done.refs_1_.other_ref
  23.1 0.0 copy-done.4
  23.2 0.6 shard_map.150
  23.8 8.6 %all_to_all.36.received_ref = bf16[8,64,128]{2,1,0:T(8,128)(2,1)S(1)} all-to-all(bf16[8,64,128]{2,1,0:T(8,128)(2,1)S(1)} %get-tuple-element.30), channel_id=1, replica_groups={{8,10,12,14,1,3,5,7},{9,11,13,15,0,2,4,6},{24,26,28,30,17,19,21,23},{25..., dimensions={0} | all-to-all | bytes 262144 | tf_op jit(solution)/shard_map/all_to_all | solution.py:524
  32.3 0.3 shard_map.151
  32.6 9.3 %all_to_all.37.refs_4_ = bf16[16,32,128]{2,1,0:T(8,128)(2,1)S(1)} all-to-all(bf16[16,32,128]{2,1,0:T(8,128)(2,1)S(1)} %get-tuple-element.31), channel_id=1, replica_groups={{9,3,4,8,13,7,1,14,12,5,15,0,11,6,10,2},{25,19,20,24,29,23,17,30,28,21,..., dimensions={0} | all-to-all | bytes 262144 | tf_op jit(solution)/shard_map/all_to_all | solution.py:524
  41.9 0.6 shard_map.152
  42.5 8.1 %all_to_all.38.last_received_ref = bf16[8,32,128]{2,1,0:T(8,128)(2,1)S(1)} all-to-all(bf16[8,32,128]{2,1,0:T(8,128)(2,1)S(1)} %get-tuple-element.33), channel_id=1, replica_groups={{8,10,12,14,1,3,5,7},{9,11,13,15,0,2,4,6},{24,26,28,30,17,19,21,23},{25..., dimensions={0} | all-to-all | bytes 131072 | tf_op jit(solution)/shard_map/all_to_all | solution.py:524
  50.6 0.5 shard_map.153
  51.1 0.7 %collective-permute-start.1 = (f32[16,32,128]{2,1,0:T(8,128)S(1)}, f32[16,32,128]{2,1,0:T(8,128)S(1)}, u32[]{:S(2)}, u32[]{:S(2)}) collective-permute-start(f32[16,32,128]{2,1,0:T(8,128)S(1)} %get-tuple-element.41.refs_8_), channel_id=1, source_target_pairs={{0,1},{1,0},{2,3},{3,2},{4,5},{5,4},{6,7},{7,6},{8,9},{9,8},{10,11... | collective-permute-start | bytes 786440 | tf_op jit(solution)/shard_map/ppermute | solution.py:535
  51.8 0.2 shard_map.154
  52.0 8.8 %all_to_all.39.refs_4_ = bf16[16,32,128]{2,1,0:T(8,128)(2,1)S(1)} all-to-all(bf16[16,32,128]{2,1,0:T(8,128)(2,1)S(1)} %get-tuple-element.39), channel_id=1, replica_groups={{9,3,4,8,13,7,1,14,12,5,15,0,11,6,10,2},{25,19,20,24,29,23,17,30,28,21,..., dimensions={0} | all-to-all | bytes 262144 | tf_op jit(solution)/shard_map/all_to_all | solution.py:524
  60.9 0.0 collective-permute-done.1.refs_9_
  60.9 0.8 %shard_map.155 = (f32[4,32,128]{2,1,0:T(8,128)S(1)}, bf16[8,80,128]{2,1,0:T(8,128)(2,1)S(1)}) custom-call(bf16[8,144,128]{2,1,0:T(8,128)(2,1)S(1)} %get-tuple-element.26.refs_0_.tiles_ref, bf16[8,144,128]{2,1,0:T(8,128)(2,1)S(1)} %collective-permute-done.refs_1_.other_ref, f32[6,128]{1,0:T(8,128)S(1)} %get-tuple-element.27.refs_2_.scale_ref, ...), custom_call_target="tpu_custom_call" | custom-call | tf_op jit(solution)/shard_map/pallas_call | solution.py:499
  61.7 8.9 %all_to_all.40.received_ref = bf16[8,80,128]{2,1,0:T(8,128)(2,1)S(1)} all-to-all(bf16[8,80,128]{2,1,0:T(8,128)(2,1)S(1)} %get-tuple-element.43), channel_id=1, replica_groups={{8,10,12,14,1,3,5,7},{9,11,13,15,0,2,4,6},{24,26,28,30,17,19,21,23},{25..., dimensions={0} | all-to-all | bytes 327680 | tf_op jit(solution)/shard_map/all_to_all | solution.py:524
  70.6 0.8 %shard_map.156 = (f32[4,32,128]{2,1,0:T(8,128)}, f32[8,32,128]{2,1,0:T(8,128)}, f32[3,32,32]{2,1,0:T(8,128)}, f32[3,32,32]{2,1,0:T(8,128)}) custom-call(f32[8,1,128]{2,1,0:T(1,128)S(1)} %all-to-all-done.wanted_ref.refs_7_.refs_4_, bf16[8,80,128]{2,1,0:T(8,128)(2,1)S(1)} %all_to_all.40.received_ref, f32[8,32,128]{2,1,0:T(8,128)S(1)} %get-tuple-element.44.cot_in, ...), custom_call_target="tpu_custom_call" | custom-call | tf_op jit(solution)/shard_map/pallas_call | solution.py:499
  (8 shorter events, 0.1 us)
Async XLA Ops:
  1.9 11.9 %all-to-all-start = ((f32[8,1,128]{2,1,0:T(1,128)}), f32[8,1,128]{2,1,0:T(1,128)S(1)}, u32[]{:S(2)}, u32[]{:S(2)}) async-start(f32[8,1,128]{2,1,0:T(1,128)} %shard_map.147), calls=%async_computation | async-start | bytes 8192 | tf_op jit(solution)/shard_map/all_to_all | solution.py:524
  13.8 9.3 %collective-permute-start = (bf16[8,144,128]{2,1,0:T(8,128)(2,1)S(1)}, bf16[8,144,128]{2,1,0:T(8,128)(2,1)S(1)}, u32[]{:S(2)}, u32[]{:S(2)}) collective-permute-start(bf16[8,144,128]{2,1,0:T(8,128)(2,1)S(1)} %get-tuple-element.26.refs_0_.tiles_ref), channel_id=1, source_target_pairs={{0,1},{1,0},{2,3},{3,2},{4,5},{5,4},{6,7},{7,6},{8,9},{9,8},{10,11... | collective-permute-start | bytes 884744 | tf_op jit(solution)/shard_map/ppermute | solution.py:535
  13.8 9.3 %copy-start.4 = (s32[3,4,128]{2,1,0:T(4,128)S(1)}, s32[3,4,128]{2,1,0:T(4,128)}, u32[]{:S(2)}) copy-start(s32[3,4,128]{2,1,0:T(4,128)} %refs_6_.5) | copy-start | bytes 18436
  13.9 9.3 %copy-start = (bf16[3,8,32,128]{3,2,1,0:T(8,128)(2,1)S(1)}, bf16[3,8,32,128]{3,2,1,0:T(8,128)(2,1)}, u32[]{:S(2)}) copy-start(bf16[3,8,32,128]{3,2,1,0:T(8,128)(2,1)} %saved_dual_ref.1) | copy-start | bytes 589828
  13.9 9.3 %copy-start.3 = (f32[4,32,128]{2,1,0:T(8,128)S(1)}, f32[4,32,128]{2,1,0:T(8,128)}, u32[]{:S(2)}) copy-start(f32[4,32,128]{2,1,0:T(8,128)} %refs_5_.1) | copy-start | bytes 196612
  23.8 8.6 %copy-start.2 = (s32[3,8,128]{2,1,0:T(8,128)S(1)}, s32[3,8,128]{2,1,0:T(8,128)}, u32[]{:S(2)}) copy-start(s32[3,8,128]{2,1,0:T(8,128)} %refs_1_.3) | copy-start | bytes 36868
  42.5 8.1 %copy-start.1 = (bf16[4,4,32,128]{3,2,1,0:T(8,128)(2,1)S(1)}, bf16[4,4,32,128]{3,2,1,0:T(8,128)(2,1)}, u32[]{:S(2)}) copy-start(bf16[4,4,32,128]{3,2,1,0:T(8,128)(2,1)} %refs_7_.1) | copy-start | bytes 393220
  51.1 9.8 %collective-permute-start.1 = (f32[16,32,128]{2,1,0:T(8,128)S(1)}, f32[16,32,128]{2,1,0:T(8,128)S(1)}, u32[]{:S(2)}, u32[]{:S(2)}) collective-permute-start(f32[16,32,128]{2,1,0:T(8,128)S(1)} %get-tuple-element.41.refs_8_), channel_id=1, source_target_pairs={{0,1},{1,0},{2,3},{3,2},{4,5},{5,4},{6,7},{7,6},{8,9},{9,8},{10,11... | collective-permute-start | bytes 786440 | tf_op jit(solution)/shard_map/ppermute | solution.py:535
